TPU v7x, 32 devices: a whole 2x2x4 slice. The times are simulated.
32 devices in a mesh: section: 4 (over y, core), expert: 4 (over z), tensor: 2 (over x).
Axes of the slice: x: 2, y: 2, z: 4, core: 2. Of those that a mesh axis runs over, the one named last changes fastest.
Arguments:
- tokens: bfloat16 [4, 1024, 2048], P('section', ('expert', 'tensor')), may hold values from -6 to 6
- routes: int32 [4, 1024, 2], P('section', ('expert', 'tensor')), may hold values from 0 to 3, all different within a row; in each aligned block of 128 rows (0 to 127, 128 to 255, ..., all dimensions but the last counted through in order) at most 128 rows name the same one
- route_weights: float32 [4, 1024, 2], P('section', ('expert', 'tensor')), may hold values from 0.2 to 1
- expert_gate: bfloat16 [4, 4, 2048, 512], P('section', 'expert'), may hold values from -0.125 to 0.125
- expert_up: bfloat16 [4, 4, 2048, 512], P('section', 'expert'), may hold values from -0.125 to 0.125
- expert_down: bfloat16 [4, 4, 512, 2048], P('section', 'expert'), may hold values from -0.25 to 0.25
Outputs:
- layer_out: bfloat16 [4, 1024, 2048], P('section', ('expert', 'tensor'))
- next_input: bfloat16 [4, 1024, 2048], P('section', ('expert', 'tensor'))
Inputs may be any that keep to these rules, and one draw needn't show every extreme that they name: Each token names 2 different experts; among the tokens of one device no expert is named by more than 128 routes, a bound that some block reaches.
All inputs are finite; a program needn't handle non-finite values.
Results may differ from a plain program's by a relative error of at most 0.0042.
Values may be sent and summed in bfloat16 or wider, within the bound.
No kernel may reach another device: no remote copies, remote signals or barrier semaphores. Data moves between devices by JAX's collectives and lax.ppermute only.
A program may use at most 64 MiB of HBM per device.

v0:
```python
import jax
import jax.numpy as jnp
from jax import lax
from jax.sharding import PartitionSpec as P


def passed_along(value, axis, steps):
    count = lax.axis_size(axis)
    leading, last = (max(0, -steps), min(count, count - steps))
    return lax.ppermute(value, axis, [(source, source + steps) for source in range(leading, last)])


def per_device(tokens, routes, route_weights, expert_gate, expert_up, expert_down):
    rows_in = tokens[0]
    tok_count, width = rows_in.shape
    top_count = routes.shape[2]
    flat_routes = routes[0].reshape(tok_count * top_count)
    flat_weights = route_weights[0].reshape(tok_count * top_count)
    n_expert = lax.axis_size("expert")
    exp_dev = expert_gate.shape[1]
    expert_count = exp_dev * n_expert
    capacity = max(2, 2 * tok_count * top_count // expert_count)
    onehot = (flat_routes[:, None] == jnp.arange(expert_count, dtype=jnp.int32)[None, :]).astype(
        jnp.int32
    )
    ranked = jnp.sum((jnp.cumsum(onehot, axis=0) - 1) * onehot, axis=1)
    slot_index = flat_routes * capacity + ranked
    token_of = jnp.arange(tok_count * top_count, dtype=jnp.int32) // top_count
    outgoing = (
        jnp.zeros((expert_count * capacity, width), jnp.bfloat16)
        .at[slot_index]
        .set(rows_in[token_of])
    )
    outgoing = outgoing.reshape(n_expert, exp_dev, capacity, width)
    arrived = lax.all_to_all(outgoing, "expert", split_axis=0, concat_axis=2, tiled=True)
    slot_rows = arrived[0]
    gate_val = jnp.einsum(
        "esd,edf->esf", slot_rows, expert_gate[0], preferred_element_type=jnp.float32
    )
    up_val = jnp.einsum("esd,edf->esf", slot_rows, expert_up[0], preferred_element_type=jnp.float32)
    hidden = (jax.nn.silu(gate_val) * up_val).astype(jnp.bfloat16)
    expert_out = jnp.einsum(
        "esf,efd->esd", hidden, expert_down[0], preferred_element_type=jnp.float32
    ).astype(jnp.bfloat16)
    expert_out = expert_out.reshape(exp_dev, n_expert, capacity, width)
    came_back = lax.all_to_all(expert_out, "expert", split_axis=1, concat_axis=0, tiled=True)
    back_rows = came_back.reshape(expert_count * capacity, width)
    picked = back_rows[slot_index].astype(jnp.float32) * flat_weights[:, None]
    routed = jnp.sum(picked.reshape(tok_count, top_count, width), axis=1)
    layer_out = (rows_in.astype(jnp.float32) + routed).astype(jnp.bfloat16)
    handed = passed_along(layer_out, "section", 1)
    return (layer_out[None], handed[None])


def solution(mesh):
    in_specs = (
        P("section", ("expert", "tensor"), None),
        P("section", ("expert", "tensor"), None),
        P("section", ("expert", "tensor"), None),
        P("section", "expert", None, None),
        P("section", "expert", None, None),
        P("section", "expert", None, None),
    )
    out_specs = (P("section", ("expert", "tensor"), None), P("section", ("expert", "tensor"), None))
    return jax.shard_map(
        per_device, mesh=mesh, in_specs=in_specs, out_specs=out_specs, check_vma=False
    )
```

profile of v0, /device:TPU:1, one launch (start us, length us, event | category | flops | bytes accessed | tf_op | source)
XLA Modules:
  0.0 148.7 jit_solution(15107265225629593894)
XLA Ops:
  0.6 0.0 copy-start
  0.6 0.9 copy.18
  1.6 0.1 eq.29
  1.7 0.1 eq.25
  1.9 0.7 broadcast_multiply_fusion
  2.6 1.2 reduce-window.6
  3.8 0.1 slice.12
  3.9 0.1 copy.20
  4.0 0.1 copy.21
  4.1 0.1 add_bitcast_fusion
  4.2 0.1 copy.17
  4.3 0.1 mul.37
  4.5 7.4 %scatter_custom_fusion = bf16[512,2048]{1,0:T(8,128)(2,1)} fusion(s32[256]{0:T(256)S(1)} %bitcast.55, bf16[128,2048]{1,0:T(8,128)(2,1)} %bitcast.53, s32[1024]{0:T(1024)S(1)} %pad_clamp_fusion.1, bf16[]{:T(256)} %constant.27.clone.1), kind=kCustom, calls=%fused_computation.14 | custom fusion | bytes 2097664 | tf_op jit(solution)/shard_map/scatter | solution.py:32
  11.9 52.9 %all_to_all.8 = bf16[4,1,128,2048]{3,2,1,0:T(8,128)(2,1)S(1)} all-to-all(bf16[4,1,128,2048]{3,2,1,0:T(8,128)(2,1)} %bitcast.49), channel_id=1, replica_groups=mesh['section'=4,'expert'=4,'tensor'=2] {'expert'}, dimensions={0} | all-to-all | bytes 4194304 | tf_op jit(solution)/shard_map/all_to_all | solution.py:35
  64.8 1.3 copy-done.1
  66.1 0.0 copy-done.4
  66.1 1.2 fusion.3
  67.3 0.0 copy-done
  67.3 6.1 %convolution_convert_fusion = bf16[512,2048]{1,0:T(8,128)(2,1)} fusion(bf16[1,1,512,2048]{3,2,1,0:T(8,128)(2,1)S(1)} %copy-done, bf16[512,2048]{1,0:T(8,128)(2,1)} %bitcast.52, bf16[1,1,2048,512]{3,2,1,0:T(8,128)(2,1)} %param.10, f32[512,512]{1,0:T(8,128)S(1)} %fusion.3), kind=kOutput, calls=%fused_computation.3 | convolution fusion | flops 2150105088 | bytes 9437184 | tf_op jit(solution)/shard_map/esf,efd->esd/dot_general | solution.py:42
  73.4 4.8 %all-to-all-start.1 = ((bf16[1,4,128,2048]{3,2,0,1:T(8,128)(2,1)}), bf16[1,4,128,2048]{3,2,0,1:T(8,128)(2,1)}, u32[]{:S(2)}, u32[]{:S(2)}) async-start(bf16[1,4,128,2048]{3,2,0,1:T(8,128)(2,1)} %bitcast.50), calls=%async_computation.1 | async-start | bytes 4194304 | tf_op jit(solution)/shard_map/all_to_all | solution.py:46
  78.2 0.0 copy-done.3
  78.2 0.1 copy.23
  78.3 47.4 %all-to-all-done.1 = bf16[1,4,128,2048]{3,2,0,1:T(8,128)(2,1)} async-done(((bf16[1,4,128,2048]{3,2,0,1:T(8,128)(2,1)}), bf16[1,4,128,2048]{3,2,0,1:T(8,128)(2,1)}, u32[]{:S(2)}, u32[]{:S(2)}) %all-to-all-start.1) | async-done | bytes 2097184 | tf_op jit(solution)/shard_map/all_to_all | solution.py:46
  125.7 4.2 %gather_fusion = bf16[256,2048]{1,0:T(8,128)(2,1)S(1)} fusion(bf16[512,2048]{1,0:T(8,128)(2,1)} %bitcast.13, s32[1024]{0:T(1024)S(1)} %pad_clamp_fusion), kind=kCustom, calls=%fused_computation.1 | custom fusion | bytes 2098176 | tf_op jit(solution)/shard_map/gather | solution.py:48
  130.0 2.4 %reshape.162 = f32[128,2,2048]{2,1,0:T(2,128)} reshape(bf16[256,2048]{1,0:T(8,128)(2,1)S(1)} %gather_fusion) | data formatting | bytes 3145728 | tf_op jit(solution)/shard_map/convert_element_type | solution.py:48
  132.3 4.9 %multiply_reduce_fusion = f32[128,2048]{1,0:T(8,128)S(1)} fusion(f32[128,2,2048]{2,1,0:T(2,128)} %reshape.162, f32[128,2]{1,0:T(8,128)S(1)} %copy.23), kind=kLoop, calls=%fused_computation.9 | loop fusion | flops 786432 | bytes 3146752 | tf_op jit(solution)/shard_map/reduce_sum | solution.py:49
  137.2 0.0 copy-done.2
  137.2 0.1 add_convert_fusion
  137.3 4.5 %collective-permute-start = (bf16[128,2048]{1,0:T(8,128)(2,1)S(1)}, bf16[128,2048]{1,0:T(8,128)(2,1)S(1)}, u32[]{:S(2)}, u32[]{:S(2)}) collective-permute-start(bf16[128,2048]{1,0:T(8,128)(2,1)S(1)} %add_convert_fusion), channel_id=1, source_target_pairs={{0,8},{8,16},{16,24},{1,9},{9,17},{17,25},{2,10},{10,18},{18,26},{... | collective-permute-start | bytes 1572872 | tf_op jit(solution)/shard_map/ppermute | solution.py:10
  141.8 0.9 fusion.11
  142.7 5.2 %collective-permute-done = bf16[128,2048]{1,0:T(8,128)(2,1)S(1)} collective-permute-done((bf16[128,2048]{1,0:T(8,128)(2,1)S(1)}, bf16[128,2048]{1,0:T(8,128)(2,1)S(1)}, u32[]{:S(2)}, u32[]{:S(2)}) %collective-permute-start) | collective-permute-done | bytes 524320 | tf_op jit(solution)/shard_map/ppermute | solution.py:10
  147.9 0.8 copy.27
  (12 shorter events, 0.1 us)
Async XLA Ops:
  0.6 66.7 %copy-start = (bf16[1,1,512,2048]{3,2,1,0:T(8,128)(2,1)S(1)}, bf16[1,1,512,2048]{3,2,1,0:T(8,128)(2,1)}, u32[]{:S(2)}) copy-start(bf16[1,1,512,2048]{3,2,1,0:T(8,128)(2,1)} %param.11) | copy-start | bytes 6291460
  11.9 54.2 %copy-start.4 = (bf16[1,1,2048,512]{3,2,1,0:T(8,128)(2,1)S(1)}, bf16[1,1,2048,512]{3,2,1,0:T(8,128)(2,1)}, u32[]{:S(2)}) copy-start(bf16[1,1,2048,512]{3,2,1,0:T(8,128)(2,1)} %param.9) | copy-start | bytes 6291460
  64.8 1.3 copy-start.1
  73.4 4.8 %copy-start.3 = (f32[1,128,2]{1,2,0:T(2,128)S(1)}, f32[1,128,2]{1,2,0:T(2,128)}, u32[]{:S(2)}) copy-start(f32[1,128,2]{1,2,0:T(2,128)} %param.8) | copy-start | bytes 3076
  73.4 52.3 %all-to-all-start.1 = ((bf16[1,4,128,2048]{3,2,0,1:T(8,128)(2,1)}), bf16[1,4,128,2048]{3,2,0,1:T(8,128)(2,1)}, u32[]{:S(2)}, u32[]{:S(2)}) async-start(bf16[1,4,128,2048]{3,2,0,1:T(8,128)(2,1)} %bitcast.50), calls=%async_computation.1 | async-start | bytes 4194304 | tf_op jit(solution)/shard_map/all_to_all | solution.py:46
  132.3 4.9 %copy-start.2 = (bf16[1,128,2048]{2,1,0:T(8,128)(2,1)S(1)}, bf16[1,128,2048]{2,1,0:T(8,128)(2,1)}, u32[]{:S(2)}) copy-start(bf16[1,128,2048]{2,1,0:T(8,128)(2,1)} %param.6) | copy-start | bytes 1572868
  137.3 10.6 %collective-permute-start = (bf16[128,2048]{1,0:T(8,128)(2,1)S(1)}, bf16[128,2048]{1,0:T(8,128)(2,1)S(1)}, u32[]{:S(2)}, u32[]{:S(2)}) collective-permute-start(bf16[128,2048]{1,0:T(8,128)(2,1)S(1)} %add_convert_fusion), channel_id=1, source_target_pairs={{0,8},{8,16},{16,24},{1,9},{9,17},{17,25},{2,10},{10,18},{18,26},{... | collective-permute-start | bytes 1572872 | tf_op jit(solution)/shard_map/ppermute | solution.py:10
where the time goes:
time: 149 us
  blocking collectives  52.9 us (36%)
  waiting for transfers between devices  52.6 us (35%)
  local copies, waits for them, and re-layouts  17.9 us (12%)
  starting transfers between devices  9.25 us (6%)
  other arithmetic  7.94 us (5%)
  matrix products  7.31 us (5%)
    all_to_all x1, blocking collectives, per_device(): lax.all_to_all(outgoing, 'expert', split_axis=0, concat_axis=2, tiled=True)  52.9 us
    all_to_all x1, waiting for transfers between devices, per_device(): lax.all_to_all(expert_out, 'expert', split_axis=1, concat_axis=0, tiled=T...  47.4 us
    scatter x1, local copies, waits for them, and re-layouts, per_device(): outgoing = jnp.zeros((expert_count * capacity, width), jnp.bfloat16).at[s...  7.39 us
    dot_general x1, matrix products, per_device(): jnp.einsum('esf,efd->esd', hidden, expert_down[0], preferred_element_type...  6.07 us
    ppermute x1, waiting for transfers between devices, passed_along(): lax.ppermute(value, axis, [(source, source + steps) for source in range(l...  5.2 us
    reduce_sum x1, other arithmetic, per_device(): routed = jnp.sum(picked.reshape(tok_count, top_count, width), axis=1)  4.86 us
    all_to_all x1, starting transfers between devices, per_device(): lax.all_to_all(expert_out, 'expert', split_axis=1, concat_axis=0, tiled=T...  4.76 us
    ppermute x1, starting transfers between devices, passed_along(): lax.ppermute(value, axis, [(source, source + steps) for source in range(l...  4.49 us
  transfers between devices with their start and end apart: 2, of which 2 were waited for; matrix products, arithmetic and copies ran while one was open for 1% of the time, Pallas kernels for 0%

commit v1 on v0

--- a/solution.py
+++ b/solution.py
@@ -10,7 +10,7 @@
     return lax.ppermute(value, axis, [(source, source + steps) for source in range(leading, last)])
 
 
-def per_device(tokens, routes, route_weights, expert_gate, expert_up, expert_down):
+def by_slots(tokens, routes, route_weights, expert_gate, expert_up, expert_down):
     rows_in = tokens[0]
     tok_count, width = rows_in.shape
     top_count = routes.shape[2]
@@ -52,6 +52,84 @@
     return (layer_out[None], handed[None])
 
 
+OUTER = [(0, 1), (1, 0), (2, 3), (3, 2)]
+INNER = [(1, 2), (2, 1)]
+
+
+def on_line(tokens, routes, route_weights, expert_gate, expert_up, expert_down):
+    rows = tokens[0]
+    half = rows.shape[0] // 2
+    first, second = rows[:half], rows[half:]
+    me = lax.axis_index("expert")
+    end = (me == 0) | (me == 3)
+
+    def outer(value):
+        return lax.ppermute(value, "expert", OUTER)
+
+    def inner(value):
+        return lax.ppermute(value, "expert", INNER)
+
+    def pick(at_end, at_mid):
+        return jnp.where(end, at_end, at_mid)
+
+    def expert(block, weight):
+        gate = jnp.dot(block, expert_gate[0, 0], preferred_element_type=jnp.float32)
+        up = jnp.dot(block, expert_up[0, 0], preferred_element_type=jnp.float32)
+        hidden = (jax.nn.silu(gate) * up).astype(jnp.bfloat16)
+        out = jnp.dot(hidden, expert_down[0, 0], preferred_element_type=jnp.float32)
+        return out.astype(jnp.bfloat16).astype(jnp.float32) * weight[:, None]
+
+    def narrow(value):
+        return value.astype(jnp.bfloat16)
+
+    def wide(value):
+        return value.astype(jnp.float32)
+
+    names = jnp.arange(4, dtype=jnp.int32)[:, None, None]
+    table = jnp.sum(
+        jnp.where(routes[0].T[None] == names, route_weights[0].T[None], 0.0), axis=1
+    )
+    oa = outer(first)
+    ia = inner(first)
+    table_near = outer(table)
+    table_mid = inner(jnp.stack([table, table_near]))
+    table_far = outer(table_mid)
+    weigh = lambda t: lax.dynamic_index_in_dim(t, me, 0, keepdims=False)
+    w_own, w_near = weigh(table), weigh(table_near)
+    w_two = weigh(pick(table_far[0], table_mid[0]))
+    w_three = weigh(pick(table_far[1], table_mid[1]))
+    lo, hi = slice(0, half), slice(half, None)
+
+    total = wide(rows) + expert(rows, w_own)
+    o1 = outer(pick(second, ia))
+    i1 = inner(oa)
+    p1 = expert(oa, w_near[lo])
+    o2 = outer(pick(narrow(p1), i1))
+    i2 = inner(o1)
+    p2 = expert(pick(o1, ia), w_two[lo])
+    o3 = outer(pick(narrow(p2), i2))
+    i3 = inner(second)
+    p3 = expert(pick(o2, i1), w_three[lo])
+    o4 = outer(pick(narrow(p3), i3))
+    i4 = inner(narrow(wide(o3) + p2))
+    p4 = expert(pick(o3, i2), w_three[hi])
+    o5 = outer(pick(narrow(p4), second))
+    i5 = inner(narrow(wide(o4) + p3))
+    p5 = expert(pick(o4, i3), w_two[hi])
+    o6 = outer(pick(narrow(p5), narrow(wide(i5) + p1)))
+    i6 = inner(narrow(wide(o5) + p4))
+    p6 = expert(pick(o5, o1), w_near[hi])
+    o7 = outer(pick(narrow(p6), narrow(wide(i6) + p6)))
+    i7 = inner(narrow(wide(o6) + p5))
+    out_lo = narrow(total[lo] + pick(wide(o6), wide(o2) + wide(i4)))
+    next_lo = passed_along(out_lo, "section", 1)
+    out_hi = narrow(total[hi] + wide(o7) + pick(0.0, wide(i7)))
+    next_hi = passed_along(out_hi, "section", 1)
+    layer_out = jnp.concatenate([out_lo, out_hi], axis=0)
+    handed = jnp.concatenate([next_lo, next_hi], axis=0)
+    return (layer_out[None], handed[None])
+
+
 def solution(mesh):
     in_specs = (
         P("section", ("expert", "tensor"), None),
@@ -62,6 +140,12 @@
         P("section", "expert", None, None),
     )
     out_specs = (P("section", ("expert", "tensor"), None), P("section", ("expert", "tensor"), None))
+
+    def per_device(*args):
+        tokens, expert_gate = args[0], args[3]
+        line = mesh.shape["expert"] == 4 and expert_gate.shape[1] == 1 and tokens.shape[1] % 32 == 0
+        return (on_line if line else by_slots)(*args)
+
     return jax.shard_map(
         per_device, mesh=mesh, in_specs=in_specs, out_specs=out_specs, check_vma=False
     )

time: 149 us -> 118 us (0.79)
  the two profiles are of different devices: /device:TPU:1 before, /device:TPU:12 now
where the time goes in v1:
time: 118 us; the launch traced here: 116 us
  starting transfers between devices  38.7 us (33%)
  matrix products  35.9 us (30%)
  waiting for transfers between devices  22.2 us (19%)
  other arithmetic  13.6 us (12%)
  local copies, waits for them, and re-layouts  5.07 us (4%)
    ppermute x9, starting transfers between devices, inner(): return lax.ppermute(value, 'expert', INNER)  30.2 us
    dot_general x7, matrix products, expert(): out = jnp.dot(hidden, expert_down[0, 0], preferred_element_type=jnp.float32)  23.3 us
    ppermute x9, waiting for transfers between devices, inner(): return lax.ppermute(value, 'expert', INNER)  10.9 us
    dot_general x6, matrix products, expert(): gate = jnp.dot(block, expert_gate[0, 0], preferred_element_type=jnp.float32)  10.5 us
    convert_element_type x5, other arithmetic, narrow(): return value.astype(jnp.bfloat16)  8.51 us
    ppermute x2, waiting for transfers between devices, passed_along(): lax.ppermute(value, axis, [(source, source + steps) for source in range(l...  5.8 us
    ppermute x10, waiting for transfers between devices, outer(): return lax.ppermute(value, 'expert', OUTER)  5.51 us
    ppermute x10, starting transfers between devices, outer(): return lax.ppermute(value, 'expert', OUTER)  4.68 us
  transfers between devices with their start and end apart: 21, of which 10 were waited for; matrix products, arithmetic and copies ran while one was open for 42% of the time, Pallas kernels for 0%

profile of v1, /device:TPU:12, one launch (start us, length us, event | category | flops | bytes accessed | tf_op | source)
XLA Modules:
  0.0 116.5 jit_solution(13727948056174506797)
XLA Ops:
  0.7 1.9 %slice_bitcast_fusion.1 = (bf16[64,2048]{1,0:T(8,128)(2,1)S(1)}, bf16[64,2048]{1,0:T(8,128)(2,1)}) fusion(bf16[1,128,2048]{2,1,0:T(8,128)(2,1)} %param.6), kind=kLoop, calls=%fused_computation.83 | loop fusion | bytes 1048576 | tf_op jit(solution)/shard_map/slice | solution.py:62
  2.6 3.5 %collective-permute-start.10 = (bf16[64,2048]{1,0:T(8,128)(2,1)S(1)}, bf16[64,2048]{1,0:T(8,128)(2,1)S(1)}, u32[]{:S(2)}, u32[]{:S(2)}) collective-permute-start(bf16[64,2048]{1,0:T(8,128)(2,1)S(1)} %get-tuple-element.4), channel_id=1, source_target_pairs={{2,4},{4,2},{3,5},{5,3},{10,12},{12,10},{11,13},{13,11},{18,20},{2... | collective-permute-start | bytes 786440 | tf_op jit(solution)/shard_map/ppermute | solution.py:70
  6.9 2.0 %collective-permute-start.1 = (f32[4,128]{1,0:T(4,128)S(1)}, f32[4,128]{1,0:T(4,128)S(1)}, u32[]{:S(2)}, u32[]{:S(2)}) collective-permute-start(f32[4,128]{1,0:T(4,128)S(1)} %select_reduce_fusion), channel_id=1, source_target_pairs={{0,2},{2,0},{4,6},{6,4},{1,3},{3,1},{5,7},{7,5},{8,10},{10,8},{12,... | collective-permute-start | bytes 6152 | tf_op jit(solution)/shard_map/ppermute | solution.py:67
  8.9 2.3 %collective-permute-start.6 = (bf16[64,2048]{1,0:T(8,128)(2,1)}, bf16[64,2048]{1,0:T(8,128)(2,1)S(1)}, u32[]{:S(2)}, u32[]{:S(2)}) collective-permute-start(bf16[64,2048]{1,0:T(8,128)(2,1)} %get-tuple-element.5), channel_id=1, source_target_pairs={{2,4},{4,2},{3,5},{5,3},{10,12},{12,10},{11,13},{13,11},{18,20},{2... | collective-permute-start | bytes 786440 | tf_op jit(solution)/shard_map/ppermute | solution.py:70
  11.2 2.9 %fusion.46 = f32[128,512]{1,0:T(8,128)} fusion(bf16[1,1,2048,512]{3,2,1,0:T(8,128)(2,1)} %param.9, bf16[1,128,2048]{2,1,0:T(8,128)(2,1)} %param.6), kind=kOutput, calls=%fused_computation.53 | convolution fusion | flops 268435456 | bytes 2883584 | tf_op jit(solution)/shard_map/dot_general | solution.py:76
  14.6 3.5 %collective-permute-start.4 = (f32[2,4,128]{2,1,0:T(4,128)S(1)}, f32[2,4,128]{2,1,0:T(4,128)S(1)}, u32[]{:S(2)}, u32[]{:S(2)}) collective-permute-start(f32[2,4,128]{2,1,0:T(4,128)S(1)} %pad_maximum_fusion), channel_id=1, source_target_pairs={{2,4},{4,2},{3,5},{5,3},{10,12},{12,10},{11,13},{13,11},{18,20},{2... | collective-permute-start | bytes 12296 | tf_op jit(solution)/shard_map/ppermute | solution.py:70
  18.1 2.0 %collective-permute-done.4 = f32[2,4,128]{2,1,0:T(4,128)S(1)} collective-permute-done((f32[2,4,128]{2,1,0:T(4,128)S(1)}, f32[2,4,128]{2,1,0:T(4,128)S(1)}, u32[]{:S(2)}, u32[]{:S(2)}) %collective-permute-start.4) | collective-permute-done | bytes 4128 | tf_op jit(solution)/shard_map/ppermute | solution.py:70
  20.2 3.5 %collective-permute-done.5 = f32[2,4,128]{2,1,0:T(4,128)S(1)} collective-permute-done((f32[2,4,128]{2,1,0:T(4,128)S(1)}, f32[2,4,128]{2,1,0:T(4,128)S(1)}, u32[]{:S(2)}, u32[]{:S(2)}) %collective-permute-start.5) | collective-permute-done | bytes 4128 | tf_op jit(solution)/shard_map/ppermute | solution.py:67
  26.3 3.5 %collective-permute-start.2 = (bf16[64,2048]{1,0:T(8,128)(2,1)}, bf16[64,2048]{1,0:T(8,128)(2,1)S(1)}, u32[]{:S(2)}, u32[]{:S(2)}) collective-permute-start(bf16[64,2048]{1,0:T(8,128)(2,1)} %collective-permute-done), channel_id=1, source_target_pairs={{2,4},{4,2},{3,5},{5,3},{10,12},{12,10},{11,13},{13,11},{18,20},{2... | collective-permute-start | bytes 786440 | tf_op jit(solution)/shard_map/ppermute | solution.py:70
  29.8 2.2 %fusion.30 = f32[64,512]{1,0:T(8,128)S(1)} fusion(bf16[64,2048]{1,0:T(8,128)(2,1)} %collective-permute-done, bf16[1,1,2048,512]{3,2,1,0:T(8,128)(2,1)} %param.10), kind=kOutput, calls=%fused_computation.37 | convolution fusion | flops 134217728 | bytes 2490368 | tf_op jit(solution)/shard_map/dot_general | solution.py:77
  32.0 2.8 %collective-permute-done.2 = bf16[64,2048]{1,0:T(8,128)(2,1)S(1)} collective-permute-done((bf16[64,2048]{1,0:T(8,128)(2,1)}, bf16[64,2048]{1,0:T(8,128)(2,1)S(1)}, u32[]{:S(2)}, u32[]{:S(2)}) %collective-permute-start.2) | collective-permute-done | bytes 262176 | tf_op jit(solution)/shard_map/ppermute | solution.py:70
  34.8 3.6 %fusion.64 = (bf16[64,2048]{1,0:T(8,128)(2,1)}, f32[64,2048]{1,0:T(8,128)}) fusion(bf16[64,2048]{1,0:T(8,128)(2,1)S(1)} %collective-permute-done.2, f32[64]{0:T(128)S(1)} %get-tuple-element.9, pred[]{:T(512)S(6)} %or.3, bf16[1,1,512,2048]{3,2,1,0:T(8,128)(2,1)S(1)} %copy-done, f32[64,512]{1,0:T(8,128)S(1)} %fusion.30, ...), kind=kOutput, calls=%fused_computation.76 | convolution fusion | flops 269287424 | bytes 5636353 | tf_op jit(solution)/shard_map/dot_general | solution.py:79
  38.4 3.5 %collective-permute-start.12 = (bf16[64,2048]{1,0:T(8,128)(2,1)S(1)}, bf16[64,2048]{1,0:T(8,128)(2,1)S(1)}, u32[]{:S(2)}, u32[]{:S(2)}) collective-permute-start(bf16[64,2048]{1,0:T(8,128)(2,1)S(1)} %collective-permute-done.11), channel_id=1, source_target_pairs={{2,4},{4,2},{3,5},{5,3},{10,12},{12,10},{11,13},{13,11},{18,20},{2... | collective-permute-start | bytes 786440 | tf_op jit(solution)/shard_map/ppermute | solution.py:70
  41.9 2.2 %fusion.38 = f32[64,512]{1,0:T(8,128)S(1)} fusion(bf16[1,1,2048,512]{3,2,1,0:T(8,128)(2,1)} %param.9, bf16[64,2048]{1,0:T(8,128)(2,1)S(1)} %collective-permute-done.11, bf16[64,2048]{1,0:T(8,128)(2,1)} %copy-done.10, pred[]{:T(512)S(6)} %or.3), kind=kOutput, calls=%fused_computation.45 | convolution fusion | flops 134348800 | bytes 2752513 | tf_op jit(solution)/shard_map/dot_general | solution.py:76
  44.1 2.6 %collective-permute-done.12 = bf16[64,2048]{1,0:T(8,128)(2,1)S(1)} collective-permute-done((bf16[64,2048]{1,0:T(8,128)(2,1)S(1)}, bf16[64,2048]{1,0:T(8,128)(2,1)S(1)}, u32[]{:S(2)}, u32[]{:S(2)}) %collective-permute-start.12) | collective-permute-done | bytes 262176 | tf_op jit(solution)/shard_map/ppermute | solution.py:70
  47.4 3.5 %convert_select_fusion.2 = (bf16[64,2048]{1,0:T(8,128)(2,1)}, f32[64,2048]{1,0:T(8,128)}) fusion(bf16[64,2048]{1,0:T(8,128)(2,1)} %copy-done.8, pred[]{:T(512)S(6)} %or.3, f32[64]{0:T(128)} %get-tuple-element.10, bf16[1,1,512,2048]{3,2,1,0:T(8,128)(2,1)S(1)} %copy-done, f32[64,512]{1,0:T(8,128)S(1)} %fusion.38, bf16[1,1,2048,512]{3,2,1,0:T(8,128)(2,1)} %param.10, ...), kind=kOutput, calls=%fused_computation.80 | convolution fusion | flops 269418496 | bytes 5898497 | tf_op jit(solution)/shard_map/dot_general | solution.py:79
  50.9 2.2 %fusion.42 = f32[64,512]{1,0:T(8,128)S(1)} fusion(bf16[1,1,2048,512]{3,2,1,0:T(8,128)(2,1)} %param.9, bf16[64,2048]{1,0:T(8,128)(2,1)S(1)} %collective-permute-done.3, bf16[64,2048]{1,0:T(8,128)(2,1)} %copy-done.7, pred[]{:T(512)S(6)} %or.3), kind=kOutput, calls=%fused_computation.49 | convolution fusion | flops 134348800 | bytes 2752513 | tf_op jit(solution)/shard_map/dot_general | solution.py:76
  53.1 3.5 %convert_select_fusion.3 = (bf16[64,2048]{1,0:T(8,128)(2,1)}, f32[64,2048]{1,0:T(8,128)}) fusion(bf16[64,2048]{1,0:T(8,128)(2,1)S(1)} %collective-permute-done.6, pred[]{:T(512)S(6)} %or.3, f32[64]{0:T(128)} %get-tuple-element.13, bf16[1,1,512,2048]{3,2,1,0:T(8,128)(2,1)S(1)} %copy-done, f32[64,512]{1,0:T(8,128)S(1)} %fusion.42, ...), kind=kOutput, calls=%fused_computation.82 | convolution fusion | flops 269418496 | bytes 5898497 | tf_op jit(solution)/shard_map/dot_general | solution.py:79
  60.0 2.2 %fusion.36 = f32[64,512]{1,0:T(8,128)S(1)} fusion(bf16[1,1,2048,512]{3,2,1,0:T(8,128)(2,1)} %param.9, bf16[64,2048]{1,0:T(8,128)(2,1)} %collective-permute-done.13, bf16[64,2048]{1,0:T(8,128)(2,1)} %copy-done.8, pred[]{:T(512)S(6)} %or.3), kind=kOutput, calls=%fused_computation.43 | convolution fusion | flops 134348800 | bytes 2752513 | tf_op jit(solution)/shard_map/dot_general | solution.py:76
  62.1 3.4 %convert_select_fusion.1 = (bf16[64,2048]{1,0:T(8,128)(2,1)}, f32[64,2048]{1,0:T(8,128)}) fusion(pred[]{:T(512)S(6)} %or.3, bf16[1,128,2048]{2,1,0:T(8,128)(2,1)S(1)} %copy-done.3, f32[64]{0:T(128)S(1)} %get-tuple-element.12, bf16[1,1,512,2048]{3,2,1,0:T(8,128)(2,1)S(1)} %copy-done, f32[64,512]{1,0:T(8,128)S(1)} %fusion.36, ...), kind=kOutput, calls=%fused_computation.79 | convolution fusion | flops 269418496 | bytes 5899520 | tf_op jit(solution)/shard_map/dot_general | solution.py:79
  65.6 2.0 %add_convert_fusion.2 = bf16[64,2048]{1,0:T(8,128)(2,1)} fusion(f32[64,2048]{1,0:T(8,128)} %get-tuple-element.19, bf16[64,2048]{1,0:T(8,128)(2,1)} %collective-permute-done.13), kind=kLoop, calls=%fused_computation.71 | loop fusion | flops 393216 | bytes 1048576 | tf_op jit(solution)/shard_map/convert_element_type | solution.py:83
  67.6 3.5 %collective-permute-start.14 = (bf16[64,2048]{1,0:T(8,128)(2,1)}, bf16[64,2048]{1,0:T(8,128)(2,1)}, u32[]{:S(2)}, u32[]{:S(2)}) collective-permute-start(bf16[64,2048]{1,0:T(8,128)(2,1)} %add_convert_fusion.2), channel_id=1, source_target_pairs={{2,4},{4,2},{3,5},{5,3},{10,12},{12,10},{11,13},{13,11},{18,20},{2... | collective-permute-start | bytes 786440 | tf_op jit(solution)/shard_map/ppermute | solution.py:70
  72.9 2.3 %collective-permute-start.8 = (bf16[64,2048]{1,0:T(8,128)(2,1)}, bf16[64,2048]{1,0:T(8,128)(2,1)}, u32[]{:S(2)}, u32[]{:S(2)}) collective-permute-start(bf16[64,2048]{1,0:T(8,128)(2,1)} %add_convert_fusion.4), channel_id=1, source_target_pairs={{2,4},{4,2},{3,5},{5,3},{10,12},{12,10},{11,13},{13,11},{18,20},{2... | collective-permute-start | bytes 786440 | tf_op jit(solution)/shard_map/ppermute | solution.py:70
  75.8 2.6 %fusion.9 = f32[64,2048]{1,0:T(8,128)S(1)} fusion(bf16[1,1,512,2048]{3,2,1,0:T(8,128)(2,1)S(1)} %copy-done, f32[64]{0:T(128)S(1)} %get-tuple-element.11, f32[64,512]{1,0:T(8,128)S(1)} %fusion.40, bf16[1,1,2048,512]{3,2,1,0:T(8,128)(2,1)} %param.10, bf16[64,2048]{1,0:T(8,128)(2,1)} %collective-permute-done.7, bf16[64,2048]{1,0:T(8,128)(2,1)} %copy-done.4, ...), kind=kOutput, calls=%fused_computation.14 | convolution fusion | flops 269156352 | bytes 5374209 | tf_op jit(solution)/shard_map/dot_general | solution.py:79
  79.8 3.5 %collective-permute-start.16 = (bf16[64,2048]{1,0:T(8,128)(2,1)S(1)}, bf16[64,2048]{1,0:T(8,128)(2,1)}, u32[]{:S(2)}, u32[]{:S(2)}) collective-permute-start(bf16[64,2048]{1,0:T(8,128)(2,1)S(1)} %add_convert_fusion.1), channel_id=1, source_target_pairs={{2,4},{4,2},{3,5},{5,3},{10,12},{12,10},{11,13},{13,11},{18,20},{2... | collective-permute-start | bytes 786440 | tf_op jit(solution)/shard_map/ppermute | solution.py:70
  83.3 2.0 %fusion.66 = bf16[64,2048]{1,0:T(8,128)(2,1)} fusion(f32[64,2048]{1,0:T(8,128)} %get-tuple-element.15, bf16[64,2048]{1,0:T(8,128)(2,1)} %collective-permute-done.8, f32[64,2048]{1,0:T(8,128)S(1)} %fusion.9, f32[64]{0:T(128)S(1)} %get-tuple-element.9, pred[]{:T(512)S(6)} %or.3), kind=kLoop, calls=%fused_computation.78 | loop fusion | flops 786432 | bytes 1573121 | tf_op jit(solution)/shard_map/jit(_where)/select_n | solution.py:73
  85.7 2.4 %collective-permute-done.16 = bf16[64,2048]{1,0:T(8,128)(2,1)} collective-permute-done((bf16[64,2048]{1,0:T(8,128)(2,1)S(1)}, bf16[64,2048]{1,0:T(8,128)(2,1)}, u32[]{:S(2)}, u32[]{:S(2)}) %collective-permute-start.16) | collective-permute-done | bytes 262176 | tf_op jit(solution)/shard_map/ppermute | solution.py:70
  88.1 3.2 %fusion.65 = bf16[64,2048]{1,0:T(8,128)(2,1)} fusion(bf16[64,2048]{1,0:T(8,128)(2,1)} %collective-permute-done.16, f32[64]{0:T(128)S(1)} %get-tuple-element.8, pred[]{:T(512)S(6)} %or.3, bf16[1,1,512,2048]{3,2,1,0:T(8,128)(2,1)S(1)} %copy-done, f32[64,512]{1,0:T(8,128)S(1)} %fusion.34, bf16[1,1,2048,512]{3,2,1,0:T(8,128)(2,1)} %param.10, ...), kind=kOutput, calls=%fused_computation.77 | convolution fusion | flops 269811712 | bytes 5374209 | tf_op jit(solution)/shard_map/dot_general | solution.py:79
  94.3 4.6 %collective-permute-start.18 = (bf16[64,2048]{1,0:T(8,128)(2,1)}, bf16[64,2048]{1,0:T(8,128)(2,1)S(1)}, u32[]{:S(2)}, u32[]{:S(2)}) collective-permute-start(bf16[64,2048]{1,0:T(8,128)(2,1)} %fusion.58), channel_id=1, source_target_pairs={{2,4},{4,2},{3,5},{5,3},{10,12},{12,10},{11,13},{13,11},{18,20},{2... | collective-permute-start | bytes 786440 | tf_op jit(solution)/shard_map/ppermute | solution.py:70
  98.9 3.4 %fusion.2 = f32[128,2048]{1,0:T(8,128)} fusion(bf16[1,1,512,2048]{3,2,1,0:T(8,128)(2,1)S(1)} %copy-done, bf16[1,1,2048,512]{3,2,1,0:T(8,128)(2,1)} %param.10, bf16[1,128,2048]{2,1,0:T(8,128)(2,1)S(1)} %copy-done.3, f32[128]{0:T(128)S(1)} %copy-done.11, f32[128,512]{1,0:T(8,128)} %fusion.46), kind=kOutput, calls=%fused_computation.3 | convolution fusion | flops 538574848 | bytes 6029824 | tf_op jit(solution)/shard_map/dot_general | solution.py:79
  109.8 3.0 %collective-permute-done.19 = bf16[64,2048]{1,0:T(8,128)(2,1)S(1)} collective-permute-done((bf16[64,2048]{1,0:T(8,128)(2,1)S(1)}, bf16[64,2048]{1,0:T(8,128)(2,1)S(1)}, u32[]{:S(2)}, u32[]{:S(2)}) %collective-permute-start.19) | collective-permute-done | bytes 262176 | tf_op jit(solution)/shard_map/ppermute | solution.py:10
  112.8 2.8 %collective-permute-done.20 = bf16[64,2048]{1,0:T(8,128)(2,1)S(1)} collective-permute-done((bf16[64,2048]{1,0:T(8,128)(2,1)S(1)}, bf16[64,2048]{1,0:T(8,128)(2,1)S(1)}, u32[]{:S(2)}, u32[]{:S(2)}) %collective-permute-start.20) | collective-permute-done | bytes 262176 | tf_op jit(solution)/shard_map/ppermute | solution.py:10
  (67 shorter events, 23.3 us)
Async XLA Ops:
  0.6 34.2 %copy-start = (bf16[1,1,512,2048]{3,2,1,0:T(8,128)(2,1)S(1)}, bf16[1,1,512,2048]{3,2,1,0:T(8,128)(2,1)}, u32[]{:S(2)}) copy-start(bf16[1,1,512,2048]{3,2,1,0:T(8,128)(2,1)} %param.11) | copy-start | bytes 6291460
  0.6 24.9 %copy-start.3 = (bf16[1,128,2048]{2,1,0:T(8,128)(2,1)S(1)}, bf16[1,128,2048]{2,1,0:T(8,128)(2,1)}, u32[]{:S(2)}) copy-start(bf16[1,128,2048]{2,1,0:T(8,128)(2,1)} %param.6) | copy-start | bytes 1572868
  2.6 22.3 %collective-permute-start.10 = (bf16[64,2048]{1,0:T(8,128)(2,1)S(1)}, bf16[64,2048]{1,0:T(8,128)(2,1)S(1)}, u32[]{:S(2)}, u32[]{:S(2)}) collective-permute-start(bf16[64,2048]{1,0:T(8,128)(2,1)S(1)} %get-tuple-element.4), channel_id=1, source_target_pairs={{2,4},{4,2},{3,5},{5,3},{10,12},{12,10},{11,13},{13,11},{18,20},{2... | collective-permute-start | bytes 786440 | tf_op jit(solution)/shard_map/ppermute | solution.py:70
  6.1 20.3 %collective-permute-start = (bf16[64,2048]{1,0:T(8,128)(2,1)S(1)}, bf16[64,2048]{1,0:T(8,128)(2,1)}, u32[]{:S(2)}, u32[]{:S(2)}) collective-permute-start(bf16[64,2048]{1,0:T(8,128)(2,1)S(1)} %get-tuple-element.4), channel_id=1, source_target_pairs={{0,2},{2,0},{4,6},{6,4},{1,3},{3,1},{5,7},{7,5},{8,10},{10,8},{12,... | collective-permute-start | bytes 786440 | tf_op jit(solution)/shard_map/ppermute | solution.py:67
  6.9 7.8 %collective-permute-start.1 = (f32[4,128]{1,0:T(4,128)S(1)}, f32[4,128]{1,0:T(4,128)S(1)}, u32[]{:S(2)}, u32[]{:S(2)}) collective-permute-start(f32[4,128]{1,0:T(4,128)S(1)} %select_reduce_fusion), channel_id=1, source_target_pairs={{0,2},{2,0},{4,6},{6,4},{1,3},{3,1},{5,7},{7,5},{8,10},{10,8},{12,... | collective-permute-start | bytes 6152 | tf_op jit(solution)/shard_map/ppermute | solution.py:67
  8.9 44.3 %collective-permute-start.6 = (bf16[64,2048]{1,0:T(8,128)(2,1)}, bf16[64,2048]{1,0:T(8,128)(2,1)S(1)}, u32[]{:S(2)}, u32[]{:S(2)}) collective-permute-start(bf16[64,2048]{1,0:T(8,128)(2,1)} %get-tuple-element.5), channel_id=1, source_target_pairs={{2,4},{4,2},{3,5},{5,3},{10,12},{12,10},{11,13},{13,11},{18,20},{2... | collective-permute-start | bytes 786440 | tf_op jit(solution)/shard_map/ppermute | solution.py:70
  14.6 5.5 %collective-permute-start.4 = (f32[2,4,128]{2,1,0:T(4,128)S(1)}, f32[2,4,128]{2,1,0:T(4,128)S(1)}, u32[]{:S(2)}, u32[]{:S(2)}) collective-permute-start(f32[2,4,128]{2,1,0:T(4,128)S(1)} %pad_maximum_fusion), channel_id=1, source_target_pairs={{2,4},{4,2},{3,5},{5,3},{10,12},{12,10},{11,13},{13,11},{18,20},{2... | collective-permute-start | bytes 12296 | tf_op jit(solution)/shard_map/ppermute | solution.py:70
  20.1 3.6 %collective-permute-start.5 = (f32[2,4,128]{2,1,0:T(4,128)S(1)}, f32[2,4,128]{2,1,0:T(4,128)S(1)}, u32[]{:S(2)}, u32[]{:S(2)}) collective-permute-start(f32[2,4,128]{2,1,0:T(4,128)S(1)} %collective-permute-done.4), channel_id=1, source_target_pairs={{0,2},{2,0},{4,6},{6,4},{1,3},{3,1},{5,7},{7,5},{8,10},{10,8},{12,... | collective-permute-start | bytes 12296 | tf_op jit(solution)/shard_map/ppermute | solution.py:67
  24.9 0.7 copy-start.10
  26.3 12.1 %collective-permute-start.11 = (bf16[64,2048]{1,0:T(8,128)(2,1)}, bf16[64,2048]{1,0:T(8,128)(2,1)S(1)}, u32[]{:S(2)}, u32[]{:S(2)}) collective-permute-start(bf16[64,2048]{1,0:T(8,128)(2,1)} %broadcast_select_fusion.3), channel_id=1, source_target_pairs={{0,2},{2,0},{4,6},{6,4},{1,3},{3,1},{5,7},{7,5},{8,10},{10,8},{12,... | collective-permute-start | bytes 786440 | tf_op jit(solution)/shard_map/ppermute | solution.py:67
  26.3 8.5 %collective-permute-start.2 = (bf16[64,2048]{1,0:T(8,128)(2,1)}, bf16[64,2048]{1,0:T(8,128)(2,1)S(1)}, u32[]{:S(2)}, u32[]{:S(2)}) collective-permute-start(bf16[64,2048]{1,0:T(8,128)(2,1)} %collective-permute-done), channel_id=1, source_target_pairs={{2,4},{4,2},{3,5},{5,3},{10,12},{12,10},{11,13},{13,11},{18,20},{2... | collective-permute-start | bytes 786440 | tf_op jit(solution)/shard_map/ppermute | solution.py:70
  34.8 3.6 %copy-start.7 = (bf16[64,2048]{1,0:T(8,128)(2,1)}, bf16[64,2048]{1,0:T(8,128)(2,1)S(1)}, u32[]{:S(2)}) copy-start(bf16[64,2048]{1,0:T(8,128)(2,1)S(1)} %collective-permute-done.2) | copy-start | bytes 786436
  38.4 12.5 %collective-permute-start.3 = (bf16[64,2048]{1,0:T(8,128)(2,1)}, bf16[64,2048]{1,0:T(8,128)(2,1)S(1)}, u32[]{:S(2)}, u32[]{:S(2)}) collective-permute-start(bf16[64,2048]{1,0:T(8,128)(2,1)} %get-tuple-element.14), channel_id=1, source_target_pairs={{0,2},{2,0},{4,6},{6,4},{1,3},{3,1},{5,7},{7,5},{8,10},{10,8},{12,... | collective-permute-start | bytes 786440 | tf_op jit(solution)/shard_map/ppermute | solution.py:67
  38.4 8.3 %collective-permute-start.12 = (bf16[64,2048]{1,0:T(8,128)(2,1)S(1)}, bf16[64,2048]{1,0:T(8,128)(2,1)S(1)}, u32[]{:S(2)}, u32[]{:S(2)}) collective-permute-start(bf16[64,2048]{1,0:T(8,128)(2,1)S(1)} %collective-permute-done.11), channel_id=1, source_target_pairs={{2,4},{4,2},{3,5},{5,3},{10,12},{12,10},{11,13},{13,11},{18,20},{2... | collective-permute-start | bytes 786440 | tf_op jit(solution)/shard_map/ppermute | solution.py:70
  50.9 9.1 %collective-permute-start.13 = (bf16[64,2048]{1,0:T(8,128)(2,1)}, bf16[64,2048]{1,0:T(8,128)(2,1)}, u32[]{:S(2)}, u32[]{:S(2)}) collective-permute-start(bf16[64,2048]{1,0:T(8,128)(2,1)} %get-tuple-element.18), channel_id=1, source_target_pairs={{0,2},{2,0},{4,6},{6,4},{1,3},{3,1},{5,7},{7,5},{8,10},{10,8},{12,... | collective-permute-start | bytes 786440 | tf_op jit(solution)/shard_map/ppermute | solution.py:67
  50.9 5.8 %copy-start.5 = (bf16[64,2048]{1,0:T(8,128)(2,1)}, bf16[64,2048]{1,0:T(8,128)(2,1)S(1)}, u32[]{:S(2)}) copy-start(bf16[64,2048]{1,0:T(8,128)(2,1)S(1)} %collective-permute-done.3) | copy-start | bytes 786436
  53.1 22.2 %copy-start.4 = (bf16[64,2048]{1,0:T(8,128)(2,1)}, bf16[64,2048]{1,0:T(8,128)(2,1)S(1)}, u32[]{:S(2)}) copy-start(bf16[64,2048]{1,0:T(8,128)(2,1)S(1)} %collective-permute-done.6) | copy-start | bytes 786436
  56.6 5.5 %copy-start.9 = (bf16[64,2048]{1,0:T(8,128)(2,1)S(1)}, bf16[64,2048]{1,0:T(8,128)(2,1)}, u32[]{:S(2)}) copy-start(bf16[64,2048]{1,0:T(8,128)(2,1)} %copy-done.8) | copy-start | bytes 786436
  56.6 14.5 %collective-permute-start.7 = (bf16[64,2048]{1,0:T(8,128)(2,1)}, bf16[64,2048]{1,0:T(8,128)(2,1)}, u32[]{:S(2)}, u32[]{:S(2)}) collective-permute-start(bf16[64,2048]{1,0:T(8,128)(2,1)} %get-tuple-element.16), channel_id=1, source_target_pairs={{0,2},{2,0},{4,6},{6,4},{1,3},{3,1},{5,7},{7,5},{8,10},{10,8},{12,... | collective-permute-start | bytes 786440 | tf_op jit(solution)/shard_map/ppermute | solution.py:67
  65.6 9.7 %copy-start.1 = (bf16[1,1,2048,512]{3,2,1,0:T(8,128)(2,1)S(1)}, bf16[1,1,2048,512]{3,2,1,0:T(8,128)(2,1)}, u32[]{:S(2)}) copy-start(bf16[1,1,2048,512]{3,2,1,0:T(8,128)(2,1)} %param.9) | copy-start | bytes 6291460
  65.6 12.9 %collective-permute-start.15 = (bf16[64,2048]{1,0:T(8,128)(2,1)}, bf16[64,2048]{1,0:T(8,128)(2,1)}, u32[]{:S(2)}, u32[]{:S(2)}) collective-permute-start(bf16[64,2048]{1,0:T(8,128)(2,1)} %get-tuple-element.20), channel_id=1, source_target_pairs={{0,2},{2,0},{4,6},{6,4},{1,3},{3,1},{5,7},{7,5},{8,10},{10,8},{12,... | collective-permute-start | bytes 786440 | tf_op jit(solution)/shard_map/ppermute | solution.py:67
  67.6 34.8 %collective-permute-start.14 = (bf16[64,2048]{1,0:T(8,128)(2,1)}, bf16[64,2048]{1,0:T(8,128)(2,1)}, u32[]{:S(2)}, u32[]{:S(2)}) collective-permute-start(bf16[64,2048]{1,0:T(8,128)(2,1)} %add_convert_fusion.2), channel_id=1, source_target_pairs={{2,4},{4,2},{3,5},{5,3},{10,12},{12,10},{11,13},{13,11},{18,20},{2... | collective-permute-start | bytes 786440 | tf_op jit(solution)/shard_map/ppermute | solution.py:70
  72.9 10.3 %collective-permute-start.8 = (bf16[64,2048]{1,0:T(8,128)(2,1)}, bf16[64,2048]{1,0:T(8,128)(2,1)}, u32[]{:S(2)}, u32[]{:S(2)}) collective-permute-start(bf16[64,2048]{1,0:T(8,128)(2,1)} %add_convert_fusion.4), channel_id=1, source_target_pairs={{2,4},{4,2},{3,5},{5,3},{10,12},{12,10},{11,13},{13,11},{18,20},{2... | collective-permute-start | bytes 786440 | tf_op jit(solution)/shard_map/ppermute | solution.py:70
  78.4 6.8 %copy-start.2 = (bf16[1,1,2048,512]{3,2,1,0:T(8,128)(2,1)S(1)}, bf16[1,1,2048,512]{3,2,1,0:T(8,128)(2,1)}, u32[]{:S(2)}) copy-start(bf16[1,1,2048,512]{3,2,1,0:T(8,128)(2,1)} %param.9) | copy-start | bytes 6291460
  79.8 8.4 %collective-permute-start.16 = (bf16[64,2048]{1,0:T(8,128)(2,1)S(1)}, bf16[64,2048]{1,0:T(8,128)(2,1)}, u32[]{:S(2)}, u32[]{:S(2)}) collective-permute-start(bf16[64,2048]{1,0:T(8,128)(2,1)S(1)} %add_convert_fusion.1), channel_id=1, source_target_pairs={{2,4},{4,2},{3,5},{5,3},{10,12},{12,10},{11,13},{13,11},{18,20},{2... | collective-permute-start | bytes 786440 | tf_op jit(solution)/shard_map/ppermute | solution.py:70
  85.2 7.4 %collective-permute-start.9 = (bf16[64,2048]{1,0:T(8,128)(2,1)}, bf16[64,2048]{1,0:T(8,128)(2,1)}, u32[]{:S(2)}, u32[]{:S(2)}) collective-permute-start(bf16[64,2048]{1,0:T(8,128)(2,1)} %fusion.66), channel_id=1, source_target_pairs={{0,2},{2,0},{4,6},{6,4},{1,3},{3,1},{5,7},{7,5},{8,10},{10,8},{12,... | collective-permute-start | bytes 786440 | tf_op jit(solution)/shard_map/ppermute | solution.py:67
  88.1 10.8 %copy-start.11 = (f32[128]{0:T(128)S(1)}, f32[128]{0:T(128)}, u32[]{:S(2)}) copy-start(f32[128]{0:T(128)} %fusion.107) | copy-start | bytes 1540
  91.4 11.0 %collective-permute-start.17 = (bf16[64,2048]{1,0:T(8,128)(2,1)}, bf16[64,2048]{1,0:T(8,128)(2,1)}, u32[]{:S(2)}, u32[]{:S(2)}) collective-permute-start(bf16[64,2048]{1,0:T(8,128)(2,1)} %fusion.65), channel_id=1, source_target_pairs={{0,2},{2,0},{4,6},{6,4},{1,3},{3,1},{5,7},{7,5},{8,10},{10,8},{12,... | collective-permute-start | bytes 786440 | tf_op jit(solution)/shard_map/ppermute | solution.py:67
  94.3 9.2 %copy-start.6 = (bf16[64,2048]{1,0:T(8,128)(2,1)S(1)}, bf16[64,2048]{1,0:T(8,128)(2,1)}, u32[]{:S(2)}) copy-start(bf16[64,2048]{1,0:T(8,128)(2,1)} %copy-done.5) | copy-start | bytes 786436
  94.3 9.2 %collective-permute-start.18 = (bf16[64,2048]{1,0:T(8,128)(2,1)}, bf16[64,2048]{1,0:T(8,128)(2,1)S(1)}, u32[]{:S(2)}, u32[]{:S(2)}) collective-permute-start(bf16[64,2048]{1,0:T(8,128)(2,1)} %fusion.58), channel_id=1, source_target_pairs={{2,4},{4,2},{3,5},{5,3},{10,12},{12,10},{11,13},{13,11},{18,20},{2... | collective-permute-start | bytes 786440 | tf_op jit(solution)/shard_map/ppermute | solution.py:70
  105.1 7.7 %collective-permute-start.19 = (bf16[64,2048]{1,0:T(8,128)(2,1)S(1)}, bf16[64,2048]{1,0:T(8,128)(2,1)S(1)}, u32[]{:S(2)}, u32[]{:S(2)}) collective-permute-start(bf16[64,2048]{1,0:T(8,128)(2,1)S(1)} %get-tuple-element.2), channel_id=1, source_target_pairs={{0,8},{8,16},{16,24},{1,9},{9,17},{17,25},{2,10},{10,18},{18,26},{... | collective-permute-start | bytes 786440 | tf_op jit(solution)/shard_map/ppermute | solution.py:10
  107.1 8.6 %collective-permute-start.20 = (bf16[64,2048]{1,0:T(8,128)(2,1)S(1)}, bf16[64,2048]{1,0:T(8,128)(2,1)S(1)}, u32[]{:S(2)}, u32[]{:S(2)}) collective-permute-start(bf16[64,2048]{1,0:T(8,128)(2,1)S(1)} %get-tuple-element.3), channel_id=1, source_target_pairs={{0,8},{8,16},{16,24},{1,9},{9,17},{17,25},{2,10},{10,18},{18,26},{... | collective-permute-start | bytes 786440 | tf_op jit(solution)/shard_map/ppermute | solution.py:10
  (1 other events, 0.7 us)

commit v2 on v0

--- a/solution.py
+++ b/solution.py
@@ -1,6 +1,8 @@
 import jax
 import jax.numpy as jnp
 from jax import lax
+from jax.experimental import pallas as pl
+from jax.experimental.pallas import tpu as pltpu
 from jax.sharding import PartitionSpec as P
 
 
@@ -10,7 +12,7 @@
     return lax.ppermute(value, axis, [(source, source + steps) for source in range(leading, last)])
 
 
-def per_device(tokens, routes, route_weights, expert_gate, expert_up, expert_down):
+def by_slots(tokens, routes, route_weights, expert_gate, expert_up, expert_down):
     rows_in = tokens[0]
     tok_count, width = rows_in.shape
     top_count = routes.shape[2]
@@ -52,6 +54,240 @@
     return (layer_out[None], handed[None])
 
 
+OUTER = [(0, 1), (1, 0), (2, 3), (3, 2)]
+INNER = [(1, 2), (2, 1)]
+IN_VMEM = pl.BlockSpec(memory_space=pltpu.VMEM)
+ANYWHERE = pl.BlockSpec(memory_space=pl.ANY)
+
+
+def held(shape, dtype=jnp.bfloat16):
+    return pltpu.VMEM(shape, dtype)
+
+
+def wide(ref):
+    return ref[...].astype(jnp.float32)
+
+
+def narrow(value):
+    return value.astype(jnp.bfloat16)
+
+
+def position():
+    me = lax.axis_index("expert")
+    return me, (me == 0) | (me == 3)
+
+
+def run(body, name, out_shape, *operands, scratch=(), specs=None, out_specs=None, work=(0, 0)):
+    several = isinstance(out_shape, list)
+    specs = specs or [IN_VMEM] * len(operands)
+    operands = [
+        pltpu.with_memory_space_constraint(x, pltpu.VMEM if s is IN_VMEM else pltpu.HBM)
+        for x, s in zip(operands, specs)
+    ]
+    return pl.pallas_call(
+        body,
+        out_shape=out_shape,
+        in_specs=specs,
+        out_specs=out_specs or ([IN_VMEM] * len(out_shape) if several else IN_VMEM),
+        scratch_shapes=list(scratch),
+        compiler_params=pltpu.CompilerParams(vmem_limit_bytes=24 * 2**20),
+        cost_estimate=pl.CostEstimate(flops=work[0], bytes_accessed=work[1], transcendentals=0),
+        name=name,
+    )(*operands)
+
+
+def prepare(tokens, routes, weights, first, second, table, sems):
+    half = first.shape[0]
+    copies = [
+        pltpu.make_async_copy(tokens.at[pl.ds(i * half, half)], part, sems.at[i])
+        for i, part in enumerate((first, second))
+    ]
+    for copy in copies:
+        copy.start()
+    names = lax.broadcasted_iota(jnp.int32, table.shape, 0)
+    total = jnp.zeros(table.shape, jnp.float32)
+    for k in range(routes.shape[0]):
+        total += jnp.where(routes[k : k + 1, :] == names, weights[k : k + 1, :], 0.0)
+    table[...] = total
+    for copy in copies:
+        copy.wait()
+
+
+def column(table, me, start, count):
+    names = lax.broadcasted_iota(jnp.int32, table.shape, 0)
+    row = jnp.sum(jnp.where(names == me, table, 0.0), axis=0, keepdims=True)[:, start : start + count]
+    across = lax.broadcasted_iota(jnp.int32, (count, count), 1)
+    down = lax.broadcasted_iota(jnp.int32, (count, count), 0)
+    return jnp.sum(jnp.where(across == down, row, 0.0), axis=1, keepdims=True)
+
+
+def expert_of(rows, gate_w, up_w, down_w):
+    gate = jnp.dot(rows, gate_w[...], preferred_element_type=jnp.float32)
+    up = jnp.dot(rows, up_w[...], preferred_element_type=jnp.float32)
+    hidden = narrow(gate / (1.0 + jnp.exp(-gate)) * up)
+    out = jnp.dot(hidden, down_w[...], preferred_element_type=jnp.float32)
+    return narrow(out).astype(jnp.float32)
+
+
+def own_pass(first, second, table, *refs):
+    from_hbm, to_vmem, totals, sems = refs[0:3], refs[3:6], refs[6:8], refs[8]
+    copies = [
+        pltpu.make_async_copy(a, b, sems.at[i]) for i, (a, b) in enumerate(zip(from_hbm, to_vmem))
+    ]
+    for copy in copies:
+        copy.start()
+    me, _ = position()
+    for copy in copies:
+        copy.wait()
+    half = first.shape[0]
+    for i, part in enumerate((first, second)):
+        out = expert_of(part[...], *to_vmem)
+        totals[i][...] = wide(part) + out * column(table[...], me, i * half, half)
+
+
+def pass_of(partner, late):
+    def body(at_end, at_mid, table_a, table_b, table_c, gate_w, up_w, down_w, result):
+        me, end = position()
+        half = result.shape[0]
+        if partner == 0:
+            came = jnp.where(me % 2 == 0, 3, 1)
+        elif partner == 1:
+            came = jnp.where(me == 1, 3, jnp.where(me == 2, 1, 2))
+        else:
+            came = jnp.where(me == 0, 1, jnp.where(me == 3, 3, 2))
+        table = jnp.where(came == 1, table_a[...], jnp.where(came == 2, table_b[...], table_c[...]))
+        rows = jnp.where(end, at_end[...], at_mid[...])
+        weight = column(table, me, half if late else 0, half)
+        result[...] = narrow(expert_of(rows, gate_w, up_w, down_w) * weight)
+
+    return body
+
+
+def choose(at_end, at_mid, result):
+    _, end = position()
+    result[...] = jnp.where(end, at_end[...], at_mid[...])
+
+
+def choose_sum(at_end, mid_a, mid_b, result):
+    _, end = position()
+    result[...] = jnp.where(end, at_end[...], narrow(wide(mid_a) + wide(mid_b)))
+
+
+def add(a, b, result):
+    result[...] = narrow(wide(a) + wide(b))
+
+
+def finish_first(total, far, near, inner, result):
+    _, end = position()
+    result[...] = narrow(total[...] + jnp.where(end, wide(far), wide(near) + wide(inner)))
+
+
+def finish_second(total, outer, inner, result):
+    _, end = position()
+    result[...] = narrow(total[...] + wide(outer) + jnp.where(end, 0.0, wide(inner)))
+
+
+def join(first, second, whole, sems):
+    half = first.shape[0]
+    copies = [
+        pltpu.make_async_copy(part, whole.at[pl.ds(i * half, half)], sems.at[i])
+        for i, part in enumerate((first, second))
+    ]
+    for copy in copies:
+        copy.start()
+    for copy in copies:
+        copy.wait()
+
+
+def on_line(tokens, routes, route_weights, expert_gate, expert_up, expert_down):
+    rows = tokens[0]
+    count, width = rows.shape
+    half = count // 2
+    block = (half, width)
+    weights = (expert_gate[0, 0], expert_up[0, 0], expert_down[0, 0])
+    two_sems = [pltpu.SemaphoreType.DMA((2,))]
+
+    def outer(value):
+        return lax.ppermute(value, "expert", OUTER)
+
+    def inner(value):
+        return lax.ppermute(value, "expert", INNER)
+
+    def turned(value, by):
+        return lax.ppermute(value, "expert", [(s, (s + by) % 4) for s in range(4)])
+
+    first, second, table = run(
+        prepare,
+        "prepare",
+        [held(block), held(block), held((4, count), jnp.float32)],
+        rows,
+        routes[0].T,
+        route_weights[0].T,
+        scratch=two_sems,
+        specs=[ANYWHERE, IN_VMEM, IN_VMEM],
+    )
+    o0, i0 = outer(first), inner(first)
+    tables = [turned(table, by) for by in (1, 2, 3)]
+    *weights, total_first, total_second = run(
+        own_pass,
+        "own_pass",
+        [held(w.shape) for w in weights] + [held(block, jnp.float32)] * 2,
+        first,
+        second,
+        table,
+        *weights,
+        scratch=[pltpu.SemaphoreType.DMA((3,))],
+        specs=[IN_VMEM] * 3 + [ANYWHERE] * 3,
+        work=(6 * count * weights[0].size, 6 * weights[0].size),
+    )
+
+    def expert(partner, late, at_end, at_mid):
+        return run(
+            pass_of(partner, late),
+            "expert_pass",
+            held(block),
+            at_end,
+            at_mid,
+            *tables,
+            *weights,
+            work=(6 * half * weights[0].size, 6 * weights[0].size),
+        )
+
+    def mixed(body, *operands):
+        return run(body, body.__name__, held(block), *operands)
+
+    o1, i1 = outer(mixed(choose, second, i0)), inner(o0)
+    p1 = expert(0, False, o0, o0)
+    o2, i2 = outer(mixed(choose, p1, i1)), inner(o1)
+    p2 = expert(1, False, o1, i0)
+    o3, i3 = outer(mixed(choose, p2, i2)), inner(second)
+    p3 = expert(2, False, o2, i1)
+    o4, i4 = outer(mixed(choose, p3, i3)), inner(mixed(add, o3, p2))
+    p4 = expert(2, True, o3, i2)
+    o5, i5 = outer(mixed(choose, p4, second)), inner(mixed(add, o4, p3))
+    p5 = expert(1, True, o4, i3)
+    o6, i6 = outer(mixed(choose_sum, p5, i5, p1)), inner(mixed(add, o5, p4))
+    p6 = expert(0, True, o5, o1)
+    o7, i7 = outer(mixed(choose_sum, p6, i6, p6)), inner(mixed(add, o6, p5))
+    out_first = mixed(finish_first, total_first, o6, o2, i4)
+    next_first = passed_along(out_first, "section", 1)
+    out_second = mixed(finish_second, total_second, o7, i7)
+    next_second = passed_along(out_second, "section", 1)
+
+    def joined(a, b):
+        return run(
+            join,
+            "join",
+            jax.ShapeDtypeStruct((count, width), jnp.bfloat16),
+            a,
+            b,
+            scratch=two_sems,
+            out_specs=ANYWHERE,
+        )
+
+    return (joined(out_first, out_second)[None], joined(next_first, next_second)[None])
+
+
 def solution(mesh):
     in_specs = (
         P("section", ("expert", "tensor"), None),
@@ -62,6 +298,12 @@
         P("section", "expert", None, None),
     )
     out_specs = (P("section", ("expert", "tensor"), None), P("section", ("expert", "tensor"), None))
+
+    def per_device(*args):
+        tokens, expert_gate = args[0], args[3]
+        line = mesh.shape["expert"] == 4 and expert_gate.shape[1] == 1 and tokens.shape[1] % 32 == 0
+        return (on_line if line else by_slots)(*args)
+
     return jax.shard_map(
         per_device, mesh=mesh, in_specs=in_specs, out_specs=out_specs, check_vma=False
     )

time: 149 us -> 83.3 us (0.56)
  the two profiles are of different devices: /device:TPU:1 before, /device:TPU:12 now
where the time goes in v2:
time: 83.3 us; the launch traced here: 82.9 us
  starting transfers between devices  36.7 us (44%)
  waiting for transfers between devices  27.3 us (33%)
  Pallas kernels  16.6 us (20%)
  local copies, waits for them, and re-layouts  1.35 us (2%)
  between operations  0.97 us (1%)
    ppermute x8, starting transfers between devices, inner(): return lax.ppermute(value, 'expert', INNER)  26.1 us
    pallas_call x23, Pallas kernels, run(): pl.pallas_call(body, out_shape=out_shape, in_specs=specs, out_specs=out_s...  16.6 us
    ppermute x8, waiting for transfers between devices, outer(): return lax.ppermute(value, 'expert', OUTER)  11.2 us
    ppermute x8, waiting for transfers between devices, inner(): return lax.ppermute(value, 'expert', INNER)  11.1 us
    ppermute x2, waiting for transfers between devices, passed_along(): lax.ppermute(value, axis, [(source, source + steps) for source in range(l...  4.95 us
    ppermute x3, starting transfers between devices, turned(): return lax.ppermute(value, 'expert', [(s, (s + by) % 4) for s in range(4)])  4.73 us
    ppermute x2, starting transfers between devices, passed_along(): lax.ppermute(value, axis, [(source, source + steps) for source in range(l...  3.84 us
    ppermute x8, starting transfers between devices, outer(): return lax.ppermute(value, 'expert', OUTER)  2.11 us
  transfers between devices with their start and end apart: 21, of which 12 were waited for; matrix products, arithmetic and copies ran while one was open for 0% of the time, Pallas kernels for 18%

profile of v2, /device:TPU:12, one launch (start us, length us, event | category | flops | bytes accessed | tf_op | source)
XLA Modules:
  0.0 82.9 jit_solution(17903146761026839060)
XLA Ops:
  2.0 1.0 %prepare.1 = (bf16[64,2048]{1,0:T(8,128)(2,1)S(1)}, bf16[64,2048]{1,0:T(8,128)(2,1)S(1)}, f32[4,128]{1,0:T(4,128)S(1)}) custom-call(bf16[128,2048]{1,0:T(8,128)(2,1)} %bitcast.17, s32[2,128]{1,0:T(2,128)S(1)} %bitcast.12, f32[2,128]{1,0:T(2,128)S(1)} %bitcast.13), custom_call_target="tpu_custom_call" | custom-call | tf_op jit(solution)/shard_map/prepare/pallas_call | solution.py:87
  3.6 4.6 %collective-permute-start.10 = (bf16[64,2048]{1,0:T(8,128)(2,1)S(1)}, bf16[64,2048]{1,0:T(8,128)(2,1)S(1)}, u32[]{:S(2)}, u32[]{:S(2)}) collective-permute-start(bf16[64,2048]{1,0:T(8,128)(2,1)S(1)} %get-tuple-element.10.first), channel_id=1, source_target_pairs={{2,4},{4,2},{3,5},{5,3},{10,12},{12,10},{11,13},{13,11},{18,20},{2... | collective-permute-start | bytes 786440 | tf_op jit(solution)/shard_map/ppermute | solution.py:214
  8.2 3.0 %collective-permute-done.at_end.at_mid = bf16[64,2048]{1,0:T(8,128)(2,1)S(1)} collective-permute-done((bf16[64,2048]{1,0:T(8,128)(2,1)S(1)}, bf16[64,2048]{1,0:T(8,128)(2,1)S(1)}, u32[]{:S(2)}, u32[]{:S(2)}) %collective-permute-start) | collective-permute-done | bytes 262176 | tf_op jit(solution)/shard_map/ppermute | solution.py:211
  11.2 3.5 %collective-permute-start.4 = (bf16[64,2048]{1,0:T(8,128)(2,1)S(1)}, bf16[64,2048]{1,0:T(8,128)(2,1)S(1)}, u32[]{:S(2)}, u32[]{:S(2)}) collective-permute-start(bf16[64,2048]{1,0:T(8,128)(2,1)S(1)} %collective-permute-done.at_end.at_mid), channel_id=1, source_target_pairs={{2,4},{4,2},{3,5},{5,3},{10,12},{12,10},{11,13},{13,11},{18,20},{2... | collective-permute-start | bytes 786440 | tf_op jit(solution)/shard_map/ppermute | solution.py:214
  14.8 1.3 %collective-permute-start.1 = (f32[4,128]{1,0:T(4,128)S(1)}, f32[4,128]{1,0:T(4,128)S(1)}, u32[]{:S(2)}, u32[]{:S(2)}) collective-permute-start(f32[4,128]{1,0:T(4,128)S(1)} %get-tuple-element.12.table), channel_id=1, source_target_pairs={{0,2},{2,4},{4,6},{6,0},{1,3},{3,5},{5,7},{7,1},{8,10},{10,12},{12... | collective-permute-start | bytes 6152 | tf_op jit(solution)/shard_map/ppermute | solution.py:217
  16.1 3.1 %collective-permute-start.2 = (f32[4,128]{1,0:T(4,128)S(1)}, f32[4,128]{1,0:T(4,128)S(1)}, u32[]{:S(2)}, u32[]{:S(2)}) collective-permute-start(f32[4,128]{1,0:T(4,128)S(1)} %get-tuple-element.12.table), channel_id=1, source_target_pairs={{0,4},{2,6},{4,0},{6,2},{1,5},{3,7},{5,1},{7,3},{8,12},{10,14},{12... | collective-permute-start | bytes 6152 | tf_op jit(solution)/shard_map/ppermute | solution.py:217
  19.5 5.4 %own_pass.1 = (bf16[2048,512]{1,0:T(8,128)(2,1)S(1)}, bf16[2048,512]{1,0:T(8,128)(2,1)S(1)}, bf16[512,2048]{1,0:T(8,128)(2,1)S(1)}, f32[64,2048]{1,0:T(8,128)S(1)}, f32[64,2048]{1,0:T(8,128)S(1)}) custom-call(bf16[64,2048]{1,0:T(8,128)(2,1)S(1)} %get-tuple-element.10.first, bf16[64,2048]{1,0:T(8,128)(2,1)S(1)} %get-tuple-element.11.second.at_end.at_mid, ...), custom_call_target="tpu_custom_call" | custom-call | flops 805306368 | bytes 6291456 | tf_op jit(solution)/shard_map/own_pass/pallas_call | solution.py:87
  24.9 1.3 %expert_pass.6.at_end.mid_b = bf16[64,2048]{1,0:T(8,128)(2,1)S(1)} custom-call(bf16[64,2048]{1,0:T(8,128)(2,1)S(1)} %collective-permute-done.at_end.at_mid, bf16[64,2048]{1,0:T(8,128)(2,1)S(1)} %collective-permute-done.at_end.at_mid, f32[4,128]{1,0:T(4,128)S(1)} %collective-permute-done.1.table_a, f32[4,128]{1,0:T(4,128)S(1)} %collective-permute-done.2.table_b, ...), custom_call_target="tpu_custom_call" | custom-call | flops 402653184 | bytes 6291456 | tf_op jit(solution)/shard_map/expert_pass/pallas_call | solution.py:87
  26.3 1.2 %collective-permute-start.5 = (bf16[64,2048]{1,0:T(8,128)(2,1)S(1)}, bf16[64,2048]{1,0:T(8,128)(2,1)S(1)}, u32[]{:S(2)}, u32[]{:S(2)}) collective-permute-start(bf16[64,2048]{1,0:T(8,128)(2,1)S(1)} %choose.5), channel_id=1, source_target_pairs={{0,2},{2,0},{4,6},{6,4},{1,3},{3,1},{5,7},{7,5},{8,10},{10,8},{12,... | collective-permute-start | bytes 786440 | tf_op jit(solution)/shard_map/ppermute | solution.py:211
  27.4 2.5 %collective-permute-start.6 = (bf16[64,2048]{1,0:T(8,128)(2,1)S(1)}, bf16[64,2048]{1,0:T(8,128)(2,1)S(1)}, u32[]{:S(2)}, u32[]{:S(2)}) collective-permute-start(bf16[64,2048]{1,0:T(8,128)(2,1)S(1)} %get-tuple-element.11.second.at_end.at_mid), channel_id=1, source_target_pairs={{2,4},{4,2},{3,5},{5,3},{10,12},{12,10},{11,13},{13,11},{18,20},{2... | collective-permute-start | bytes 786440 | tf_op jit(solution)/shard_map/ppermute | solution.py:214
  29.9 3.3 %collective-permute-start.12 = (bf16[64,2048]{1,0:T(8,128)(2,1)S(1)}, bf16[64,2048]{1,0:T(8,128)(2,1)S(1)}, u32[]{:S(2)}, u32[]{:S(2)}) collective-permute-start(bf16[64,2048]{1,0:T(8,128)(2,1)S(1)} %collective-permute-done.11.at_end.at_mid), channel_id=1, source_target_pairs={{2,4},{4,2},{3,5},{5,3},{10,12},{12,10},{11,13},{13,11},{18,20},{2... | collective-permute-start | bytes 786440 | tf_op jit(solution)/shard_map/ppermute | solution.py:214
  33.3 1.3 %expert_pass.9.at_end.b = bf16[64,2048]{1,0:T(8,128)(2,1)S(1)} custom-call(bf16[64,2048]{1,0:T(8,128)(2,1)S(1)} %collective-permute-done.11.at_end.at_mid, bf16[64,2048]{1,0:T(8,128)(2,1)S(1)} %collective-permute-done.10.at_mid, f32[4,128]{1,0:T(4,128)S(1)} %collective-permute-done.1.table_a, f32[4,128]{1,0:T(4,128)S(1)} %collective-permute-done.2.table_b, ...), custom_call_target="tpu_custom_call" | custom-call | flops 402653184 | bytes 6291456 | tf_op jit(solution)/shard_map/expert_pass/pallas_call | solution.py:87
  34.6 1.3 %expert_pass.7.at_end.b = bf16[64,2048]{1,0:T(8,128)(2,1)S(1)} custom-call(bf16[64,2048]{1,0:T(8,128)(2,1)S(1)} %collective-permute-done.5.at_end.near, bf16[64,2048]{1,0:T(8,128)(2,1)S(1)} %collective-permute-done.4.at_mid, f32[4,128]{1,0:T(4,128)S(1)} %collective-permute-done.1.table_a, f32[4,128]{1,0:T(4,128)S(1)} %collective-permute-done.2.table_b, ...), custom_call_target="tpu_custom_call" | custom-call | flops 402653184 | bytes 6291456 | tf_op jit(solution)/shard_map/expert_pass/pallas_call | solution.py:87
  35.9 2.0 %collective-permute-done.6.at_mid = bf16[64,2048]{1,0:T(8,128)(2,1)S(1)} collective-permute-done((bf16[64,2048]{1,0:T(8,128)(2,1)S(1)}, bf16[64,2048]{1,0:T(8,128)(2,1)S(1)}, u32[]{:S(2)}, u32[]{:S(2)}) %collective-permute-start.6) | collective-permute-done | bytes 262176 | tf_op jit(solution)/shard_map/ppermute | solution.py:214
  38.0 2.7 %collective-permute-done.12.at_mid = bf16[64,2048]{1,0:T(8,128)(2,1)S(1)} collective-permute-done((bf16[64,2048]{1,0:T(8,128)(2,1)S(1)}, bf16[64,2048]{1,0:T(8,128)(2,1)S(1)}, u32[]{:S(2)}, u32[]{:S(2)}) %collective-permute-start.12) | collective-permute-done | bytes 262176 | tf_op jit(solution)/shard_map/ppermute | solution.py:214
  40.8 4.8 %collective-permute-done.7.at_end.a = bf16[64,2048]{1,0:T(8,128)(2,1)S(1)} collective-permute-done((bf16[64,2048]{1,0:T(8,128)(2,1)S(1)}, bf16[64,2048]{1,0:T(8,128)(2,1)S(1)}, u32[]{:S(2)}, u32[]{:S(2)}) %collective-permute-start.7) | collective-permute-done | bytes 262176 | tf_op jit(solution)/shard_map/ppermute | solution.py:211
  45.8 3.1 %collective-permute-start.8 = (bf16[64,2048]{1,0:T(8,128)(2,1)S(1)}, bf16[64,2048]{1,0:T(8,128)(2,1)S(1)}, u32[]{:S(2)}, u32[]{:S(2)}) collective-permute-start(bf16[64,2048]{1,0:T(8,128)(2,1)S(1)} %add.4), channel_id=1, source_target_pairs={{2,4},{4,2},{3,5},{5,3},{10,12},{12,10},{11,13},{13,11},{18,20},{2... | collective-permute-start | bytes 786440 | tf_op jit(solution)/shard_map/ppermute | solution.py:214
  48.9 1.3 %expert_pass.10.at_end.b = bf16[64,2048]{1,0:T(8,128)(2,1)S(1)} custom-call(bf16[64,2048]{1,0:T(8,128)(2,1)S(1)} %collective-permute-done.13.a.at_end, bf16[64,2048]{1,0:T(8,128)(2,1)S(1)} %collective-permute-done.12.at_mid, f32[4,128]{1,0:T(4,128)S(1)} %collective-permute-done.1.table_a, f32[4,128]{1,0:T(4,128)S(1)} %collective-permute-done.2.table_b, ...), custom_call_target="tpu_custom_call" | custom-call | flops 402653184 | bytes 6291456 | tf_op jit(solution)/shard_map/expert_pass/pallas_call | solution.py:87
  50.3 1.3 %expert_pass.8.at_end.b = bf16[64,2048]{1,0:T(8,128)(2,1)S(1)} custom-call(bf16[64,2048]{1,0:T(8,128)(2,1)S(1)} %collective-permute-done.7.at_end.a, bf16[64,2048]{1,0:T(8,128)(2,1)S(1)} %collective-permute-done.6.at_mid, f32[4,128]{1,0:T(4,128)S(1)} %collective-permute-done.1.table_a, f32[4,128]{1,0:T(4,128)S(1)} %collective-permute-done.2.table_b, ...), custom_call_target="tpu_custom_call" | custom-call | flops 402653184 | bytes 6291456 | tf_op jit(solution)/shard_map/expert_pass/pallas_call | solution.py:87
  51.6 2.4 %collective-permute-done.8.mid_a = bf16[64,2048]{1,0:T(8,128)(2,1)S(1)} collective-permute-done((bf16[64,2048]{1,0:T(8,128)(2,1)S(1)}, bf16[64,2048]{1,0:T(8,128)(2,1)S(1)}, u32[]{:S(2)}, u32[]{:S(2)}) %collective-permute-start.8) | collective-permute-done | bytes 262176 | tf_op jit(solution)/shard_map/ppermute | solution.py:214
  54.2 2.7 %collective-permute-done.15.at_end.a = bf16[64,2048]{1,0:T(8,128)(2,1)S(1)} collective-permute-done((bf16[64,2048]{1,0:T(8,128)(2,1)S(1)}, bf16[64,2048]{1,0:T(8,128)(2,1)S(1)}, u32[]{:S(2)}, u32[]{:S(2)}) %collective-permute-start.15) | collective-permute-done | bytes 262176 | tf_op jit(solution)/shard_map/ppermute | solution.py:211
  57.0 3.2 %collective-permute-start.16 = (bf16[64,2048]{1,0:T(8,128)(2,1)S(1)}, bf16[64,2048]{1,0:T(8,128)(2,1)S(1)}, u32[]{:S(2)}, u32[]{:S(2)}) collective-permute-start(bf16[64,2048]{1,0:T(8,128)(2,1)S(1)} %add.6), channel_id=1, source_target_pairs={{2,4},{4,2},{3,5},{5,3},{10,12},{12,10},{11,13},{13,11},{18,20},{2... | collective-permute-start | bytes 786440 | tf_op jit(solution)/shard_map/ppermute | solution.py:214
  60.3 2.6 %collective-permute-start.14 = (bf16[64,2048]{1,0:T(8,128)(2,1)S(1)}, bf16[64,2048]{1,0:T(8,128)(2,1)S(1)}, u32[]{:S(2)}, u32[]{:S(2)}) collective-permute-start(bf16[64,2048]{1,0:T(8,128)(2,1)S(1)} %add.5), channel_id=1, source_target_pairs={{2,4},{4,2},{3,5},{5,3},{10,12},{12,10},{11,13},{13,11},{18,20},{2... | collective-permute-start | bytes 786440 | tf_op jit(solution)/shard_map/ppermute | solution.py:214
  62.9 1.3 %expert_pass.11.at_end.mid_b = bf16[64,2048]{1,0:T(8,128)(2,1)S(1)} custom-call(bf16[64,2048]{1,0:T(8,128)(2,1)S(1)} %collective-permute-done.15.at_end.a, bf16[64,2048]{1,0:T(8,128)(2,1)S(1)} %collective-permute-done.11.at_end.at_mid, f32[4,128]{1,0:T(4,128)S(1)} %collective-permute-done.1.table_a, f32[4,128]{1,0:T(4,128)S(1)} %collective-permute-done.2.table_b, ...), custom_call_target="tpu_custom_call" | custom-call | flops 402653184 | bytes 6291456 | tf_op jit(solution)/shard_map/expert_pass/pallas_call | solution.py:87
  64.3 3.2 %collective-permute-start.18 = (bf16[64,2048]{1,0:T(8,128)(2,1)S(1)}, bf16[64,2048]{1,0:T(8,128)(2,1)S(1)}, u32[]{:S(2)}, u32[]{:S(2)}) collective-permute-start(bf16[64,2048]{1,0:T(8,128)(2,1)S(1)} %add.7), channel_id=1, source_target_pairs={{2,4},{4,2},{3,5},{5,3},{10,12},{12,10},{11,13},{13,11},{18,20},{2... | collective-permute-start | bytes 786440 | tf_op jit(solution)/shard_map/ppermute | solution.py:214
  67.9 2.9 %collective-permute-done.14.inner = bf16[64,2048]{1,0:T(8,128)(2,1)S(1)} collective-permute-done((bf16[64,2048]{1,0:T(8,128)(2,1)S(1)}, bf16[64,2048]{1,0:T(8,128)(2,1)S(1)}, u32[]{:S(2)}, u32[]{:S(2)}) %collective-permute-start.14) | collective-permute-done | bytes 262176 | tf_op jit(solution)/shard_map/ppermute | solution.py:214
  71.0 1.9 %collective-permute-start.19 = (bf16[64,2048]{1,0:T(8,128)(2,1)S(1)}, bf16[64,2048]{1,0:T(8,128)(2,1)S(1)}, u32[]{:S(2)}, u32[]{:S(2)}) collective-permute-start(bf16[64,2048]{1,0:T(8,128)(2,1)S(1)} %finish_first.1.first), channel_id=1, source_target_pairs={{0,8},{8,16},{16,24},{1,9},{9,17},{17,25},{2,10},{10,18},{18,26},{... | collective-permute-start | bytes 786440 | tf_op jit(solution)/shard_map/ppermute | solution.py:12
  74.4 1.9 %collective-permute-start.20 = (bf16[64,2048]{1,0:T(8,128)(2,1)S(1)}, bf16[64,2048]{1,0:T(8,128)(2,1)S(1)}, u32[]{:S(2)}, u32[]{:S(2)}) collective-permute-start(bf16[64,2048]{1,0:T(8,128)(2,1)S(1)} %finish_second.1.second), channel_id=1, source_target_pairs={{0,8},{8,16},{16,24},{1,9},{9,17},{17,25},{2,10},{10,18},{18,26},{... | collective-permute-start | bytes 786440 | tf_op jit(solution)/shard_map/ppermute | solution.py:12
  76.3 0.8 join.2
  77.2 1.5 %collective-permute-done.19.first = bf16[64,2048]{1,0:T(8,128)(2,1)S(1)} collective-permute-done((bf16[64,2048]{1,0:T(8,128)(2,1)S(1)}, bf16[64,2048]{1,0:T(8,128)(2,1)S(1)}, u32[]{:S(2)}, u32[]{:S(2)}) %collective-permute-start.19) | collective-permute-done | bytes 262176 | tf_op jit(solution)/shard_map/ppermute | solution.py:12
  78.7 3.4 %collective-permute-done.20.second = bf16[64,2048]{1,0:T(8,128)(2,1)S(1)} collective-permute-done((bf16[64,2048]{1,0:T(8,128)(2,1)S(1)}, bf16[64,2048]{1,0:T(8,128)(2,1)S(1)}, u32[]{:S(2)}, u32[]{:S(2)}) %collective-permute-start.20) | collective-permute-done | bytes 262176 | tf_op jit(solution)/shard_map/ppermute | solution.py:12
  82.1 0.8 join.3
  (37 shorter events, 5.1 us)
Async XLA Ops:
  0.6 0.7 copy-start
  1.3 0.7 copy-start.1
  3.0 8.1 %collective-permute-start = (bf16[64,2048]{1,0:T(8,128)(2,1)S(1)}, bf16[64,2048]{1,0:T(8,128)(2,1)S(1)}, u32[]{:S(2)}, u32[]{:S(2)}) collective-permute-start(bf16[64,2048]{1,0:T(8,128)(2,1)S(1)} %get-tuple-element.10.first), channel_id=1, source_target_pairs={{0,2},{2,0},{4,6},{6,4},{1,3},{3,1},{5,7},{7,5},{8,10},{10,8},{12,... | collective-permute-start | bytes 786440 | tf_op jit(solution)/shard_map/ppermute | solution.py:211
  3.6 11.1 %collective-permute-start.10 = (bf16[64,2048]{1,0:T(8,128)(2,1)S(1)}, bf16[64,2048]{1,0:T(8,128)(2,1)S(1)}, u32[]{:S(2)}, u32[]{:S(2)}) collective-permute-start(bf16[64,2048]{1,0:T(8,128)(2,1)S(1)} %get-tuple-element.10.first), channel_id=1, source_target_pairs={{2,4},{4,2},{3,5},{5,3},{10,12},{12,10},{11,13},{13,11},{18,20},{2... | collective-permute-start | bytes 786440 | tf_op jit(solution)/shard_map/ppermute | solution.py:214
  11.2 15.1 %collective-permute-start.4 = (bf16[64,2048]{1,0:T(8,128)(2,1)S(1)}, bf16[64,2048]{1,0:T(8,128)(2,1)S(1)}, u32[]{:S(2)}, u32[]{:S(2)}) collective-permute-start(bf16[64,2048]{1,0:T(8,128)(2,1)S(1)} %collective-permute-done.at_end.at_mid), channel_id=1, source_target_pairs={{2,4},{4,2},{3,5},{5,3},{10,12},{12,10},{11,13},{13,11},{18,20},{2... | collective-permute-start | bytes 786440 | tf_op jit(solution)/shard_map/ppermute | solution.py:214
  14.7 15.3 %collective-permute-start.11 = (bf16[64,2048]{1,0:T(8,128)(2,1)S(1)}, bf16[64,2048]{1,0:T(8,128)(2,1)S(1)}, u32[]{:S(2)}, u32[]{:S(2)}) collective-permute-start(bf16[64,2048]{1,0:T(8,128)(2,1)S(1)} %choose.7), channel_id=1, source_target_pairs={{0,2},{2,0},{4,6},{6,4},{1,3},{3,1},{5,7},{7,5},{8,10},{10,8},{12,... | collective-permute-start | bytes 786440 | tf_op jit(solution)/shard_map/ppermute | solution.py:211
  14.8 10.1 %collective-permute-start.1 = (f32[4,128]{1,0:T(4,128)S(1)}, f32[4,128]{1,0:T(4,128)S(1)}, u32[]{:S(2)}, u32[]{:S(2)}) collective-permute-start(f32[4,128]{1,0:T(4,128)S(1)} %get-tuple-element.12.table), channel_id=1, source_target_pairs={{0,2},{2,4},{4,6},{6,0},{1,3},{3,5},{5,7},{7,1},{8,10},{10,12},{12... | collective-permute-start | bytes 6152 | tf_op jit(solution)/shard_map/ppermute | solution.py:217
  16.1 8.8 %collective-permute-start.2 = (f32[4,128]{1,0:T(4,128)S(1)}, f32[4,128]{1,0:T(4,128)S(1)}, u32[]{:S(2)}, u32[]{:S(2)}) collective-permute-start(f32[4,128]{1,0:T(4,128)S(1)} %get-tuple-element.12.table), channel_id=1, source_target_pairs={{0,4},{2,6},{4,0},{6,2},{1,5},{3,7},{5,1},{7,3},{8,12},{10,14},{12... | collective-permute-start | bytes 6152 | tf_op jit(solution)/shard_map/ppermute | solution.py:217
  19.1 5.8 %collective-permute-start.3 = (f32[4,128]{1,0:T(4,128)S(1)}, f32[4,128]{1,0:T(4,128)S(1)}, u32[]{:S(2)}, u32[]{:S(2)}) collective-permute-start(f32[4,128]{1,0:T(4,128)S(1)} %get-tuple-element.12.table), channel_id=1, source_target_pairs={{0,6},{2,0},{4,2},{6,4},{1,7},{3,1},{5,3},{7,5},{8,14},{10,8},{12,... | collective-permute-start | bytes 6152 | tf_op jit(solution)/shard_map/ppermute | solution.py:217
  26.3 8.3 %collective-permute-start.5 = (bf16[64,2048]{1,0:T(8,128)(2,1)S(1)}, bf16[64,2048]{1,0:T(8,128)(2,1)S(1)}, u32[]{:S(2)}, u32[]{:S(2)}) collective-permute-start(bf16[64,2048]{1,0:T(8,128)(2,1)S(1)} %choose.5), channel_id=1, source_target_pairs={{0,2},{2,0},{4,6},{6,4},{1,3},{3,1},{5,7},{7,5},{8,10},{10,8},{12,... | collective-permute-start | bytes 786440 | tf_op jit(solution)/shard_map/ppermute | solution.py:211
  27.4 10.5 %collective-permute-start.6 = (bf16[64,2048]{1,0:T(8,128)(2,1)S(1)}, bf16[64,2048]{1,0:T(8,128)(2,1)S(1)}, u32[]{:S(2)}, u32[]{:S(2)}) collective-permute-start(bf16[64,2048]{1,0:T(8,128)(2,1)S(1)} %get-tuple-element.11.second.at_end.at_mid), channel_id=1, source_target_pairs={{2,4},{4,2},{3,5},{5,3},{10,12},{12,10},{11,13},{13,11},{18,20},{2... | collective-permute-start | bytes 786440 | tf_op jit(solution)/shard_map/ppermute | solution.py:214
  29.9 10.8 %collective-permute-start.12 = (bf16[64,2048]{1,0:T(8,128)(2,1)S(1)}, bf16[64,2048]{1,0:T(8,128)(2,1)S(1)}, u32[]{:S(2)}, u32[]{:S(2)}) collective-permute-start(bf16[64,2048]{1,0:T(8,128)(2,1)S(1)} %collective-permute-done.11.at_end.at_mid), channel_id=1, source_target_pairs={{2,4},{4,2},{3,5},{5,3},{10,12},{12,10},{11,13},{13,11},{18,20},{2... | collective-permute-start | bytes 786440 | tf_op jit(solution)/shard_map/ppermute | solution.py:214
  38.0 7.7 %collective-permute-start.7 = (bf16[64,2048]{1,0:T(8,128)(2,1)S(1)}, bf16[64,2048]{1,0:T(8,128)(2,1)S(1)}, u32[]{:S(2)}, u32[]{:S(2)}) collective-permute-start(bf16[64,2048]{1,0:T(8,128)(2,1)S(1)} %choose.6), channel_id=1, source_target_pairs={{0,2},{2,0},{4,6},{6,4},{1,3},{3,1},{5,7},{7,5},{8,10},{10,8},{12,... | collective-permute-start | bytes 786440 | tf_op jit(solution)/shard_map/ppermute | solution.py:211
  40.8 8.1 %collective-permute-start.13 = (bf16[64,2048]{1,0:T(8,128)(2,1)S(1)}, bf16[64,2048]{1,0:T(8,128)(2,1)S(1)}, u32[]{:S(2)}, u32[]{:S(2)}) collective-permute-start(bf16[64,2048]{1,0:T(8,128)(2,1)S(1)} %choose.8), channel_id=1, source_target_pairs={{0,2},{2,0},{4,6},{6,4},{1,3},{3,1},{5,7},{7,5},{8,10},{10,8},{12,... | collective-permute-start | bytes 786440 | tf_op jit(solution)/shard_map/ppermute | solution.py:211
  45.8 8.3 %collective-permute-start.8 = (bf16[64,2048]{1,0:T(8,128)(2,1)S(1)}, bf16[64,2048]{1,0:T(8,128)(2,1)S(1)}, u32[]{:S(2)}, u32[]{:S(2)}) collective-permute-start(bf16[64,2048]{1,0:T(8,128)(2,1)S(1)} %add.4), channel_id=1, source_target_pairs={{2,4},{4,2},{3,5},{5,3},{10,12},{12,10},{11,13},{13,11},{18,20},{2... | collective-permute-start | bytes 786440 | tf_op jit(solution)/shard_map/ppermute | solution.py:214
  50.2 6.7 %collective-permute-start.15 = (bf16[64,2048]{1,0:T(8,128)(2,1)S(1)}, bf16[64,2048]{1,0:T(8,128)(2,1)S(1)}, u32[]{:S(2)}, u32[]{:S(2)}) collective-permute-start(bf16[64,2048]{1,0:T(8,128)(2,1)S(1)} %choose.9), channel_id=1, source_target_pairs={{0,2},{2,0},{4,6},{6,4},{1,3},{3,1},{5,7},{7,5},{8,10},{10,8},{12,... | collective-permute-start | bytes 786440 | tf_op jit(solution)/shard_map/ppermute | solution.py:211
  54.1 10.1 %collective-permute-start.9 = (bf16[64,2048]{1,0:T(8,128)(2,1)S(1)}, bf16[64,2048]{1,0:T(8,128)(2,1)S(1)}, u32[]{:S(2)}, u32[]{:S(2)}) collective-permute-start(bf16[64,2048]{1,0:T(8,128)(2,1)S(1)} %choose_sum.2), channel_id=1, source_target_pairs={{0,2},{2,0},{4,6},{6,4},{1,3},{3,1},{5,7},{7,5},{8,10},{10,8},{12,... | collective-permute-start | bytes 786440 | tf_op jit(solution)/shard_map/ppermute | solution.py:211
  57.0 10.8 %collective-permute-start.16 = (bf16[64,2048]{1,0:T(8,128)(2,1)S(1)}, bf16[64,2048]{1,0:T(8,128)(2,1)S(1)}, u32[]{:S(2)}, u32[]{:S(2)}) collective-permute-start(bf16[64,2048]{1,0:T(8,128)(2,1)S(1)} %add.6), channel_id=1, source_target_pairs={{2,4},{4,2},{3,5},{5,3},{10,12},{12,10},{11,13},{13,11},{18,20},{2... | collective-permute-start | bytes 786440 | tf_op jit(solution)/shard_map/ppermute | solution.py:214
  60.3 10.6 %collective-permute-start.14 = (bf16[64,2048]{1,0:T(8,128)(2,1)S(1)}, bf16[64,2048]{1,0:T(8,128)(2,1)S(1)}, u32[]{:S(2)}, u32[]{:S(2)}) collective-permute-start(bf16[64,2048]{1,0:T(8,128)(2,1)S(1)} %add.5), channel_id=1, source_target_pairs={{2,4},{4,2},{3,5},{5,3},{10,12},{12,10},{11,13},{13,11},{18,20},{2... | collective-permute-start | bytes 786440 | tf_op jit(solution)/shard_map/ppermute | solution.py:214
  64.3 9.4 %collective-permute-start.18 = (bf16[64,2048]{1,0:T(8,128)(2,1)S(1)}, bf16[64,2048]{1,0:T(8,128)(2,1)S(1)}, u32[]{:S(2)}, u32[]{:S(2)}) collective-permute-start(bf16[64,2048]{1,0:T(8,128)(2,1)S(1)} %add.7), channel_id=1, source_target_pairs={{2,4},{4,2},{3,5},{5,3},{10,12},{12,10},{11,13},{13,11},{18,20},{2... | collective-permute-start | bytes 786440 | tf_op jit(solution)/shard_map/ppermute | solution.py:214
  67.9 6.4 %collective-permute-start.17 = (bf16[64,2048]{1,0:T(8,128)(2,1)S(1)}, bf16[64,2048]{1,0:T(8,128)(2,1)S(1)}, u32[]{:S(2)}, u32[]{:S(2)}) collective-permute-start(bf16[64,2048]{1,0:T(8,128)(2,1)S(1)} %choose_sum.3), channel_id=1, source_target_pairs={{0,2},{2,0},{4,6},{6,4},{1,3},{3,1},{5,7},{7,5},{8,10},{10,8},{12,... | collective-permute-start | bytes 786440 | tf_op jit(solution)/shard_map/ppermute | solution.py:211
  71.0 7.7 %collective-permute-start.19 = (bf16[64,2048]{1,0:T(8,128)(2,1)S(1)}, bf16[64,2048]{1,0:T(8,128)(2,1)S(1)}, u32[]{:S(2)}, u32[]{:S(2)}) collective-permute-start(bf16[64,2048]{1,0:T(8,128)(2,1)S(1)} %finish_first.1.first), channel_id=1, source_target_pairs={{0,8},{8,16},{16,24},{1,9},{9,17},{17,25},{2,10},{10,18},{18,26},{... | collective-permute-start | bytes 786440 | tf_op jit(solution)/shard_map/ppermute | solution.py:12
  74.4 7.7 %collective-permute-start.20 = (bf16[64,2048]{1,0:T(8,128)(2,1)S(1)}, bf16[64,2048]{1,0:T(8,128)(2,1)S(1)}, u32[]{:S(2)}, u32[]{:S(2)}) collective-permute-start(bf16[64,2048]{1,0:T(8,128)(2,1)S(1)} %finish_second.1.second), channel_id=1, source_target_pairs={{0,8},{8,16},{16,24},{1,9},{9,17},{17,25},{2,10},{10,18},{18,26},{... | collective-permute-start | bytes 786440 | tf_op jit(solution)/shard_map/ppermute | solution.py:12

commit v3 on v2

--- a/solution.py
+++ b/solution.py
@@ -54,8 +54,7 @@
     return (layer_out[None], handed[None])
 
 
-OUTER = [(0, 1), (1, 0), (2, 3), (3, 2)]
-INNER = [(1, 2), (2, 1)]
+TAG = 128
 IN_VMEM = pl.BlockSpec(memory_space=pltpu.VMEM)
 ANYWHERE = pl.BlockSpec(memory_space=pl.ANY)
 
@@ -96,29 +95,45 @@
     )(*operands)
 
 
-def prepare(tokens, routes, weights, first, second, table, sems):
-    half = first.shape[0]
+def prepare(tokens, routes, weights, first, second, routes_here, weights_here, sems):
+    half, width = first.shape[0], tokens.shape[1]
     copies = [
-        pltpu.make_async_copy(tokens.at[pl.ds(i * half, half)], part, sems.at[i])
-        for i, part in enumerate((first, second))
+        pltpu.make_async_copy(source, target, sems.at[i])
+        for i, (source, target) in enumerate(
+            (
+                (routes, routes_here),
+                (weights, weights_here),
+                (tokens.at[pl.ds(0, half)], first.at[:, pl.ds(0, width)]),
+                (tokens.at[pl.ds(half, half)], second),
+            )
+        )
     ]
     for copy in copies:
         copy.start()
-    names = lax.broadcasted_iota(jnp.int32, table.shape, 0)
-    total = jnp.zeros(table.shape, jnp.float32)
+    for copy in copies[:2]:
+        copy.wait()
+    names = lax.broadcasted_iota(jnp.int32, (8, 2 * half), 0)
+    rest = jnp.zeros((8, 2 * half), jnp.float32)
     for k in range(routes.shape[0]):
-        total += jnp.where(routes[k : k + 1, :] == names, weights[k : k + 1, :], 0.0)
-    table[...] = total
-    for copy in copies:
+        rest += jnp.where(routes_here[k : k + 1, :] == names, weights_here[k : k + 1, :], 0.0)
+    pieces = []
+    for _ in range(3):
+        pieces.append(narrow(rest).astype(jnp.float32))
+        rest = rest - pieces[-1]
+    pieces += [pltpu.roll(piece, half, 1) for piece in pieces]
+    pieces.append(jnp.zeros((TAG - 48, 2 * half), jnp.float32))
+    tags = narrow(jnp.concatenate(pieces, axis=0).T[:half])
+    for copy in copies[2:]:
         copy.wait()
-
-
-def column(table, me, start, count):
-    names = lax.broadcasted_iota(jnp.int32, table.shape, 0)
-    row = jnp.sum(jnp.where(names == me, table, 0.0), axis=0, keepdims=True)[:, start : start + count]
-    across = lax.broadcasted_iota(jnp.int32, (count, count), 1)
-    down = lax.broadcasted_iota(jnp.int32, (count, count), 0)
-    return jnp.sum(jnp.where(across == down, row, 0.0), axis=1, keepdims=True)
+    first[:, width:] = tags
+
+
+def weight_of(tags, late):
+    me, _ = position()
+    lane = lax.broadcasted_iota(jnp.int32, tags.shape, 1)
+    start = 24 if late else 0
+    mine = (lane >= start) & (lane < start + 24) & (lane % 8 == me)
+    return jnp.sum(jnp.where(mine, tags.astype(jnp.float32), 0.0), axis=1, keepdims=True)
 
 
 def expert_of(rows, gate_w, up_w, down_w):
@@ -129,35 +144,35 @@
     return narrow(out).astype(jnp.float32)
 
 
-def own_pass(first, second, table, *refs):
-    from_hbm, to_vmem, totals, sems = refs[0:3], refs[3:6], refs[6:8], refs[8]
+def own_pass(first, second, gate_hbm, up_hbm, down_hbm, gate_w, up_w, down_w, total, sems):
     copies = [
-        pltpu.make_async_copy(a, b, sems.at[i]) for i, (a, b) in enumerate(zip(from_hbm, to_vmem))
+        pltpu.make_async_copy(source, target, sems.at[i])
+        for i, (source, target) in enumerate(
+            ((gate_hbm, gate_w), (up_hbm, up_w), (down_hbm, down_w))
+        )
     ]
     for copy in copies:
         copy.start()
-    me, _ = position()
-    for copy in copies:
-        copy.wait()
-    half = first.shape[0]
-    for i, part in enumerate((first, second)):
-        out = expert_of(part[...], *to_vmem)
-        totals[i][...] = wide(part) + out * column(table[...], me, i * half, half)
-
-
-def pass_of(partner, late):
-    def body(at_end, at_mid, table_a, table_b, table_c, gate_w, up_w, down_w, result):
-        me, end = position()
-        half = result.shape[0]
-        if partner == 0:
-            came = jnp.where(me % 2 == 0, 3, 1)
-        elif partner == 1:
-            came = jnp.where(me == 1, 3, jnp.where(me == 2, 1, 2))
-        else:
-            came = jnp.where(me == 0, 1, jnp.where(me == 3, 3, 2))
-        table = jnp.where(came == 1, table_a[...], jnp.where(came == 2, table_b[...], table_c[...]))
-        rows = jnp.where(end, at_end[...], at_mid[...])
-        weight = column(table, me, half if late else 0, half)
+    half, width = first.shape[0], total.shape[1]
+    rows = jnp.concatenate([first[:, :width], second[...]], axis=0)
+    tags = first[:, width:]
+    weight = jnp.concatenate([weight_of(tags, False), weight_of(tags, True)], axis=0)
+    copies[0].wait()
+    gate = jnp.dot(rows, gate_w[...], preferred_element_type=jnp.float32)
+    copies[1].wait()
+    up = jnp.dot(rows, up_w[...], preferred_element_type=jnp.float32)
+    hidden = narrow(gate / (1.0 + jnp.exp(-gate)) * up)
+    copies[2].wait()
+    out = jnp.dot(hidden, down_w[...], preferred_element_type=jnp.float32)
+    total[...] = rows.astype(jnp.float32) + narrow(out).astype(jnp.float32) * weight
+
+
+def pass_of(late):
+    def body(at_end, at_mid, tag_end, tag_mid, gate_w, up_w, down_w, result):
+        _, end = position()
+        width = result.shape[1]
+        rows = jnp.where(end, at_end[:, :width], at_mid[:, :width])
+        weight = weight_of(jnp.where(end, tag_end[:, width:], tag_mid[:, width:]), late)
         result[...] = narrow(expert_of(rows, gate_w, up_w, down_w) * weight)
 
     return body
@@ -165,7 +180,12 @@
 
 def choose(at_end, at_mid, result):
     _, end = position()
-    result[...] = jnp.where(end, at_end[...], at_mid[...])
+    width = min(at_end.shape[1], at_mid.shape[1], result.shape[1])
+    result[:, :width] = jnp.where(end, at_end[:, :width], at_mid[:, :width])
+    if result.shape[1] > width:
+        wider, here = (at_mid, ~end) if at_mid.shape[1] > width else (at_end, end)
+        rest = wider[:, width:]
+        result[:, width:] = jnp.where(here, rest, jnp.zeros_like(rest))
 
 
 def choose_sum(at_end, mid_a, mid_b, result):
@@ -179,12 +199,15 @@
 
 def finish_first(total, far, near, inner, result):
     _, end = position()
-    result[...] = narrow(total[...] + jnp.where(end, wide(far), wide(near) + wide(inner)))
+    half, width = result.shape
+    at_mid = near[:, :width].astype(jnp.float32) + wide(inner)
+    result[...] = narrow(total[:half] + jnp.where(end, wide(far), at_mid))
 
 
 def finish_second(total, outer, inner, result):
     _, end = position()
-    result[...] = narrow(total[...] + wide(outer) + jnp.where(end, 0.0, wide(inner)))
+    half = result.shape[0]
+    result[...] = narrow(total[half:] + wide(outer) + jnp.where(end, 0.0, wide(inner)))
 
 
 def join(first, second, whole, sems):
@@ -205,73 +228,83 @@
     half = count // 2
     block = (half, width)
     weights = (expert_gate[0, 0], expert_up[0, 0], expert_down[0, 0])
-    two_sems = [pltpu.SemaphoreType.DMA((2,))]
+    axes = ("section", "expert")
+    sections = range(lax.axis_size("section"))
+    outer_pairs = [(s * 4 + e, s * 4 + (e ^ 1)) for s in sections for e in range(4)]
+    inner_pairs = [
+        (s * 4 + e, s * 4 + 3 - e if e in (1, 2) else (s ^ 1) * 4 + e)
+        for s in sections
+        for e in range(4)
+    ]
 
     def outer(value):
-        return lax.ppermute(value, "expert", OUTER)
+        return lax.ppermute(value, axes, outer_pairs)
 
     def inner(value):
-        return lax.ppermute(value, "expert", INNER)
-
-    def turned(value, by):
-        return lax.ppermute(value, "expert", [(s, (s + by) % 4) for s in range(4)])
-
-    first, second, table = run(
+        return lax.ppermute(value, axes, inner_pairs)
+
+    tagged = (half, width + TAG)
+    first, second = run(
         prepare,
         "prepare",
-        [held(block), held(block), held((4, count), jnp.float32)],
+        [held(tagged), held(block)],
         rows,
         routes[0].T,
         route_weights[0].T,
-        scratch=two_sems,
-        specs=[ANYWHERE, IN_VMEM, IN_VMEM],
+        scratch=[
+            held((routes.shape[2], count), jnp.int32),
+            held((routes.shape[2], count), jnp.float32),
+            pltpu.SemaphoreType.DMA((4,)),
+        ],
+        specs=[ANYWHERE] * 3,
     )
     o0, i0 = outer(first), inner(first)
-    tables = [turned(table, by) for by in (1, 2, 3)]
-    *weights, total_first, total_second = run(
+    *weights, total = run(
         own_pass,
         "own_pass",
-        [held(w.shape) for w in weights] + [held(block, jnp.float32)] * 2,
+        [held(w.shape) for w in weights] + [held((count, width), jnp.float32)],
         first,
         second,
-        table,
         *weights,
         scratch=[pltpu.SemaphoreType.DMA((3,))],
-        specs=[IN_VMEM] * 3 + [ANYWHERE] * 3,
+        specs=[IN_VMEM] * 2 + [ANYWHERE] * 3,
         work=(6 * count * weights[0].size, 6 * weights[0].size),
     )
-
-    def expert(partner, late, at_end, at_mid):
+    o0, i0, total, *weights = lax.optimization_barrier((o0, i0, total, *weights))
+
+    def expert(late, rows, tags):
         return run(
-            pass_of(partner, late),
+            pass_of(late),
             "expert_pass",
             held(block),
-            at_end,
-            at_mid,
-            *tables,
+            *rows,
+            *tags,
             *weights,
             work=(6 * half * weights[0].size, 6 * weights[0].size),
         )
 
-    def mixed(body, *operands):
-        return run(body, body.__name__, held(block), *operands)
-
-    o1, i1 = outer(mixed(choose, second, i0)), inner(o0)
-    p1 = expert(0, False, o0, o0)
-    o2, i2 = outer(mixed(choose, p1, i1)), inner(o1)
-    p2 = expert(1, False, o1, i0)
+    def mixed(body, *operands, shape=block):
+        return run(body, body.__name__, held(shape), *operands)
+
+    near = (o0, o0)
+    o1, i1 = outer(mixed(choose, second, i0, shape=tagged)), inner(o0)
+    p1 = expert(False, near, near)
+    o2, i2 = outer(mixed(choose, p1, i1, shape=tagged)), inner(o1)
+    two = (o1, i0)
+    p2 = expert(False, two, two)
     o3, i3 = outer(mixed(choose, p2, i2)), inner(second)
-    p3 = expert(2, False, o2, i1)
+    three = (o2, i1)
+    p3 = expert(False, three, three)
     o4, i4 = outer(mixed(choose, p3, i3)), inner(mixed(add, o3, p2))
-    p4 = expert(2, True, o3, i2)
+    p4 = expert(True, (o3, i2), three)
     o5, i5 = outer(mixed(choose, p4, second)), inner(mixed(add, o4, p3))
-    p5 = expert(1, True, o4, i3)
+    p5 = expert(True, (o4, i3), two)
     o6, i6 = outer(mixed(choose_sum, p5, i5, p1)), inner(mixed(add, o5, p4))
-    p6 = expert(0, True, o5, o1)
+    p6 = expert(True, (o5, o1), near)
     o7, i7 = outer(mixed(choose_sum, p6, i6, p6)), inner(mixed(add, o6, p5))
-    out_first = mixed(finish_first, total_first, o6, o2, i4)
+    out_first = run(finish_first, "finish_first", held(block), total, o6, o2, i4)
     next_first = passed_along(out_first, "section", 1)
-    out_second = mixed(finish_second, total_second, o7, i7)
+    out_second = run(finish_second, "finish_second", held(block), total, o7, i7)
     next_second = passed_along(out_second, "section", 1)
 
     def joined(a, b):
@@ -281,7 +314,7 @@
             jax.ShapeDtypeStruct((count, width), jnp.bfloat16),
             a,
             b,
-            scratch=two_sems,
+            scratch=[pltpu.SemaphoreType.DMA((2,))],
             out_specs=ANYWHERE,
         )
 
@@ -301,7 +334,8 @@
 
     def per_device(*args):
         tokens, expert_gate = args[0], args[3]
-        line = mesh.shape["expert"] == 4 and expert_gate.shape[1] == 1 and tokens.shape[1] % 32 == 0
+        line = mesh.shape["expert"] == 4 and mesh.shape["section"] % 2 == 0
+        line = line and expert_gate.shape[1] == 1 and tokens.shape[1] == 128
         return (on_line if line else by_slots)(*args)
 
     return jax.shard_map(

time: 83.3 us -> 73.4 us (0.88)
  starting transfers between devices: 36.7 us -> 17.2 us
  waiting for transfers between devices: 27.3 us -> 40.7 us
  Pallas kernels: 16.6 us -> 14.5 us
  local copies, waits for them, and re-layouts: 1.35 us -> 0 us
    ppermute x19 -> x16, starting transfers between devices: 32.9 us -> 13.4 us  [the longest x8 11.8 us: inner(): return lax.ppermute(value, axes, inner_pairs)]
    ppermute x19 -> x16, waiting for transfers between devices: 22.3 us -> 35.7 us  [the longest x8 19.5 us: outer(): return lax.ppermute(value, axes, outer_pairs)]
    pallas_call x23, Pallas kernels: 16.6 us -> 14.5 us  [run(): pl.pallas_call(body, out_shape=out_shape, in_specs=specs, out_specs=out_s...]
    unnamed x4 -> x0, local copies, waits for them, and re-layouts: 1.35 us -> none
  transfers between devices with their start and end apart: 21 -> 18, of which waited for: 12 -> 15; matrix products, arithmetic and copies ran while one was open for 0% -> 0% of each run, Pallas kernels for 18% -> 17%
where the time goes in v3:
time: 73.4 us; the launch traced here: 73.3 us
  waiting for transfers between devices  40.7 us (55%)
  starting transfers between devices  17.2 us (23%)
  Pallas kernels  14.5 us (20%)
  between operations  0.84 us (1%)
    ppermute x8, waiting for transfers between devices, outer(): return lax.ppermute(value, axes, outer_pairs)  19.5 us
    ppermute x8, waiting for transfers between devices, inner(): return lax.ppermute(value, axes, inner_pairs)  16.2 us
    pallas_call x23, Pallas kernels, run(): pl.pallas_call(body, out_shape=out_shape, in_specs=specs, out_specs=out_s...  14.5 us
    ppermute x8, starting transfers between devices, inner(): return lax.ppermute(value, axes, inner_pairs)  11.8 us
    ppermute x2, waiting for transfers between devices, passed_along(): lax.ppermute(value, axis, [(source, source + steps) for source in range(l...  4.94 us
    ppermute x2, starting transfers between devices, passed_along(): lax.ppermute(value, axis, [(source, source + steps) for source in range(l...  3.84 us
    ppermute x8, starting transfers between devices, outer(): return lax.ppermute(value, axes, outer_pairs)  1.63 us
  transfers between devices with their start and end apart: 18, of which 15 were waited for; matrix products, arithmetic and copies ran while one was open for 0% of the time, Pallas kernels for 17%

profile of v3, /device:TPU:12, one launch (start us, length us, event | category | flops | bytes accessed | tf_op | source)
XLA Modules:
  0.0 73.3 jit_solution(11356547359729667124)
XLA Ops:
  0.6 1.1 %prepare.1 = (bf16[64,2176]{1,0:T(8,128)(2,1)S(1)}, bf16[64,2048]{1,0:T(8,128)(2,1)S(1)}) custom-call(bf16[128,2048]{1,0:T(8,128)(2,1)} %bitcast.15, s32[2,128]{1,0:T(2,128)} %bitcast.18, f32[2,128]{1,0:T(2,128)} %bitcast.19), custom_call_target="tpu_custom_call" | custom-call | tf_op jit(solution)/shard_map/prepare/pallas_call | solution.py:86
  2.3 2.7 %collective-permute-start.1 = (bf16[64,2176]{1,0:T(8,128)(2,1)S(1)}, bf16[64,2176]{1,0:T(8,128)(2,1)S(1)}, u32[]{:S(2)}, u32[]{:S(2)}) collective-permute-start(bf16[64,2176]{1,0:T(8,128)(2,1)S(1)} %get-tuple-element.14.first), channel_id=1, source_target_pairs={{0,8},{2,4},{4,2},{6,14},{8,0},{10,12},{12,10},{14,6},{16,24},{18,... | collective-permute-start | bytes 835592 | tf_op jit(solution)/shard_map/ppermute | solution.py:244
  5.0 3.4 %own_pass.1 = (bf16[2048,512]{1,0:T(8,128)(2,1)S(1)}, bf16[2048,512]{1,0:T(8,128)(2,1)S(1)}, bf16[512,2048]{1,0:T(8,128)(2,1)S(1)}, f32[128,2048]{1,0:T(8,128)S(1)}) custom-call(bf16[64,2176]{1,0:T(8,128)(2,1)S(1)} %get-tuple-element.14.first, bf16[64,2048]{1,0:T(8,128)(2,1)S(1)} %get-tuple-element.15.second.at_end.at_mid, bf16[2048,512]{1,0:T(8,128)(2,1)} %bitcast.12, ...), custom_call_target="tpu_custom_call" | custom-call | flops 805306368 | bytes 6291456 | tf_op jit(solution)/shard_map/own_pass/pallas_call | solution.py:86
  8.3 1.9 %collective-permute-done.at_end.at_mid.tag_end.tag_mid = bf16[64,2176]{1,0:T(8,128)(2,1)S(1)} collective-permute-done((bf16[64,2176]{1,0:T(8,128)(2,1)S(1)}, bf16[64,2176]{1,0:T(8,128)(2,1)S(1)}, u32[]{:S(2)}, u32[]{:S(2)}) %collective-permute-start) | collective-permute-done | bytes 278560 | tf_op jit(solution)/shard_map/ppermute | solution.py:241
  10.2 1.1 %collective-permute-done.1.at_mid.tag_mid = bf16[64,2176]{1,0:T(8,128)(2,1)S(1)} collective-permute-done((bf16[64,2176]{1,0:T(8,128)(2,1)S(1)}, bf16[64,2176]{1,0:T(8,128)(2,1)S(1)}, u32[]{:S(2)}, u32[]{:S(2)}) %collective-permute-start.1) | collective-permute-done | bytes 278560 | tf_op jit(solution)/shard_map/ppermute | solution.py:244
  11.4 2.0 %collective-permute-start.2 = (bf16[64,2176]{1,0:T(8,128)(2,1)S(1)}, bf16[64,2176]{1,0:T(8,128)(2,1)S(1)}, u32[]{:S(2)}, u32[]{:S(2)}) collective-permute-start(bf16[64,2176]{1,0:T(8,128)(2,1)S(1)} %collective-permute-done.at_end.at_mid.tag_end.tag_mid), channel_id=1, source_target_pairs={{0,8},{2,4},{4,2},{6,14},{8,0},{10,12},{12,10},{14,6},{16,24},{18,... | collective-permute-start | bytes 835592 | tf_op jit(solution)/shard_map/ppermute | solution.py:244
  13.5 1.3 %expert_pass.6.at_end.mid_b = bf16[64,2048]{1,0:T(8,128)(2,1)S(1)} custom-call(bf16[64,2176]{1,0:T(8,128)(2,1)S(1)} %collective-permute-done.at_end.at_mid.tag_end.tag_mid, bf16[64,2176]{1,0:T(8,128)(2,1)S(1)} %collective-permute-done.at_end.at_mid.tag_end.tag_mid, bf16[64,2176]{1,0:T(8,128)(2,1)S(1)} %collective-permute-done.at_end.at_mid.tag_end.tag_mid, ...), custom_call_target="tpu_custom_call" | custom-call | flops 402653184 | bytes 6291456 | tf_op jit(solution)/shard_map/expert_pass/pallas_call | solution.py:86
  14.7 4.2 %collective-permute-done.6.tag_end.at_end.at_mid = bf16[64,2176]{1,0:T(8,128)(2,1)S(1)} collective-permute-done((bf16[64,2176]{1,0:T(8,128)(2,1)S(1)}, bf16[64,2176]{1,0:T(8,128)(2,1)S(1)}, u32[]{:S(2)}, u32[]{:S(2)}) %collective-permute-start.6) | collective-permute-done | bytes 278560 | tf_op jit(solution)/shard_map/ppermute | solution.py:241
  19.0 1.4 %collective-permute-start.9 = (bf16[64,2176]{1,0:T(8,128)(2,1)S(1)}, bf16[64,2176]{1,0:T(8,128)(2,1)S(1)}, u32[]{:S(2)}, u32[]{:S(2)}) collective-permute-start(bf16[64,2176]{1,0:T(8,128)(2,1)S(1)} %collective-permute-done.6.tag_end.at_end.at_mid), channel_id=1, source_target_pairs={{0,8},{2,4},{4,2},{6,14},{8,0},{10,12},{12,10},{14,6},{16,24},{18,... | collective-permute-start | bytes 835592 | tf_op jit(solution)/shard_map/ppermute | solution.py:244
  21.2 1.3 %expert_pass.9.at_end.b = bf16[64,2048]{1,0:T(8,128)(2,1)S(1)} custom-call(bf16[64,2176]{1,0:T(8,128)(2,1)S(1)} %collective-permute-done.6.tag_end.at_end.at_mid, bf16[64,2176]{1,0:T(8,128)(2,1)S(1)} %collective-permute-done.1.at_mid.tag_mid, bf16[64,2176]{1,0:T(8,128)(2,1)S(1)} %collective-permute-done.6.tag_end.at_end.at_mid, ...), custom_call_target="tpu_custom_call" | custom-call | flops 402653184 | bytes 6291456 | tf_op jit(solution)/shard_map/expert_pass/pallas_call | solution.py:86
  22.5 5.9 %collective-permute-done.9.at_mid = bf16[64,2176]{1,0:T(8,128)(2,1)S(1)} collective-permute-done((bf16[64,2176]{1,0:T(8,128)(2,1)S(1)}, bf16[64,2176]{1,0:T(8,128)(2,1)S(1)}, u32[]{:S(2)}, u32[]{:S(2)}) %collective-permute-start.9) | collective-permute-done | bytes 278560 | tf_op jit(solution)/shard_map/ppermute | solution.py:244
  28.8 1.3 %expert_pass.7.at_end.b = bf16[64,2048]{1,0:T(8,128)(2,1)S(1)} custom-call(bf16[64,2176]{1,0:T(8,128)(2,1)S(1)} %collective-permute-done.3.at_end.tag_end.near, bf16[64,2176]{1,0:T(8,128)(2,1)S(1)} %collective-permute-done.2.at_mid.tag_mid, bf16[64,2176]{1,0:T(8,128)(2,1)S(1)} %collective-permute-done.3.at_end.tag_end.near, ...), custom_call_target="tpu_custom_call" | custom-call | flops 402653184 | bytes 6291456 | tf_op jit(solution)/shard_map/expert_pass/pallas_call | solution.py:86
  30.0 1.1 %collective-permute-done.4.at_mid = bf16[64,2048]{1,0:T(8,128)(2,1)S(1)} collective-permute-done((bf16[64,2048]{1,0:T(8,128)(2,1)S(1)}, bf16[64,2048]{1,0:T(8,128)(2,1)S(1)}, u32[]{:S(2)}, u32[]{:S(2)}) %collective-permute-start.4) | collective-permute-done | bytes 262176 | tf_op jit(solution)/shard_map/ppermute | solution.py:244
  31.9 5.8 %collective-permute-done.10.a.at_end = bf16[64,2048]{1,0:T(8,128)(2,1)S(1)} collective-permute-done((bf16[64,2048]{1,0:T(8,128)(2,1)S(1)}, bf16[64,2048]{1,0:T(8,128)(2,1)S(1)}, u32[]{:S(2)}, u32[]{:S(2)}) %collective-permute-start.10) | collective-permute-done | bytes 262176 | tf_op jit(solution)/shard_map/ppermute | solution.py:241
  37.7 1.3 %expert_pass.10.at_end.b = bf16[64,2048]{1,0:T(8,128)(2,1)S(1)} custom-call(bf16[64,2048]{1,0:T(8,128)(2,1)S(1)} %collective-permute-done.10.a.at_end, bf16[64,2176]{1,0:T(8,128)(2,1)S(1)} %collective-permute-done.9.at_mid, bf16[64,2176]{1,0:T(8,128)(2,1)S(1)} %collective-permute-done.3.at_end.tag_end.near, ...), custom_call_target="tpu_custom_call" | custom-call | flops 402653184 | bytes 6291456 | tf_op jit(solution)/shard_map/expert_pass/pallas_call | solution.py:86
  39.1 3.2 %collective-permute-done.5.at_end.a = bf16[64,2048]{1,0:T(8,128)(2,1)S(1)} collective-permute-done((bf16[64,2048]{1,0:T(8,128)(2,1)S(1)}, bf16[64,2048]{1,0:T(8,128)(2,1)S(1)}, u32[]{:S(2)}, u32[]{:S(2)}) %collective-permute-start.5) | collective-permute-done | bytes 262176 | tf_op jit(solution)/shard_map/ppermute | solution.py:241
  42.3 1.4 %collective-permute-start.7 = (bf16[64,2048]{1,0:T(8,128)(2,1)S(1)}, bf16[64,2048]{1,0:T(8,128)(2,1)S(1)}, u32[]{:S(2)}, u32[]{:S(2)}) collective-permute-start(bf16[64,2048]{1,0:T(8,128)(2,1)S(1)} %add.4), channel_id=1, source_target_pairs={{0,8},{2,4},{4,2},{6,14},{8,0},{10,12},{12,10},{14,6},{16,24},{18,... | collective-permute-start | bytes 786440 | tf_op jit(solution)/shard_map/ppermute | solution.py:244
  43.7 1.3 %expert_pass.8.at_end.b = bf16[64,2048]{1,0:T(8,128)(2,1)S(1)} custom-call(bf16[64,2048]{1,0:T(8,128)(2,1)S(1)} %collective-permute-done.5.at_end.a, bf16[64,2048]{1,0:T(8,128)(2,1)S(1)} %collective-permute-done.4.at_mid, bf16[64,2176]{1,0:T(8,128)(2,1)S(1)} %collective-permute-done.6.tag_end.at_end.at_mid, ...), custom_call_target="tpu_custom_call" | custom-call | flops 402653184 | bytes 6291456 | tf_op jit(solution)/shard_map/expert_pass/pallas_call | solution.py:86
  45.5 1.4 %collective-permute-start.13 = (bf16[64,2048]{1,0:T(8,128)(2,1)S(1)}, bf16[64,2048]{1,0:T(8,128)(2,1)S(1)}, u32[]{:S(2)}, u32[]{:S(2)}) collective-permute-start(bf16[64,2048]{1,0:T(8,128)(2,1)S(1)} %add.6), channel_id=1, source_target_pairs={{0,8},{2,4},{4,2},{6,14},{8,0},{10,12},{12,10},{14,6},{16,24},{18,... | collective-permute-start | bytes 786440 | tf_op jit(solution)/shard_map/ppermute | solution.py:244
  46.9 3.4 %collective-permute-done.7.mid_a = bf16[64,2048]{1,0:T(8,128)(2,1)S(1)} collective-permute-done((bf16[64,2048]{1,0:T(8,128)(2,1)S(1)}, bf16[64,2048]{1,0:T(8,128)(2,1)S(1)}, u32[]{:S(2)}, u32[]{:S(2)}) %collective-permute-start.7) | collective-permute-done | bytes 262176 | tf_op jit(solution)/shard_map/ppermute | solution.py:244
  50.5 1.1 %collective-permute-start.11 = (bf16[64,2048]{1,0:T(8,128)(2,1)S(1)}, bf16[64,2048]{1,0:T(8,128)(2,1)S(1)}, u32[]{:S(2)}, u32[]{:S(2)}) collective-permute-start(bf16[64,2048]{1,0:T(8,128)(2,1)S(1)} %add.5), channel_id=1, source_target_pairs={{0,8},{2,4},{4,2},{6,14},{8,0},{10,12},{12,10},{14,6},{16,24},{18,... | collective-permute-start | bytes 786440 | tf_op jit(solution)/shard_map/ppermute | solution.py:244
  51.6 1.3 %expert_pass.11.at_end.mid_b = bf16[64,2048]{1,0:T(8,128)(2,1)S(1)} custom-call(bf16[64,2048]{1,0:T(8,128)(2,1)S(1)} %collective-permute-done.12.at_end.a, bf16[64,2176]{1,0:T(8,128)(2,1)S(1)} %collective-permute-done.6.tag_end.at_end.at_mid, bf16[64,2176]{1,0:T(8,128)(2,1)S(1)} %collective-permute-done.at_end.at_mid.tag_end.tag_mid, ...), custom_call_target="tpu_custom_call" | custom-call | flops 402653184 | bytes 6291456 | tf_op jit(solution)/shard_map/expert_pass/pallas_call | solution.py:86
  52.9 2.4 %collective-permute-done.13.mid_a = bf16[64,2048]{1,0:T(8,128)(2,1)S(1)} collective-permute-done((bf16[64,2048]{1,0:T(8,128)(2,1)S(1)}, bf16[64,2048]{1,0:T(8,128)(2,1)S(1)}, u32[]{:S(2)}, u32[]{:S(2)}) %collective-permute-start.13) | collective-permute-done | bytes 262176 | tf_op jit(solution)/shard_map/ppermute | solution.py:244
  55.4 2.8 %collective-permute-done.8.far.a = bf16[64,2048]{1,0:T(8,128)(2,1)S(1)} collective-permute-done((bf16[64,2048]{1,0:T(8,128)(2,1)S(1)}, bf16[64,2048]{1,0:T(8,128)(2,1)S(1)}, u32[]{:S(2)}, u32[]{:S(2)}) %collective-permute-start.8) | collective-permute-done | bytes 262176 | tf_op jit(solution)/shard_map/ppermute | solution.py:241
  58.2 1.1 %collective-permute-start.15 = (bf16[64,2048]{1,0:T(8,128)(2,1)S(1)}, bf16[64,2048]{1,0:T(8,128)(2,1)S(1)}, u32[]{:S(2)}, u32[]{:S(2)}) collective-permute-start(bf16[64,2048]{1,0:T(8,128)(2,1)S(1)} %add.7), channel_id=1, source_target_pairs={{0,8},{2,4},{4,2},{6,14},{8,0},{10,12},{12,10},{14,6},{16,24},{18,... | collective-permute-start | bytes 786440 | tf_op jit(solution)/shard_map/ppermute | solution.py:244
  59.4 1.9 %collective-permute-start.16 = (bf16[64,2048]{1,0:T(8,128)(2,1)S(1)}, bf16[64,2048]{1,0:T(8,128)(2,1)S(1)}, u32[]{:S(2)}, u32[]{:S(2)}) collective-permute-start(bf16[64,2048]{1,0:T(8,128)(2,1)S(1)} %finish_first.1.first), channel_id=1, source_target_pairs={{0,8},{8,16},{16,24},{1,9},{9,17},{17,25},{2,10},{10,18},{18,26},{... | collective-permute-start | bytes 786440 | tf_op jit(solution)/shard_map/ppermute | solution.py:12
  61.4 1.1 %collective-permute-done.14.outer = bf16[64,2048]{1,0:T(8,128)(2,1)S(1)} collective-permute-done((bf16[64,2048]{1,0:T(8,128)(2,1)S(1)}, bf16[64,2048]{1,0:T(8,128)(2,1)S(1)}, u32[]{:S(2)}, u32[]{:S(2)}) %collective-permute-start.14) | collective-permute-done | bytes 262176 | tf_op jit(solution)/shard_map/ppermute | solution.py:241
  62.4 2.2 %collective-permute-done.15.inner = bf16[64,2048]{1,0:T(8,128)(2,1)S(1)} collective-permute-done((bf16[64,2048]{1,0:T(8,128)(2,1)S(1)}, bf16[64,2048]{1,0:T(8,128)(2,1)S(1)}, u32[]{:S(2)}, u32[]{:S(2)}) %collective-permute-start.15) | collective-permute-done | bytes 262176 | tf_op jit(solution)/shard_map/ppermute | solution.py:244
  64.8 1.9 %collective-permute-start.17 = (bf16[64,2048]{1,0:T(8,128)(2,1)S(1)}, bf16[64,2048]{1,0:T(8,128)(2,1)S(1)}, u32[]{:S(2)}, u32[]{:S(2)}) collective-permute-start(bf16[64,2048]{1,0:T(8,128)(2,1)S(1)} %finish_second.1.second), channel_id=1, source_target_pairs={{0,8},{8,16},{16,24},{1,9},{9,17},{17,25},{2,10},{10,18},{18,26},{... | collective-permute-start | bytes 786440 | tf_op jit(solution)/shard_map/ppermute | solution.py:12
  66.7 0.8 %join.2 = bf16[128,2048]{1,0:T(8,128)(2,1)} custom-call(bf16[64,2048]{1,0:T(8,128)(2,1)S(1)} %finish_first.1.first, bf16[64,2048]{1,0:T(8,128)(2,1)S(1)} %finish_second.1.second), custom_call_target="tpu_custom_call" | custom-call | tf_op jit(solution)/shard_map/join/pallas_call | solution.py:86
  67.5 4.9 %collective-permute-done.17.second = bf16[64,2048]{1,0:T(8,128)(2,1)S(1)} collective-permute-done((bf16[64,2048]{1,0:T(8,128)(2,1)S(1)}, bf16[64,2048]{1,0:T(8,128)(2,1)S(1)}, u32[]{:S(2)}, u32[]{:S(2)}) %collective-permute-start.17) | collective-permute-done | bytes 262176 | tf_op jit(solution)/shard_map/ppermute | solution.py:12
  72.5 0.8 %join.3 = bf16[128,2048]{1,0:T(8,128)(2,1)} custom-call(bf16[64,2048]{1,0:T(8,128)(2,1)S(1)} %collective-permute-done.16.first, bf16[64,2048]{1,0:T(8,128)(2,1)S(1)} %collective-permute-done.17.second), custom_call_target="tpu_custom_call" | custom-call | tf_op jit(solution)/shard_map/join/pallas_call | solution.py:86
  (27 shorter events, 3.8 us)
Async XLA Ops:
  1.7 8.5 %collective-permute-start = (bf16[64,2176]{1,0:T(8,128)(2,1)S(1)}, bf16[64,2176]{1,0:T(8,128)(2,1)S(1)}, u32[]{:S(2)}, u32[]{:S(2)}) collective-permute-start(bf16[64,2176]{1,0:T(8,128)(2,1)S(1)} %get-tuple-element.14.first), channel_id=1, source_target_pairs={{0,2},{2,0},{4,6},{6,4},{8,10},{10,8},{12,14},{14,12},{16,18},{18,... | collective-permute-start | bytes 835592 | tf_op jit(solution)/shard_map/ppermute | solution.py:241
  2.3 9.1 %collective-permute-start.1 = (bf16[64,2176]{1,0:T(8,128)(2,1)S(1)}, bf16[64,2176]{1,0:T(8,128)(2,1)S(1)}, u32[]{:S(2)}, u32[]{:S(2)}) collective-permute-start(bf16[64,2176]{1,0:T(8,128)(2,1)S(1)} %get-tuple-element.14.first), channel_id=1, source_target_pairs={{0,8},{2,4},{4,2},{6,14},{8,0},{10,12},{12,10},{14,6},{16,24},{18,... | collective-permute-start | bytes 835592 | tf_op jit(solution)/shard_map/ppermute | solution.py:244
  11.4 7.6 %collective-permute-start.6 = (bf16[64,2176]{1,0:T(8,128)(2,1)S(1)}, bf16[64,2176]{1,0:T(8,128)(2,1)S(1)}, u32[]{:S(2)}, u32[]{:S(2)}) collective-permute-start(bf16[64,2176]{1,0:T(8,128)(2,1)S(1)} %choose.7), channel_id=1, source_target_pairs={{0,2},{2,0},{4,6},{6,4},{8,10},{10,8},{12,14},{14,12},{16,18},{18,... | collective-permute-start | bytes 835592 | tf_op jit(solution)/shard_map/ppermute | solution.py:241
  11.4 8.9 %collective-permute-start.2 = (bf16[64,2176]{1,0:T(8,128)(2,1)S(1)}, bf16[64,2176]{1,0:T(8,128)(2,1)S(1)}, u32[]{:S(2)}, u32[]{:S(2)}) collective-permute-start(bf16[64,2176]{1,0:T(8,128)(2,1)S(1)} %collective-permute-done.at_end.at_mid.tag_end.tag_mid), channel_id=1, source_target_pairs={{0,8},{2,4},{4,2},{6,14},{8,0},{10,12},{12,10},{14,6},{16,24},{18,... | collective-permute-start | bytes 835592 | tf_op jit(solution)/shard_map/ppermute | solution.py:244
  19.0 9.4 %collective-permute-start.9 = (bf16[64,2176]{1,0:T(8,128)(2,1)S(1)}, bf16[64,2176]{1,0:T(8,128)(2,1)S(1)}, u32[]{:S(2)}, u32[]{:S(2)}) collective-permute-start(bf16[64,2176]{1,0:T(8,128)(2,1)S(1)} %collective-permute-done.6.tag_end.at_end.at_mid), channel_id=1, source_target_pairs={{0,8},{2,4},{4,2},{6,14},{8,0},{10,12},{12,10},{14,6},{16,24},{18,... | collective-permute-start | bytes 835592 | tf_op jit(solution)/shard_map/ppermute | solution.py:244
  20.4 8.3 %collective-permute-start.3 = (bf16[64,2176]{1,0:T(8,128)(2,1)S(1)}, bf16[64,2176]{1,0:T(8,128)(2,1)S(1)}, u32[]{:S(2)}, u32[]{:S(2)}) collective-permute-start(bf16[64,2176]{1,0:T(8,128)(2,1)S(1)} %choose.5), channel_id=1, source_target_pairs={{0,2},{2,0},{4,6},{6,4},{8,10},{10,8},{12,14},{14,12},{16,18},{18,... | collective-permute-start | bytes 835592 | tf_op jit(solution)/shard_map/ppermute | solution.py:241
  20.5 10.7 %collective-permute-start.4 = (bf16[64,2048]{1,0:T(8,128)(2,1)S(1)}, bf16[64,2048]{1,0:T(8,128)(2,1)S(1)}, u32[]{:S(2)}, u32[]{:S(2)}) collective-permute-start(bf16[64,2048]{1,0:T(8,128)(2,1)S(1)} %get-tuple-element.15.second.at_end.at_mid), channel_id=1, source_target_pairs={{0,8},{2,4},{4,2},{6,14},{8,0},{10,12},{12,10},{14,6},{16,24},{18,... | collective-permute-start | bytes 786440 | tf_op jit(solution)/shard_map/ppermute | solution.py:244
  28.4 9.2 %collective-permute-start.10 = (bf16[64,2048]{1,0:T(8,128)(2,1)S(1)}, bf16[64,2048]{1,0:T(8,128)(2,1)S(1)}, u32[]{:S(2)}, u32[]{:S(2)}) collective-permute-start(bf16[64,2048]{1,0:T(8,128)(2,1)S(1)} %choose.8), channel_id=1, source_target_pairs={{0,2},{2,0},{4,6},{6,4},{8,10},{10,8},{12,14},{14,12},{16,18},{18,... | collective-permute-start | bytes 786440 | tf_op jit(solution)/shard_map/ppermute | solution.py:241
  31.2 11.0 %collective-permute-start.5 = (bf16[64,2048]{1,0:T(8,128)(2,1)S(1)}, bf16[64,2048]{1,0:T(8,128)(2,1)S(1)}, u32[]{:S(2)}, u32[]{:S(2)}) collective-permute-start(bf16[64,2048]{1,0:T(8,128)(2,1)S(1)} %choose.6), channel_id=1, source_target_pairs={{0,2},{2,0},{4,6},{6,4},{8,10},{10,8},{12,14},{14,12},{16,18},{18,... | collective-permute-start | bytes 786440 | tf_op jit(solution)/shard_map/ppermute | solution.py:241
  39.0 6.4 %collective-permute-start.12 = (bf16[64,2048]{1,0:T(8,128)(2,1)S(1)}, bf16[64,2048]{1,0:T(8,128)(2,1)S(1)}, u32[]{:S(2)}, u32[]{:S(2)}) collective-permute-start(bf16[64,2048]{1,0:T(8,128)(2,1)S(1)} %choose.9), channel_id=1, source_target_pairs={{0,2},{2,0},{4,6},{6,4},{8,10},{10,8},{12,14},{14,12},{16,18},{18,... | collective-permute-start | bytes 786440 | tf_op jit(solution)/shard_map/ppermute | solution.py:241
  42.3 8.0 %collective-permute-start.7 = (bf16[64,2048]{1,0:T(8,128)(2,1)S(1)}, bf16[64,2048]{1,0:T(8,128)(2,1)S(1)}, u32[]{:S(2)}, u32[]{:S(2)}) collective-permute-start(bf16[64,2048]{1,0:T(8,128)(2,1)S(1)} %add.4), channel_id=1, source_target_pairs={{0,8},{2,4},{4,2},{6,14},{8,0},{10,12},{12,10},{14,6},{16,24},{18,... | collective-permute-start | bytes 786440 | tf_op jit(solution)/shard_map/ppermute | solution.py:244
  45.5 9.8 %collective-permute-start.13 = (bf16[64,2048]{1,0:T(8,128)(2,1)S(1)}, bf16[64,2048]{1,0:T(8,128)(2,1)S(1)}, u32[]{:S(2)}, u32[]{:S(2)}) collective-permute-start(bf16[64,2048]{1,0:T(8,128)(2,1)S(1)} %add.6), channel_id=1, source_target_pairs={{0,8},{2,4},{4,2},{6,14},{8,0},{10,12},{12,10},{14,6},{16,24},{18,... | collective-permute-start | bytes 786440 | tf_op jit(solution)/shard_map/ppermute | solution.py:244
  50.4 7.8 %collective-permute-start.8 = (bf16[64,2048]{1,0:T(8,128)(2,1)S(1)}, bf16[64,2048]{1,0:T(8,128)(2,1)S(1)}, u32[]{:S(2)}, u32[]{:S(2)}) collective-permute-start(bf16[64,2048]{1,0:T(8,128)(2,1)S(1)} %choose_sum.2), channel_id=1, source_target_pairs={{0,2},{2,0},{4,6},{6,4},{8,10},{10,8},{12,14},{14,12},{16,18},{18,... | collective-permute-start | bytes 786440 | tf_op jit(solution)/shard_map/ppermute | solution.py:241
  50.5 8.8 %collective-permute-start.11 = (bf16[64,2048]{1,0:T(8,128)(2,1)S(1)}, bf16[64,2048]{1,0:T(8,128)(2,1)S(1)}, u32[]{:S(2)}, u32[]{:S(2)}) collective-permute-start(bf16[64,2048]{1,0:T(8,128)(2,1)S(1)} %add.5), channel_id=1, source_target_pairs={{0,8},{2,4},{4,2},{6,14},{8,0},{10,12},{12,10},{14,6},{16,24},{18,... | collective-permute-start | bytes 786440 | tf_op jit(solution)/shard_map/ppermute | solution.py:244
  55.3 7.1 %collective-permute-start.14 = (bf16[64,2048]{1,0:T(8,128)(2,1)S(1)}, bf16[64,2048]{1,0:T(8,128)(2,1)S(1)}, u32[]{:S(2)}, u32[]{:S(2)}) collective-permute-start(bf16[64,2048]{1,0:T(8,128)(2,1)S(1)} %choose_sum.3), channel_id=1, source_target_pairs={{0,2},{2,0},{4,6},{6,4},{8,10},{10,8},{12,14},{14,12},{16,18},{18,... | collective-permute-start | bytes 786440 | tf_op jit(solution)/shard_map/ppermute | solution.py:241
  58.2 6.4 %collective-permute-start.15 = (bf16[64,2048]{1,0:T(8,128)(2,1)S(1)}, bf16[64,2048]{1,0:T(8,128)(2,1)S(1)}, u32[]{:S(2)}, u32[]{:S(2)}) collective-permute-start(bf16[64,2048]{1,0:T(8,128)(2,1)S(1)} %add.7), channel_id=1, source_target_pairs={{0,8},{2,4},{4,2},{6,14},{8,0},{10,12},{12,10},{14,6},{16,24},{18,... | collective-permute-start | bytes 786440 | tf_op jit(solution)/shard_map/ppermute | solution.py:244
  59.4 8.1 %collective-permute-start.16 = (bf16[64,2048]{1,0:T(8,128)(2,1)S(1)}, bf16[64,2048]{1,0:T(8,128)(2,1)S(1)}, u32[]{:S(2)}, u32[]{:S(2)}) collective-permute-start(bf16[64,2048]{1,0:T(8,128)(2,1)S(1)} %finish_first.1.first), channel_id=1, source_target_pairs={{0,8},{8,16},{16,24},{1,9},{9,17},{17,25},{2,10},{10,18},{18,26},{... | collective-permute-start | bytes 786440 | tf_op jit(solution)/shard_map/ppermute | solution.py:12
  64.8 7.7 %collective-permute-start.17 = (bf16[64,2048]{1,0:T(8,128)(2,1)S(1)}, bf16[64,2048]{1,0:T(8,128)(2,1)S(1)}, u32[]{:S(2)}, u32[]{:S(2)}) collective-permute-start(bf16[64,2048]{1,0:T(8,128)(2,1)S(1)} %finish_second.1.second), channel_id=1, source_target_pairs={{0,8},{8,16},{16,24},{1,9},{9,17},{17,25},{2,10},{10,18},{18,26},{... | collective-permute-start | bytes 786440 | tf_op jit(solution)/shard_map/ppermute | solution.py:12

commit v4 on v3

--- a/solution.py
+++ b/solution.py
@@ -55,6 +55,7 @@
 
 
 TAG = 128
+STREAMS = 2
 IN_VMEM = pl.BlockSpec(memory_space=pltpu.VMEM)
 ANYWHERE = pl.BlockSpec(memory_space=pl.ANY)
 
@@ -95,37 +96,33 @@
     )(*operands)
 
 
-def prepare(tokens, routes, weights, first, second, routes_here, weights_here, sems):
-    half, width = first.shape[0], tokens.shape[1]
-    copies = [
-        pltpu.make_async_copy(source, target, sems.at[i])
-        for i, (source, target) in enumerate(
-            (
-                (routes, routes_here),
-                (weights, weights_here),
-                (tokens.at[pl.ds(0, half)], first.at[:, pl.ds(0, width)]),
-                (tokens.at[pl.ds(half, half)], second),
-            )
-        )
-    ]
+def prepare(tokens, routes, weights, *refs):
+    pieces, (routes_here, weights_here, sems) = refs[: 2 * STREAMS], refs[2 * STREAMS :]
+    (count, width), piece = tokens.shape, pieces[0].shape[0]
+    moves = [(routes, routes_here), (weights, weights_here)] + [
+        (tokens.at[pl.ds(i * piece, piece)], ref if i % 2 else ref.at[:, pl.ds(0, width)])
+        for i, ref in enumerate(pieces)
+    ]
+    copies = [pltpu.make_async_copy(*move, sems.at[i]) for i, move in enumerate(moves)]
     for copy in copies:
         copy.start()
     for copy in copies[:2]:
         copy.wait()
-    names = lax.broadcasted_iota(jnp.int32, (8, 2 * half), 0)
-    rest = jnp.zeros((8, 2 * half), jnp.float32)
+    names = lax.broadcasted_iota(jnp.int32, (8, count), 0)
+    rest = jnp.zeros((8, count), jnp.float32)
     for k in range(routes.shape[0]):
         rest += jnp.where(routes_here[k : k + 1, :] == names, weights_here[k : k + 1, :], 0.0)
-    pieces = []
+    parts = []
     for _ in range(3):
-        pieces.append(narrow(rest).astype(jnp.float32))
-        rest = rest - pieces[-1]
-    pieces += [pltpu.roll(piece, half, 1) for piece in pieces]
-    pieces.append(jnp.zeros((TAG - 48, 2 * half), jnp.float32))
-    tags = narrow(jnp.concatenate(pieces, axis=0).T[:half])
+        parts.append(narrow(rest).astype(jnp.float32))
+        rest = rest - parts[-1]
+    parts += [pltpu.roll(part, count - piece, 1) for part in parts]
+    parts.append(jnp.zeros((TAG - 48, count), jnp.float32))
+    tags = narrow(jnp.concatenate(parts, axis=0).T)
     for copy in copies[2:]:
         copy.wait()
-    first[:, width:] = tags
+    for s in range(STREAMS):
+        pieces[2 * s][:, width:] = tags[2 * s * piece : (2 * s + 1) * piece]
 
 
 def weight_of(tags, late):
@@ -144,19 +141,20 @@
     return narrow(out).astype(jnp.float32)
 
 
-def own_pass(first, second, gate_hbm, up_hbm, down_hbm, gate_w, up_w, down_w, total, sems):
+def own_pass(*refs):
+    pieces, refs = refs[: 2 * STREAMS], refs[2 * STREAMS :]
+    from_hbm, (gate_w, up_w, down_w), total, sems = refs[:3], refs[3:6], refs[6], refs[7]
     copies = [
         pltpu.make_async_copy(source, target, sems.at[i])
-        for i, (source, target) in enumerate(
-            ((gate_hbm, gate_w), (up_hbm, up_w), (down_hbm, down_w))
-        )
+        for i, (source, target) in enumerate(zip(from_hbm, (gate_w, up_w, down_w)))
     ]
     for copy in copies:
         copy.start()
-    half, width = first.shape[0], total.shape[1]
-    rows = jnp.concatenate([first[:, :width], second[...]], axis=0)
-    tags = first[:, width:]
-    weight = jnp.concatenate([weight_of(tags, False), weight_of(tags, True)], axis=0)
+    width = total.shape[1]
+    rows = jnp.concatenate([piece[:, :width] for piece in pieces], axis=0)
+    weight = jnp.concatenate(
+        [weight_of(pieces[i // 2 * 2][:, width:], i % 2) for i in range(2 * STREAMS)], axis=0
+    )
     copies[0].wait()
     gate = jnp.dot(rows, gate_w[...], preferred_element_type=jnp.float32)
     copies[1].wait()
@@ -168,12 +166,19 @@
 
 
 def pass_of(late):
-    def body(at_end, at_mid, tag_end, tag_mid, gate_w, up_w, down_w, result):
+    def body(*refs):
         _, end = position()
-        width = result.shape[1]
-        rows = jnp.where(end, at_end[:, :width], at_mid[:, :width])
-        weight = weight_of(jnp.where(end, tag_end[:, width:], tag_mid[:, width:]), late)
-        result[...] = narrow(expert_of(rows, gate_w, up_w, down_w) * weight)
+        given, (gate_w, up_w, down_w), results = refs[: -3 - STREAMS], refs[-3 - STREAMS : -STREAMS], refs[-STREAMS:]
+        piece, width = results[0].shape
+        rows, weight = [], []
+        for s in range(STREAMS):
+            at_end, at_mid, tag_end, tag_mid = given[4 * s : 4 * s + 4]
+            rows.append(jnp.where(end, at_end[:, :width], at_mid[:, :width]))
+            weight.append(weight_of(jnp.where(end, tag_end[:, width:], tag_mid[:, width:]), late))
+        out = expert_of(jnp.concatenate(rows, axis=0), gate_w, up_w, down_w)
+        out = narrow(out * jnp.concatenate(weight, axis=0))
+        for s in range(STREAMS):
+            results[s][...] = out[s * piece : (s + 1) * piece]
 
     return body
 
@@ -197,36 +202,57 @@
     result[...] = narrow(wide(a) + wide(b))
 
 
-def finish_first(total, far, near, inner, result):
+def finish_first(total, *refs):
     _, end = position()
-    half, width = result.shape
-    at_mid = near[:, :width].astype(jnp.float32) + wide(inner)
-    result[...] = narrow(total[:half] + jnp.where(end, wide(far), at_mid))
-
-
-def finish_second(total, outer, inner, result):
-    _, end = position()
-    half = result.shape[0]
-    result[...] = narrow(total[half:] + wide(outer) + jnp.where(end, 0.0, wide(inner)))
-
-
-def join(first, second, whole, sems):
-    half = first.shape[0]
-    copies = [
-        pltpu.make_async_copy(part, whole.at[pl.ds(i * half, half)], sems.at[i])
-        for i, part in enumerate((first, second))
-    ]
+    given, result = refs[:-1], refs[-1]
+    (rows, width), piece = result.shape, result.shape[0] // STREAMS
+    for s in range(STREAMS):
+        far, near, inner = given[3 * s : 3 * s + 3]
+        at_mid = near[:, :width].astype(jnp.float32) + wide(inner)
+        own = total[2 * s * piece : (2 * s + 1) * piece]
+        result[s * piece : (s + 1) * piece] = narrow(own + jnp.where(end, wide(far), at_mid))
+
+
+def finish_second(stream):
+    def body(total, outer, inner, result):
+        _, end = position()
+        piece = result.shape[0]
+        own = total[(2 * stream + 1) * piece : (2 * stream + 2) * piece]
+        result[...] = narrow(own + wide(outer) + jnp.where(end, 0.0, wide(inner)))
+
+    return body
+
+
+def join(firsts, *refs):
+    seconds, whole, sems = refs[:STREAMS], refs[STREAMS], refs[STREAMS + 1]
+    piece = seconds[0].shape[0]
+    copies = []
+    for s in range(STREAMS):
+        for i, part in enumerate((firsts.at[pl.ds(s * piece, piece)], seconds[s])):
+            place = 2 * s + i
+            there = whole.at[pl.ds(place * piece, piece)]
+            copies.append(pltpu.make_async_copy(part, there, sems.at[place]))
     for copy in copies:
         copy.start()
     for copy in copies:
         copy.wait()
 
 
+def join_handed(*refs):
+    @pl.when(lax.axis_index("section") == 0)
+    def _():
+        for ref in refs[: 1 + STREAMS]:
+            ref[...] = jnp.zeros_like(ref)
+
+    join(*refs)
+
+
 def on_line(tokens, routes, route_weights, expert_gate, expert_up, expert_down):
     rows = tokens[0]
     count, width = rows.shape
-    half = count // 2
-    block = (half, width)
+    piece = count // (2 * STREAMS)
+    block = (piece, width)
+    both = range(STREAMS)
     weights = (expert_gate[0, 0], expert_up[0, 0], expert_down[0, 0])
     axes = ("section", "expert")
     sections = range(lax.axis_size("section"))
@@ -243,82 +269,104 @@
     def inner(value):
         return lax.ppermute(value, axes, inner_pairs)
 
-    tagged = (half, width + TAG)
-    first, second = run(
+    tagged = (piece, width + TAG)
+    pieces = run(
         prepare,
         "prepare",
-        [held(tagged), held(block)],
+        [held(tagged), held(block)] * STREAMS,
         rows,
         routes[0].T,
         route_weights[0].T,
         scratch=[
             held((routes.shape[2], count), jnp.int32),
             held((routes.shape[2], count), jnp.float32),
-            pltpu.SemaphoreType.DMA((4,)),
+            pltpu.SemaphoreType.DMA((2 + 2 * STREAMS,)),
         ],
         specs=[ANYWHERE] * 3,
     )
-    o0, i0 = outer(first), inner(first)
+    first, second = pieces[::2], pieces[1::2]
+    o, i, p = [[None] * 8 for _ in both], [[None] * 8 for _ in both], [None] * 8
+
+    def swap(k, s, to_outer, to_inner):
+        o[s][k], i[s][k] = outer(to_outer), inner(to_inner)
+
+    for s in both:
+        swap(0, s, first[s], first[s])
     *weights, total = run(
         own_pass,
         "own_pass",
         [held(w.shape) for w in weights] + [held((count, width), jnp.float32)],
-        first,
-        second,
+        *pieces,
         *weights,
         scratch=[pltpu.SemaphoreType.DMA((3,))],
-        specs=[IN_VMEM] * 2 + [ANYWHERE] * 3,
+        specs=[IN_VMEM] * len(pieces) + [ANYWHERE] * 3,
         work=(6 * count * weights[0].size, 6 * weights[0].size),
     )
-    o0, i0, total, *weights = lax.optimization_barrier((o0, i0, total, *weights))
-
-    def expert(late, rows, tags):
+    o[0][0], i[0][0], total, *weights = lax.optimization_barrier(
+        (o[0][0], i[0][0], total, *weights)
+    )
+
+    def expert(late, given):
         return run(
             pass_of(late),
             "expert_pass",
-            held(block),
-            *rows,
-            *tags,
+            [held(block)] * STREAMS,
+            *(x for s in both for x in given(s)),
             *weights,
-            work=(6 * half * weights[0].size, 6 * weights[0].size),
+            work=(6 * piece * STREAMS * weights[0].size, 6 * weights[0].size),
         )
 
     def mixed(body, *operands, shape=block):
         return run(body, body.__name__, held(shape), *operands)
 
-    near = (o0, o0)
-    o1, i1 = outer(mixed(choose, second, i0, shape=tagged)), inner(o0)
-    p1 = expert(False, near, near)
-    o2, i2 = outer(mixed(choose, p1, i1, shape=tagged)), inner(o1)
-    two = (o1, i0)
-    p2 = expert(False, two, two)
-    o3, i3 = outer(mixed(choose, p2, i2)), inner(second)
-    three = (o2, i1)
-    p3 = expert(False, three, three)
-    o4, i4 = outer(mixed(choose, p3, i3)), inner(mixed(add, o3, p2))
-    p4 = expert(True, (o3, i2), three)
-    o5, i5 = outer(mixed(choose, p4, second)), inner(mixed(add, o4, p3))
-    p5 = expert(True, (o4, i3), two)
-    o6, i6 = outer(mixed(choose_sum, p5, i5, p1)), inner(mixed(add, o5, p4))
-    p6 = expert(True, (o5, o1), near)
-    o7, i7 = outer(mixed(choose_sum, p6, i6, p6)), inner(mixed(add, o6, p5))
-    out_first = run(finish_first, "finish_first", held(block), total, o6, o2, i4)
-    next_first = passed_along(out_first, "section", 1)
-    out_second = run(finish_second, "finish_second", held(block), total, o7, i7)
-    next_second = passed_along(out_second, "section", 1)
-
-    def joined(a, b):
+    for s in both:
+        swap(1, s, mixed(choose, second[s], i[s][0], shape=tagged), o[s][0])
+    p[1] = expert(False, lambda s: (o[s][0],) * 4)
+    for s in both:
+        swap(2, s, mixed(choose, p[1][s], i[s][1], shape=tagged), o[s][1])
+    p[2] = expert(False, lambda s: (o[s][1], i[s][0]) * 2)
+    for s in both:
+        swap(3, s, mixed(choose, p[2][s], i[s][2]), second[s])
+    p[3] = expert(False, lambda s: (o[s][2], i[s][1]) * 2)
+    for s in both:
+        swap(4, s, mixed(choose, p[3][s], i[s][3]), mixed(add, o[s][3], p[2][s]))
+    p[4] = expert(True, lambda s: (o[s][3], i[s][2], o[s][2], i[s][1]))
+    for s in both:
+        swap(5, s, mixed(choose, p[4][s], second[s]), mixed(add, o[s][4], p[3][s]))
+    p[5] = expert(True, lambda s: (o[s][4], i[s][3], o[s][1], i[s][0]))
+    for s in both:
+        at_outer = mixed(choose_sum, p[5][s], i[s][5], p[1][s])
+        swap(6, s, at_outer, mixed(add, o[s][5], p[4][s]))
+    p[6] = expert(True, lambda s: (o[s][5], o[s][1], o[s][0], o[s][0]))
+    for s in both:
+        at_outer = mixed(choose_sum, p[6][s], i[s][6], p[6][s])
+        swap(7, s, at_outer, mixed(add, o[s][6], p[5][s]))
+    firsts = run(
+        finish_first,
+        "finish_first",
+        held((STREAMS * piece, width)),
+        total,
+        *(x for s in both for x in (o[s][6], o[s][2], i[s][4])),
+    )
+    seconds = [
+        run(finish_second(s), "finish_second", held(block), total, o[s][7], i[s][7]) for s in both
+    ]
+
+    def joined(body, parts):
         return run(
-            join,
-            "join",
+            body,
+            body.__name__,
             jax.ShapeDtypeStruct((count, width), jnp.bfloat16),
-            a,
-            b,
-            scratch=[pltpu.SemaphoreType.DMA((2,))],
+            *parts,
+            scratch=[pltpu.SemaphoreType.DMA((2 * STREAMS,))],
             out_specs=ANYWHERE,
         )
 
-    return (joined(out_first, out_second)[None], joined(next_first, next_second)[None])
+    parts = [firsts, *seconds]
+    count_s = lax.axis_size("section")
+    ring = [(s, (s + 1) % count_s) for s in range(count_s)]
+    handed = [lax.ppermute(part, "section", ring) for part in parts]
+    return (joined(join, parts)[None], joined(join_handed, handed)[None])
 
 
 def solution(mesh):

time: 73.4 us -> 69.6 us (0.948)
  waiting for transfers between devices: 40.7 us -> 22.8 us
  starting transfers between devices: 17.2 us -> 30.9 us
    ppermute x8 -> x16, waiting for transfers between devices: 19.5 us -> 9.36 us  [outer(): return lax.ppermute(value, axes, outer_pairs)]
    ppermute x8 -> x16, starting transfers between devices: 11.8 us -> 21.1 us  [inner(): return lax.ppermute(value, axes, inner_pairs)]
    ppermute x8 -> x16, starting transfers between devices: 1.63 us -> 9.59 us  [outer(): return lax.ppermute(value, axes, outer_pairs)]
    ppermute x8 -> x16, waiting for transfers between devices: 16.2 us -> 9.91 us  [inner(): return lax.ppermute(value, axes, inner_pairs)]
    ppermute x2 -> x3, starting transfers between devices: 3.84 us -> 0.17 us  [on_line(): handed = [lax.ppermute(part, 'section', ring) for part in parts]]
    ppermute x2 -> x3, waiting for transfers between devices: 4.94 us -> 3.55 us  [on_line(): handed = [lax.ppermute(part, 'section', ring) for part in parts]]
    pallas_call x23 -> x35, Pallas kernels: 14.5 us -> 14.7 us  [run(): pl.pallas_call(body, out_shape=out_shape, in_specs=specs, out_specs=out_s...]
  transfers between devices with their start and end apart: 18 -> 35, of which waited for: 15 -> 18; matrix products, arithmetic and copies ran while one was open for 0% -> 0% of each run, Pallas kernels for 17% -> 18%
where the time goes in v4:
time: 69.6 us; the launch traced here: 69.4 us
  starting transfers between devices  30.9 us (44%)
  waiting for transfers between devices  22.8 us (33%)
  Pallas kernels  14.7 us (21%)
  between operations  0.98 us (1%)
    ppermute x16, starting transfers between devices, inner(): return lax.ppermute(value, axes, inner_pairs)  21.1 us
    pallas_call x35, Pallas kernels, run(): pl.pallas_call(body, out_shape=out_shape, in_specs=specs, out_specs=out_s...  14.7 us
    ppermute x16, waiting for transfers between devices, inner(): return lax.ppermute(value, axes, inner_pairs)  9.91 us
    ppermute x16, starting transfers between devices, outer(): return lax.ppermute(value, axes, outer_pairs)  9.59 us
    ppermute x16, waiting for transfers between devices, outer(): return lax.ppermute(value, axes, outer_pairs)  9.36 us
    ppermute x3, waiting for transfers between devices, on_line(): handed = [lax.ppermute(part, 'section', ring) for part in parts]  3.55 us
  transfers between devices with their start and end apart: 35, of which 18 were waited for; matrix products, arithmetic and copies ran while one was open for 0% of the time, Pallas kernels for 18%

profile of v4, /device:TPU:12, one launch (start us, length us, event | category | flops | bytes accessed | tf_op | source)
XLA Modules:
  0.0 69.4 jit_solution(8121080494965024857)
XLA Ops:
  0.6 1.2 %prepare.1 = (bf16[32,2176]{1,0:T(8,128)(2,1)S(1)}, bf16[32,2048]{1,0:T(8,128)(2,1)S(1)}, bf16[32,2176]{1,0:T(8,128)(2,1)S(1)}, bf16[32,2048]{1,0:T(8,128)(2,1)S(1)}) custom-call(bf16[128,2048]{1,0:T(8,128)(2,1)} %bitcast.15, s32[2,128]{1,0:T(2,128)} %bitcast.18, f32[2,128]{1,0:T(2,128)} %bitcast.19), custom_call_target="tpu_custom_call" | custom-call | tf_op jit(solution)/shard_map/prepare/pallas_call | solution.py:87
  2.3 2.7 %collective-permute-start.1 = (bf16[32,2176]{1,0:T(8,128)(2,1)S(1)}, bf16[32,2176]{1,0:T(8,128)(2,1)S(1)}, u32[]{:S(2)}, u32[]{:S(2)}) collective-permute-start(bf16[32,2176]{1,0:T(8,128)(2,1)S(1)} %get-tuple-element.28.refs_0_), channel_id=1, source_target_pairs={{0,8},{2,4},{4,2},{6,14},{8,0},{10,12},{12,10},{14,6},{16,24},{18,... | collective-permute-start | bytes 417800 | tf_op jit(solution)/shard_map/ppermute | solution.py:270
  5.1 3.4 %own_pass.1 = (bf16[2048,512]{1,0:T(8,128)(2,1)S(1)}, bf16[2048,512]{1,0:T(8,128)(2,1)S(1)}, bf16[512,2048]{1,0:T(8,128)(2,1)S(1)}, f32[128,2048]{1,0:T(8,128)S(1)}) custom-call(bf16[32,2176]{1,0:T(8,128)(2,1)S(1)} %get-tuple-element.28.refs_0_, bf16[32,2048]{1,0:T(8,128)(2,1)S(1)} %get-tuple-element.29.refs_1_.at_end.at_mid, ...), custom_call_target="tpu_custom_call" | custom-call | flops 805306368 | bytes 6291456 | tf_op jit(solution)/shard_map/own_pass/pallas_call | solution.py:87
  8.5 1.1 %collective-permute-done.1.at_mid.refs_3_.refs_1_ = bf16[32,2176]{1,0:T(8,128)(2,1)S(1)} collective-permute-done((bf16[32,2176]{1,0:T(8,128)(2,1)S(1)}, bf16[32,2176]{1,0:T(8,128)(2,1)S(1)}, u32[]{:S(2)}, u32[]{:S(2)}) %collective-permute-start.1) | collective-permute-done | bytes 139296 | tf_op jit(solution)/shard_map/ppermute | solution.py:270
  9.6 1.0 %collective-permute-start.9 = (bf16[32,2176]{1,0:T(8,128)(2,1)S(1)}, bf16[32,2176]{1,0:T(8,128)(2,1)S(1)}, u32[]{:S(2)}, u32[]{:S(2)}) collective-permute-start(bf16[32,2176]{1,0:T(8,128)(2,1)S(1)} %choose.13), channel_id=1, source_target_pairs={{0,2},{2,0},{4,6},{6,4},{8,10},{10,8},{12,14},{14,12},{16,18},{18,... | collective-permute-start | bytes 417800 | tf_op jit(solution)/shard_map/ppermute | solution.py:267
  11.8 2.1 %collective-permute-start.3 = (bf16[32,2176]{1,0:T(8,128)(2,1)S(1)}, bf16[32,2176]{1,0:T(8,128)(2,1)S(1)}, u32[]{:S(2)}, u32[]{:S(2)}) collective-permute-start(bf16[32,2176]{1,0:T(8,128)(2,1)S(1)} %collective-permute-done.refs_0_.refs_1_.refs_2_.refs_3_), channel_id=1, source_target_pairs={{0,8},{2,4},{4,2},{6,14},{8,0},{10,12},{12,10},{14,6},{16,24},{18,... | collective-permute-start | bytes 417800 | tf_op jit(solution)/shard_map/ppermute | solution.py:270
  13.9 2.2 %collective-permute-done.9.refs_2_.refs_0_.refs_1_ = bf16[32,2176]{1,0:T(8,128)(2,1)S(1)} collective-permute-done((bf16[32,2176]{1,0:T(8,128)(2,1)S(1)}, bf16[32,2176]{1,0:T(8,128)(2,1)S(1)}, u32[]{:S(2)}, u32[]{:S(2)}) %collective-permute-start.9) | collective-permute-done | bytes 139296 | tf_op jit(solution)/shard_map/ppermute | solution.py:267
  16.0 1.4 %collective-permute-start.16 = (bf16[32,2176]{1,0:T(8,128)(2,1)S(1)}, bf16[32,2176]{1,0:T(8,128)(2,1)S(1)}, u32[]{:S(2)}, u32[]{:S(2)}) collective-permute-start(bf16[32,2176]{1,0:T(8,128)(2,1)S(1)} %collective-permute-done.9.refs_2_.refs_0_.refs_1_), channel_id=1, source_target_pairs={{0,8},{2,4},{4,2},{6,14},{8,0},{10,12},{12,10},{14,6},{16,24},{18,... | collective-permute-start | bytes 417800 | tf_op jit(solution)/shard_map/ppermute | solution.py:270
  17.5 1.3 %expert_pass.6 = (bf16[32,2048]{1,0:T(8,128)(2,1)S(1)}, bf16[32,2048]{1,0:T(8,128)(2,1)S(1)}) custom-call(bf16[32,2176]{1,0:T(8,128)(2,1)S(1)} %collective-permute-done.refs_0_.refs_1_.refs_2_.refs_3_, bf16[32,2176]{1,0:T(8,128)(2,1)S(1)} %collective-permute-done.refs_0_.refs_1_.refs_2_.refs_3_, ...), custom_call_target="tpu_custom_call" | custom-call | flops 402653184 | bytes 6291456 | tf_op jit(solution)/shard_map/expert_pass/pallas_call | solution.py:87
  19.5 1.9 %collective-permute-done.5.at_mid.refs_5_.refs_7_ = bf16[32,2176]{1,0:T(8,128)(2,1)S(1)} collective-permute-done((bf16[32,2176]{1,0:T(8,128)(2,1)S(1)}, bf16[32,2176]{1,0:T(8,128)(2,1)S(1)}, u32[]{:S(2)}, u32[]{:S(2)}) %collective-permute-start.5) | collective-permute-done | bytes 139296 | tf_op jit(solution)/shard_map/ppermute | solution.py:270
  21.7 2.0 %collective-permute-start.7 = (bf16[32,2048]{1,0:T(8,128)(2,1)S(1)}, bf16[32,2048]{1,0:T(8,128)(2,1)S(1)}, u32[]{:S(2)}, u32[]{:S(2)}) collective-permute-start(bf16[32,2048]{1,0:T(8,128)(2,1)S(1)} %get-tuple-element.29.refs_1_.at_end.at_mid), channel_id=1, source_target_pairs={{0,8},{2,4},{4,2},{6,14},{8,0},{10,12},{12,10},{14,6},{16,24},{18,... | collective-permute-start | bytes 393224 | tf_op jit(solution)/shard_map/ppermute | solution.py:270
  23.6 1.3 %expert_pass.9 = (bf16[32,2048]{1,0:T(8,128)(2,1)S(1)}, bf16[32,2048]{1,0:T(8,128)(2,1)S(1)}) custom-call(bf16[32,2176]{1,0:T(8,128)(2,1)S(1)} %collective-permute-done.9.refs_2_.refs_0_.refs_1_, bf16[32,2176]{1,0:T(8,128)(2,1)S(1)} %collective-permute-done.1.at_mid.refs_3_.refs_1_, bf16[32,2176]{1,0:T(8,128)(2,1)S(1)} %collective-permute-done.9.refs_2_.refs_0_.refs_1_, ...), custom_call_target="tpu_custom_call" | custom-call | flops 402653184 | bytes 6291456 | tf_op jit(solution)/shard_map/expert_pass/pallas_call | solution.py:87
  24.9 1.5 %collective-permute-start.10 = (bf16[32,2048]{1,0:T(8,128)(2,1)S(1)}, bf16[32,2048]{1,0:T(8,128)(2,1)S(1)}, u32[]{:S(2)}, u32[]{:S(2)}) collective-permute-start(bf16[32,2048]{1,0:T(8,128)(2,1)S(1)} %get-tuple-element.31.refs_3_.at_end.at_mid), channel_id=1, source_target_pairs={{0,8},{2,4},{4,2},{6,14},{8,0},{10,12},{12,10},{14,6},{16,24},{18,... | collective-permute-start | bytes 393224 | tf_op jit(solution)/shard_map/ppermute | solution.py:270
  27.4 2.1 %collective-permute-start.22 = (bf16[32,2048]{1,0:T(8,128)(2,1)S(1)}, bf16[32,2048]{1,0:T(8,128)(2,1)S(1)}, u32[]{:S(2)}, u32[]{:S(2)}) collective-permute-start(bf16[32,2048]{1,0:T(8,128)(2,1)S(1)} %choose.17), channel_id=1, source_target_pairs={{0,2},{2,0},{4,6},{6,4},{8,10},{10,8},{12,14},{14,12},{16,18},{18,... | collective-permute-start | bytes 393224 | tf_op jit(solution)/shard_map/ppermute | solution.py:267
  29.5 1.3 %expert_pass.7 = (bf16[32,2048]{1,0:T(8,128)(2,1)S(1)}, bf16[32,2048]{1,0:T(8,128)(2,1)S(1)}) custom-call(bf16[32,2176]{1,0:T(8,128)(2,1)S(1)} %collective-permute-done.4.refs_0_.refs_2_.refs_1_, bf16[32,2176]{1,0:T(8,128)(2,1)S(1)} %collective-permute-done.3.at_mid.refs_1_.refs_3_, bf16[32,2176]{1,0:T(8,128)(2,1)S(1)} %collective-permute-done.4.refs_0_.refs_2_.refs_1_, ...), custom_call_target="tpu_custom_call" | custom-call | flops 402653184 | bytes 6291456 | tf_op jit(solution)/shard_map/expert_pass/pallas_call | solution.py:87
  31.0 2.1 %collective-permute-start.11 = (bf16[32,2048]{1,0:T(8,128)(2,1)S(1)}, bf16[32,2048]{1,0:T(8,128)(2,1)S(1)}, u32[]{:S(2)}, u32[]{:S(2)}) collective-permute-start(bf16[32,2048]{1,0:T(8,128)(2,1)S(1)} %choose.14), channel_id=1, source_target_pairs={{0,2},{2,0},{4,6},{6,4},{8,10},{10,8},{12,14},{14,12},{16,18},{18,... | collective-permute-start | bytes 393224 | tf_op jit(solution)/shard_map/ppermute | solution.py:267
  33.5 2.8 %collective-permute-done.22.a.refs_4_ = bf16[32,2048]{1,0:T(8,128)(2,1)S(1)} collective-permute-done((bf16[32,2048]{1,0:T(8,128)(2,1)S(1)}, bf16[32,2048]{1,0:T(8,128)(2,1)S(1)}, u32[]{:S(2)}, u32[]{:S(2)}) %collective-permute-start.22) | collective-permute-done | bytes 131104 | tf_op jit(solution)/shard_map/ppermute | solution.py:267
  36.4 1.3 %expert_pass.10 = (bf16[32,2048]{1,0:T(8,128)(2,1)S(1)}, bf16[32,2048]{1,0:T(8,128)(2,1)S(1)}) custom-call(bf16[32,2048]{1,0:T(8,128)(2,1)S(1)} %collective-permute-done.17.a.refs_0_, bf16[32,2176]{1,0:T(8,128)(2,1)S(1)} %collective-permute-done.16.at_mid.refs_1_, bf16[32,2176]{1,0:T(8,128)(2,1)S(1)} %collective-permute-done.4.refs_0_.refs_2_.refs_1_, ...), custom_call_target="tpu_custom_call" | custom-call | flops 402653184 | bytes 6291456 | tf_op jit(solution)/shard_map/expert_pass/pallas_call | solution.py:87
  38.0 2.0 %collective-permute-start.14 = (bf16[32,2048]{1,0:T(8,128)(2,1)S(1)}, bf16[32,2048]{1,0:T(8,128)(2,1)S(1)}, u32[]{:S(2)}, u32[]{:S(2)}) collective-permute-start(bf16[32,2048]{1,0:T(8,128)(2,1)S(1)} %add.8), channel_id=1, source_target_pairs={{0,8},{2,4},{4,2},{6,14},{8,0},{10,12},{12,10},{14,6},{16,24},{18,... | collective-permute-start | bytes 393224 | tf_op jit(solution)/shard_map/ppermute | solution.py:270
  40.2 2.0 %collective-permute-start.19 = (bf16[32,2048]{1,0:T(8,128)(2,1)S(1)}, bf16[32,2048]{1,0:T(8,128)(2,1)S(1)}, u32[]{:S(2)}, u32[]{:S(2)}) collective-permute-start(bf16[32,2048]{1,0:T(8,128)(2,1)S(1)} %add.10), channel_id=1, source_target_pairs={{0,8},{2,4},{4,2},{6,14},{8,0},{10,12},{12,10},{14,6},{16,24},{18,... | collective-permute-start | bytes 393224 | tf_op jit(solution)/shard_map/ppermute | solution.py:270
  42.2 1.9 %collective-permute-done.24.refs_0_.a = bf16[32,2048]{1,0:T(8,128)(2,1)S(1)} collective-permute-done((bf16[32,2048]{1,0:T(8,128)(2,1)S(1)}, bf16[32,2048]{1,0:T(8,128)(2,1)S(1)}, u32[]{:S(2)}, u32[]{:S(2)}) %collective-permute-start.24) | collective-permute-done | bytes 131104 | tf_op jit(solution)/shard_map/ppermute | solution.py:267
  44.1 2.1 %collective-permute-start.26 = (bf16[32,2048]{1,0:T(8,128)(2,1)S(1)}, bf16[32,2048]{1,0:T(8,128)(2,1)S(1)}, u32[]{:S(2)}, u32[]{:S(2)}) collective-permute-start(bf16[32,2048]{1,0:T(8,128)(2,1)S(1)} %add.12), channel_id=1, source_target_pairs={{0,8},{2,4},{4,2},{6,14},{8,0},{10,12},{12,10},{14,6},{16,24},{18,... | collective-permute-start | bytes 393224 | tf_op jit(solution)/shard_map/ppermute | solution.py:270
  46.3 1.3 %expert_pass.8 = (bf16[32,2048]{1,0:T(8,128)(2,1)S(1)}, bf16[32,2048]{1,0:T(8,128)(2,1)S(1)}) custom-call(bf16[32,2048]{1,0:T(8,128)(2,1)S(1)} %collective-permute-done.8.refs_0_.a, bf16[32,2048]{1,0:T(8,128)(2,1)S(1)} %collective-permute-done.7.at_mid.refs_1_, bf16[32,2176]{1,0:T(8,128)(2,1)S(1)} %collective-permute-done.9.refs_2_.refs_0_.refs_1_, ...), custom_call_target="tpu_custom_call" | custom-call | flops 402653184 | bytes 6291456 | tf_op jit(solution)/shard_map/expert_pass/pallas_call | solution.py:87
  47.9 2.1 %collective-permute-start.20 = (bf16[32,2048]{1,0:T(8,128)(2,1)S(1)}, bf16[32,2048]{1,0:T(8,128)(2,1)S(1)}, u32[]{:S(2)}, u32[]{:S(2)}) collective-permute-start(bf16[32,2048]{1,0:T(8,128)(2,1)S(1)} %choose_sum.5), channel_id=1, source_target_pairs={{0,2},{2,0},{4,6},{6,4},{8,10},{10,8},{12,14},{14,12},{16,18},{18,... | collective-permute-start | bytes 393224 | tf_op jit(solution)/shard_map/ppermute | solution.py:267
  50.1 2.2 %collective-permute-start.23 = (bf16[32,2048]{1,0:T(8,128)(2,1)S(1)}, bf16[32,2048]{1,0:T(8,128)(2,1)S(1)}, u32[]{:S(2)}, u32[]{:S(2)}) collective-permute-start(bf16[32,2048]{1,0:T(8,128)(2,1)S(1)} %add.11), channel_id=1, source_target_pairs={{0,8},{2,4},{4,2},{6,14},{8,0},{10,12},{12,10},{14,6},{16,24},{18,... | collective-permute-start | bytes 393224 | tf_op jit(solution)/shard_map/ppermute | solution.py:270
  52.3 1.3 %expert_pass.11 = (bf16[32,2048]{1,0:T(8,128)(2,1)S(1)}, bf16[32,2048]{1,0:T(8,128)(2,1)S(1)}) custom-call(bf16[32,2048]{1,0:T(8,128)(2,1)S(1)} %collective-permute-done.24.refs_0_.a, bf16[32,2176]{1,0:T(8,128)(2,1)S(1)} %collective-permute-done.9.refs_2_.refs_0_.refs_1_, bf16[32,2176]{1,0:T(8,128)(2,1)S(1)} %collective-permute-done.refs_0_.refs_1_.refs_2_.refs_3_, ...), custom_call_target="tpu_custom_call" | custom-call | flops 402653184 | bytes 6291456 | tf_op jit(solution)/shard_map/expert_pass/pallas_call | solution.py:87
  56.4 1.3 %collective-permute-start.31 = (bf16[32,2048]{1,0:T(8,128)(2,1)S(1)}, bf16[32,2048]{1,0:T(8,128)(2,1)S(1)}, u32[]{:S(2)}, u32[]{:S(2)}) collective-permute-start(bf16[32,2048]{1,0:T(8,128)(2,1)S(1)} %add.15), channel_id=1, source_target_pairs={{0,8},{2,4},{4,2},{6,14},{8,0},{10,12},{12,10},{14,6},{16,24},{18,... | collective-permute-start | bytes 393224 | tf_op jit(solution)/shard_map/ppermute | solution.py:270
  57.7 1.5 %collective-permute-done.23.refs_5_ = bf16[32,2048]{1,0:T(8,128)(2,1)S(1)} collective-permute-done((bf16[32,2048]{1,0:T(8,128)(2,1)S(1)}, bf16[32,2048]{1,0:T(8,128)(2,1)S(1)}, u32[]{:S(2)}, u32[]{:S(2)}) %collective-permute-start.23) | collective-permute-done | bytes 131104 | tf_op jit(solution)/shard_map/ppermute | solution.py:270
  60.3 1.7 %collective-permute-done.28.inner = bf16[32,2048]{1,0:T(8,128)(2,1)S(1)} collective-permute-done((bf16[32,2048]{1,0:T(8,128)(2,1)S(1)}, bf16[32,2048]{1,0:T(8,128)(2,1)S(1)}, u32[]{:S(2)}, u32[]{:S(2)}) %collective-permute-start.28) | collective-permute-done | bytes 131104 | tf_op jit(solution)/shard_map/ppermute | solution.py:270
  62.1 1.9 %collective-permute-done.31.inner = bf16[32,2048]{1,0:T(8,128)(2,1)S(1)} collective-permute-done((bf16[32,2048]{1,0:T(8,128)(2,1)S(1)}, bf16[32,2048]{1,0:T(8,128)(2,1)S(1)}, u32[]{:S(2)}, u32[]{:S(2)}) %collective-permute-start.31) | collective-permute-done | bytes 131104 | tf_op jit(solution)/shard_map/ppermute | solution.py:270
  65.0 1.5 %collective-permute-done.33.refs_1_ = bf16[32,2048]{1,0:T(8,128)(2,1)S(1)} collective-permute-done((bf16[32,2048]{1,0:T(8,128)(2,1)S(1)}, bf16[32,2048]{1,0:T(8,128)(2,1)S(1)}, u32[]{:S(2)}, u32[]{:S(2)}) %collective-permute-start.33) | collective-permute-done | bytes 131104 | tf_op jit(solution)/shard_map/ppermute | solution.py:368
  66.6 2.0 %collective-permute-done.34.refs_2_ = bf16[32,2048]{1,0:T(8,128)(2,1)S(1)} collective-permute-done((bf16[32,2048]{1,0:T(8,128)(2,1)S(1)}, bf16[32,2048]{1,0:T(8,128)(2,1)S(1)}, u32[]{:S(2)}, u32[]{:S(2)}) %collective-permute-start.34) | collective-permute-done | bytes 131104 | tf_op jit(solution)/shard_map/ppermute | solution.py:368
  (73 shorter events, 11.1 us)
Async XLA Ops:
  1.8 6.7 %collective-permute-start = (bf16[32,2176]{1,0:T(8,128)(2,1)S(1)}, bf16[32,2176]{1,0:T(8,128)(2,1)S(1)}, u32[]{:S(2)}, u32[]{:S(2)}) collective-permute-start(bf16[32,2176]{1,0:T(8,128)(2,1)S(1)} %get-tuple-element.28.refs_0_), channel_id=1, source_target_pairs={{0,2},{2,0},{4,6},{6,4},{8,10},{10,8},{12,14},{14,12},{16,18},{18,... | collective-permute-start | bytes 417800 | tf_op jit(solution)/shard_map/ppermute | solution.py:267
  2.3 7.2 %collective-permute-start.1 = (bf16[32,2176]{1,0:T(8,128)(2,1)S(1)}, bf16[32,2176]{1,0:T(8,128)(2,1)S(1)}, u32[]{:S(2)}, u32[]{:S(2)}) collective-permute-start(bf16[32,2176]{1,0:T(8,128)(2,1)S(1)} %get-tuple-element.28.refs_0_), channel_id=1, source_target_pairs={{0,8},{2,4},{4,2},{6,14},{8,0},{10,12},{12,10},{14,6},{16,24},{18,... | collective-permute-start | bytes 417800 | tf_op jit(solution)/shard_map/ppermute | solution.py:270
  5.0 6.4 %collective-permute-start.12 = (bf16[32,2176]{1,0:T(8,128)(2,1)S(1)}, bf16[32,2176]{1,0:T(8,128)(2,1)S(1)}, u32[]{:S(2)}, u32[]{:S(2)}) collective-permute-start(bf16[32,2176]{1,0:T(8,128)(2,1)S(1)} %get-tuple-element.30.refs_2_), channel_id=1, source_target_pairs={{0,8},{2,4},{4,2},{6,14},{8,0},{10,12},{12,10},{14,6},{16,24},{18,... | collective-permute-start | bytes 417800 | tf_op jit(solution)/shard_map/ppermute | solution.py:270
  5.1 8.8 %collective-permute-start.2 = (bf16[32,2176]{1,0:T(8,128)(2,1)S(1)}, bf16[32,2176]{1,0:T(8,128)(2,1)S(1)}, u32[]{:S(2)}, u32[]{:S(2)}) collective-permute-start(bf16[32,2176]{1,0:T(8,128)(2,1)S(1)} %get-tuple-element.30.refs_2_), channel_id=1, source_target_pairs={{0,2},{2,0},{4,6},{6,4},{8,10},{10,8},{12,14},{14,12},{16,18},{18,... | collective-permute-start | bytes 417800 | tf_op jit(solution)/shard_map/ppermute | solution.py:267
  9.6 6.4 %collective-permute-start.9 = (bf16[32,2176]{1,0:T(8,128)(2,1)S(1)}, bf16[32,2176]{1,0:T(8,128)(2,1)S(1)}, u32[]{:S(2)}, u32[]{:S(2)}) collective-permute-start(bf16[32,2176]{1,0:T(8,128)(2,1)S(1)} %choose.13), channel_id=1, source_target_pairs={{0,2},{2,0},{4,6},{6,4},{8,10},{10,8},{12,14},{14,12},{16,18},{18,... | collective-permute-start | bytes 417800 | tf_op jit(solution)/shard_map/ppermute | solution.py:267
  11.4 7.3 %collective-permute-start.13 = (bf16[32,2176]{1,0:T(8,128)(2,1)S(1)}, bf16[32,2176]{1,0:T(8,128)(2,1)S(1)}, u32[]{:S(2)}, u32[]{:S(2)}) collective-permute-start(bf16[32,2176]{1,0:T(8,128)(2,1)S(1)} %choose.15), channel_id=1, source_target_pairs={{0,2},{2,0},{4,6},{6,4},{8,10},{10,8},{12,14},{14,12},{16,18},{18,... | collective-permute-start | bytes 417800 | tf_op jit(solution)/shard_map/ppermute | solution.py:267
  11.8 7.6 %collective-permute-start.3 = (bf16[32,2176]{1,0:T(8,128)(2,1)S(1)}, bf16[32,2176]{1,0:T(8,128)(2,1)S(1)}, u32[]{:S(2)}, u32[]{:S(2)}) collective-permute-start(bf16[32,2176]{1,0:T(8,128)(2,1)S(1)} %collective-permute-done.refs_0_.refs_1_.refs_2_.refs_3_), channel_id=1, source_target_pairs={{0,8},{2,4},{4,2},{6,14},{8,0},{10,12},{12,10},{14,6},{16,24},{18,... | collective-permute-start | bytes 417800 | tf_op jit(solution)/shard_map/ppermute | solution.py:270
  13.9 7.6 %collective-permute-start.5 = (bf16[32,2176]{1,0:T(8,128)(2,1)S(1)}, bf16[32,2176]{1,0:T(8,128)(2,1)S(1)}, u32[]{:S(2)}, u32[]{:S(2)}) collective-permute-start(bf16[32,2176]{1,0:T(8,128)(2,1)S(1)} %collective-permute-done.2.refs_4_.refs_5_.refs_6_.refs_7_), channel_id=1, source_target_pairs={{0,8},{2,4},{4,2},{6,14},{8,0},{10,12},{12,10},{14,6},{16,24},{18,... | collective-permute-start | bytes 417800 | tf_op jit(solution)/shard_map/ppermute | solution.py:270
  16.0 8.9 %collective-permute-start.16 = (bf16[32,2176]{1,0:T(8,128)(2,1)S(1)}, bf16[32,2176]{1,0:T(8,128)(2,1)S(1)}, u32[]{:S(2)}, u32[]{:S(2)}) collective-permute-start(bf16[32,2176]{1,0:T(8,128)(2,1)S(1)} %collective-permute-done.9.refs_2_.refs_0_.refs_1_), channel_id=1, source_target_pairs={{0,8},{2,4},{4,2},{6,14},{8,0},{10,12},{12,10},{14,6},{16,24},{18,... | collective-permute-start | bytes 417800 | tf_op jit(solution)/shard_map/ppermute | solution.py:270
  18.8 8.6 %collective-permute-start.21 = (bf16[32,2176]{1,0:T(8,128)(2,1)S(1)}, bf16[32,2176]{1,0:T(8,128)(2,1)S(1)}, u32[]{:S(2)}, u32[]{:S(2)}) collective-permute-start(bf16[32,2176]{1,0:T(8,128)(2,1)S(1)} %collective-permute-done.13.refs_6_.refs_4_.refs_5_), channel_id=1, source_target_pairs={{0,8},{2,4},{4,2},{6,14},{8,0},{10,12},{12,10},{14,6},{16,24},{18,... | collective-permute-start | bytes 417800 | tf_op jit(solution)/shard_map/ppermute | solution.py:270
  19.5 8.0 %collective-permute-start.4 = (bf16[32,2176]{1,0:T(8,128)(2,1)S(1)}, bf16[32,2176]{1,0:T(8,128)(2,1)S(1)}, u32[]{:S(2)}, u32[]{:S(2)}) collective-permute-start(bf16[32,2176]{1,0:T(8,128)(2,1)S(1)} %choose.10), channel_id=1, source_target_pairs={{0,2},{2,0},{4,6},{6,4},{8,10},{10,8},{12,14},{14,12},{16,18},{18,... | collective-permute-start | bytes 417800 | tf_op jit(solution)/shard_map/ppermute | solution.py:267
  21.5 8.1 %collective-permute-start.6 = (bf16[32,2176]{1,0:T(8,128)(2,1)S(1)}, bf16[32,2176]{1,0:T(8,128)(2,1)S(1)}, u32[]{:S(2)}, u32[]{:S(2)}) collective-permute-start(bf16[32,2176]{1,0:T(8,128)(2,1)S(1)} %choose.11), channel_id=1, source_target_pairs={{0,2},{2,0},{4,6},{6,4},{8,10},{10,8},{12,14},{14,12},{16,18},{18,... | collective-permute-start | bytes 417800 | tf_op jit(solution)/shard_map/ppermute | solution.py:267
  21.7 9.2 %collective-permute-start.7 = (bf16[32,2048]{1,0:T(8,128)(2,1)S(1)}, bf16[32,2048]{1,0:T(8,128)(2,1)S(1)}, u32[]{:S(2)}, u32[]{:S(2)}) collective-permute-start(bf16[32,2048]{1,0:T(8,128)(2,1)S(1)} %get-tuple-element.29.refs_1_.at_end.at_mid), channel_id=1, source_target_pairs={{0,8},{2,4},{4,2},{6,14},{8,0},{10,12},{12,10},{14,6},{16,24},{18,... | collective-permute-start | bytes 393224 | tf_op jit(solution)/shard_map/ppermute | solution.py:270
  24.9 6.0 %collective-permute-start.10 = (bf16[32,2048]{1,0:T(8,128)(2,1)S(1)}, bf16[32,2048]{1,0:T(8,128)(2,1)S(1)}, u32[]{:S(2)}, u32[]{:S(2)}) collective-permute-start(bf16[32,2048]{1,0:T(8,128)(2,1)S(1)} %get-tuple-element.31.refs_3_.at_end.at_mid), channel_id=1, source_target_pairs={{0,8},{2,4},{4,2},{6,14},{8,0},{10,12},{12,10},{14,6},{16,24},{18,... | collective-permute-start | bytes 393224 | tf_op jit(solution)/shard_map/ppermute | solution.py:270
  27.4 6.2 %collective-permute-start.17 = (bf16[32,2048]{1,0:T(8,128)(2,1)S(1)}, bf16[32,2048]{1,0:T(8,128)(2,1)S(1)}, u32[]{:S(2)}, u32[]{:S(2)}) collective-permute-start(bf16[32,2048]{1,0:T(8,128)(2,1)S(1)} %choose.16), channel_id=1, source_target_pairs={{0,2},{2,0},{4,6},{6,4},{8,10},{10,8},{12,14},{14,12},{16,18},{18,... | collective-permute-start | bytes 393224 | tf_op jit(solution)/shard_map/ppermute | solution.py:267
  27.4 8.9 %collective-permute-start.22 = (bf16[32,2048]{1,0:T(8,128)(2,1)S(1)}, bf16[32,2048]{1,0:T(8,128)(2,1)S(1)}, u32[]{:S(2)}, u32[]{:S(2)}) collective-permute-start(bf16[32,2048]{1,0:T(8,128)(2,1)S(1)} %choose.17), channel_id=1, source_target_pairs={{0,2},{2,0},{4,6},{6,4},{8,10},{10,8},{12,14},{14,12},{16,18},{18,... | collective-permute-start | bytes 393224 | tf_op jit(solution)/shard_map/ppermute | solution.py:267
  30.8 7.1 %collective-permute-start.8 = (bf16[32,2048]{1,0:T(8,128)(2,1)S(1)}, bf16[32,2048]{1,0:T(8,128)(2,1)S(1)}, u32[]{:S(2)}, u32[]{:S(2)}) collective-permute-start(bf16[32,2048]{1,0:T(8,128)(2,1)S(1)} %choose.12), channel_id=1, source_target_pairs={{0,2},{2,0},{4,6},{6,4},{8,10},{10,8},{12,14},{14,12},{16,18},{18,... | collective-permute-start | bytes 393224 | tf_op jit(solution)/shard_map/ppermute | solution.py:267
  31.0 9.1 %collective-permute-start.11 = (bf16[32,2048]{1,0:T(8,128)(2,1)S(1)}, bf16[32,2048]{1,0:T(8,128)(2,1)S(1)}, u32[]{:S(2)}, u32[]{:S(2)}) collective-permute-start(bf16[32,2048]{1,0:T(8,128)(2,1)S(1)} %choose.14), channel_id=1, source_target_pairs={{0,2},{2,0},{4,6},{6,4},{8,10},{10,8},{12,14},{14,12},{16,18},{18,... | collective-permute-start | bytes 393224 | tf_op jit(solution)/shard_map/ppermute | solution.py:267
  37.7 6.4 %collective-permute-start.24 = (bf16[32,2048]{1,0:T(8,128)(2,1)S(1)}, bf16[32,2048]{1,0:T(8,128)(2,1)S(1)}, u32[]{:S(2)}, u32[]{:S(2)}) collective-permute-start(bf16[32,2048]{1,0:T(8,128)(2,1)S(1)} %choose.18), channel_id=1, source_target_pairs={{0,2},{2,0},{4,6},{6,4},{8,10},{10,8},{12,14},{14,12},{16,18},{18,... | collective-permute-start | bytes 393224 | tf_op jit(solution)/shard_map/ppermute | solution.py:267
  38.0 9.5 %collective-permute-start.14 = (bf16[32,2048]{1,0:T(8,128)(2,1)S(1)}, bf16[32,2048]{1,0:T(8,128)(2,1)S(1)}, u32[]{:S(2)}, u32[]{:S(2)}) collective-permute-start(bf16[32,2048]{1,0:T(8,128)(2,1)S(1)} %add.8), channel_id=1, source_target_pairs={{0,8},{2,4},{4,2},{6,14},{8,0},{10,12},{12,10},{14,6},{16,24},{18,... | collective-permute-start | bytes 393224 | tf_op jit(solution)/shard_map/ppermute | solution.py:270
  40.0 7.7 %collective-permute-start.25 = (bf16[32,2048]{1,0:T(8,128)(2,1)S(1)}, bf16[32,2048]{1,0:T(8,128)(2,1)S(1)}, u32[]{:S(2)}, u32[]{:S(2)}) collective-permute-start(bf16[32,2048]{1,0:T(8,128)(2,1)S(1)} %choose.19), channel_id=1, source_target_pairs={{0,2},{2,0},{4,6},{6,4},{8,10},{10,8},{12,14},{14,12},{16,18},{18,... | collective-permute-start | bytes 393224 | tf_op jit(solution)/shard_map/ppermute | solution.py:267
  40.2 7.7 %collective-permute-start.19 = (bf16[32,2048]{1,0:T(8,128)(2,1)S(1)}, bf16[32,2048]{1,0:T(8,128)(2,1)S(1)}, u32[]{:S(2)}, u32[]{:S(2)}) collective-permute-start(bf16[32,2048]{1,0:T(8,128)(2,1)S(1)} %add.10), channel_id=1, source_target_pairs={{0,8},{2,4},{4,2},{6,14},{8,0},{10,12},{12,10},{14,6},{16,24},{18,... | collective-permute-start | bytes 393224 | tf_op jit(solution)/shard_map/ppermute | solution.py:270
  47.6 6.4 %collective-permute-start.15 = (bf16[32,2048]{1,0:T(8,128)(2,1)S(1)}, bf16[32,2048]{1,0:T(8,128)(2,1)S(1)}, u32[]{:S(2)}, u32[]{:S(2)}) collective-permute-start(bf16[32,2048]{1,0:T(8,128)(2,1)S(1)} %choose_sum.4), channel_id=1, source_target_pairs={{0,2},{2,0},{4,6},{6,4},{8,10},{10,8},{12,14},{14,12},{16,18},{18,... | collective-permute-start | bytes 393224 | tf_op jit(solution)/shard_map/ppermute | solution.py:267
  47.7 6.3 %collective-permute-start.29 = (bf16[32,2048]{1,0:T(8,128)(2,1)S(1)}, bf16[32,2048]{1,0:T(8,128)(2,1)S(1)}, u32[]{:S(2)}, u32[]{:S(2)}) collective-permute-start(bf16[32,2048]{1,0:T(8,128)(2,1)S(1)} %add.14), channel_id=1, source_target_pairs={{0,8},{2,4},{4,2},{6,14},{8,0},{10,12},{12,10},{14,6},{16,24},{18,... | collective-permute-start | bytes 393224 | tf_op jit(solution)/shard_map/ppermute | solution.py:270
  47.9 7.6 %collective-permute-start.20 = (bf16[32,2048]{1,0:T(8,128)(2,1)S(1)}, bf16[32,2048]{1,0:T(8,128)(2,1)S(1)}, u32[]{:S(2)}, u32[]{:S(2)}) collective-permute-start(bf16[32,2048]{1,0:T(8,128)(2,1)S(1)} %choose_sum.5), channel_id=1, source_target_pairs={{0,2},{2,0},{4,6},{6,4},{8,10},{10,8},{12,14},{14,12},{16,18},{18,... | collective-permute-start | bytes 393224 | tf_op jit(solution)/shard_map/ppermute | solution.py:267
  50.0 6.4 %collective-permute-start.18 = (bf16[32,2048]{1,0:T(8,128)(2,1)S(1)}, bf16[32,2048]{1,0:T(8,128)(2,1)S(1)}, u32[]{:S(2)}, u32[]{:S(2)}) collective-permute-start(bf16[32,2048]{1,0:T(8,128)(2,1)S(1)} %add.9), channel_id=1, source_target_pairs={{0,8},{2,4},{4,2},{6,14},{8,0},{10,12},{12,10},{14,6},{16,24},{18,... | collective-permute-start | bytes 393224 | tf_op jit(solution)/shard_map/ppermute | solution.py:270
  50.1 9.1 %collective-permute-start.23 = (bf16[32,2048]{1,0:T(8,128)(2,1)S(1)}, bf16[32,2048]{1,0:T(8,128)(2,1)S(1)}, u32[]{:S(2)}, u32[]{:S(2)}) collective-permute-start(bf16[32,2048]{1,0:T(8,128)(2,1)S(1)} %add.11), channel_id=1, source_target_pairs={{0,8},{2,4},{4,2},{6,14},{8,0},{10,12},{12,10},{14,6},{16,24},{18,... | collective-permute-start | bytes 393224 | tf_op jit(solution)/shard_map/ppermute | solution.py:270
  54.0 6.3 %collective-permute-start.27 = (bf16[32,2048]{1,0:T(8,128)(2,1)S(1)}, bf16[32,2048]{1,0:T(8,128)(2,1)S(1)}, u32[]{:S(2)}, u32[]{:S(2)}) collective-permute-start(bf16[32,2048]{1,0:T(8,128)(2,1)S(1)} %choose_sum.6), channel_id=1, source_target_pairs={{0,2},{2,0},{4,6},{6,4},{8,10},{10,8},{12,14},{14,12},{16,18},{18,... | collective-permute-start | bytes 393224 | tf_op jit(solution)/shard_map/ppermute | solution.py:267
  54.0 7.9 %collective-permute-start.28 = (bf16[32,2048]{1,0:T(8,128)(2,1)S(1)}, bf16[32,2048]{1,0:T(8,128)(2,1)S(1)}, u32[]{:S(2)}, u32[]{:S(2)}) collective-permute-start(bf16[32,2048]{1,0:T(8,128)(2,1)S(1)} %add.13), channel_id=1, source_target_pairs={{0,8},{2,4},{4,2},{6,14},{8,0},{10,12},{12,10},{14,6},{16,24},{18,... | collective-permute-start | bytes 393224 | tf_op jit(solution)/shard_map/ppermute | solution.py:270
  55.4 6.7 %collective-permute-start.30 = (bf16[32,2048]{1,0:T(8,128)(2,1)S(1)}, bf16[32,2048]{1,0:T(8,128)(2,1)S(1)}, u32[]{:S(2)}, u32[]{:S(2)}) collective-permute-start(bf16[32,2048]{1,0:T(8,128)(2,1)S(1)} %choose_sum.7), channel_id=1, source_target_pairs={{0,2},{2,0},{4,6},{6,4},{8,10},{10,8},{12,14},{14,12},{16,18},{18,... | collective-permute-start | bytes 393224 | tf_op jit(solution)/shard_map/ppermute | solution.py:267
  56.4 7.7 %collective-permute-start.31 = (bf16[32,2048]{1,0:T(8,128)(2,1)S(1)}, bf16[32,2048]{1,0:T(8,128)(2,1)S(1)}, u32[]{:S(2)}, u32[]{:S(2)}) collective-permute-start(bf16[32,2048]{1,0:T(8,128)(2,1)S(1)} %add.15), channel_id=1, source_target_pairs={{0,8},{2,4},{4,2},{6,14},{8,0},{10,12},{12,10},{14,6},{16,24},{18,... | collective-permute-start | bytes 393224 | tf_op jit(solution)/shard_map/ppermute | solution.py:270
  59.3 9.3 %collective-permute-start.32 = (bf16[64,2048]{1,0:T(8,128)(2,1)S(1)}, bf16[64,2048]{1,0:T(8,128)(2,1)S(1)}, u32[]{:S(2)}, u32[]{:S(2)}) collective-permute-start(bf16[64,2048]{1,0:T(8,128)(2,1)S(1)} %finish_first.1.firsts), channel_id=1, source_target_pairs={{0,8},{8,16},{16,24},{24,0},{1,9},{9,17},{17,25},{25,1},{2,10},{10... | collective-permute-start | bytes 786440 | tf_op jit(solution)/shard_map/ppermute | solution.py:368
  (3 other events, 14.9 us)

commit v5 on v4

--- a/solution.py
+++ b/solution.py
@@ -142,27 +142,22 @@
 
 
 def own_pass(*refs):
-    pieces, refs = refs[: 2 * STREAMS], refs[2 * STREAMS :]
-    from_hbm, (gate_w, up_w, down_w), total, sems = refs[:3], refs[3:6], refs[6], refs[7]
-    copies = [
-        pltpu.make_async_copy(source, target, sems.at[i])
-        for i, (source, target) in enumerate(zip(from_hbm, (gate_w, up_w, down_w)))
-    ]
-    for copy in copies:
-        copy.start()
+    pieces, (gate_w, up_w, down_w, total) = refs[: 2 * STREAMS], refs[2 * STREAMS :]
     width = total.shape[1]
     rows = jnp.concatenate([piece[:, :width] for piece in pieces], axis=0)
     weight = jnp.concatenate(
         [weight_of(pieces[i // 2 * 2][:, width:], i % 2) for i in range(2 * STREAMS)], axis=0
     )
-    copies[0].wait()
-    gate = jnp.dot(rows, gate_w[...], preferred_element_type=jnp.float32)
-    copies[1].wait()
-    up = jnp.dot(rows, up_w[...], preferred_element_type=jnp.float32)
-    hidden = narrow(gate / (1.0 + jnp.exp(-gate)) * up)
-    copies[2].wait()
-    out = jnp.dot(hidden, down_w[...], preferred_element_type=jnp.float32)
-    total[...] = rows.astype(jnp.float32) + narrow(out).astype(jnp.float32) * weight
+    total[...] = rows.astype(jnp.float32) + expert_of(rows, gate_w, up_w, down_w) * weight
+
+
+def load(*refs):
+    sems = refs[6]
+    copies = [pltpu.make_async_copy(refs[i], refs[3 + i], sems.at[i]) for i in range(3)]
+    for copy in copies:
+        copy.start()
+    for copy in copies:
+        copy.wait()
 
 
 def pass_of(late):
@@ -288,23 +283,22 @@
     o, i, p = [[None] * 8 for _ in both], [[None] * 8 for _ in both], [None] * 8
 
     def swap(k, s, to_outer, to_inner):
+        if 5 <= k <= 7:
+            i[s][k - 1], to_inner = lax.optimization_barrier((i[s][k - 1], to_inner))
         o[s][k], i[s][k] = outer(to_outer), inner(to_inner)
 
     for s in both:
         swap(0, s, first[s], first[s])
-    *weights, total = run(
-        own_pass,
-        "own_pass",
-        [held(w.shape) for w in weights] + [held((count, width), jnp.float32)],
-        *pieces,
+    weights = run(
+        load,
+        "load",
+        [held(w.shape) for w in weights],
         *weights,
         scratch=[pltpu.SemaphoreType.DMA((3,))],
-        specs=[IN_VMEM] * len(pieces) + [ANYWHERE] * 3,
-        work=(6 * count * weights[0].size, 6 * weights[0].size),
-    )
-    o[0][0], i[0][0], total, *weights = lax.optimization_barrier(
-        (o[0][0], i[0][0], total, *weights)
-    )
+        specs=[ANYWHERE] * 3,
+        work=(0, 6 * weights[0].size),
+    )
+    i[0][0], *weights = lax.optimization_barrier((i[0][0], *weights))
 
     def expert(late, given):
         return run(
@@ -325,6 +319,15 @@
     for s in both:
         swap(2, s, mixed(choose, p[1][s], i[s][1], shape=tagged), o[s][1])
     p[2] = expert(False, lambda s: (o[s][1], i[s][0]) * 2)
+    total = run(
+        own_pass,
+        "own_pass",
+        held((count, width), jnp.float32),
+        *pieces,
+        *weights,
+        work=(6 * count * weights[0].size, 6 * weights[0].size),
+    )
+    o[0][2], i[0][2], total = lax.optimization_barrier((o[0][2], i[0][2], total))
     for s in both:
         swap(3, s, mixed(choose, p[2][s], i[s][2]), second[s])
     p[3] = expert(False, lambda s: (o[s][2], i[s][1]) * 2)

time: 69.6 us -> 64.8 us (0.931); the launches traced: 69.4 us -> 63.7 us
  waiting for transfers between devices: 22.8 us -> 17.7 us
  starting transfers between devices: 30.9 us -> 29.7 us
  Pallas kernels: 14.7 us -> 15.4 us
    ppermute x16, waiting for transfers between devices: 9.91 us -> 5.66 us  [inner(): return lax.ppermute(value, axes, inner_pairs)]
    ppermute x16, starting transfers between devices: 21.1 us -> 19.4 us  [inner(): return lax.ppermute(value, axes, inner_pairs)]
    ppermute x16, waiting for transfers between devices: 9.36 us -> 8.47 us  [outer(): return lax.ppermute(value, axes, outer_pairs)]
    pallas_call x35 -> x36, Pallas kernels: 14.7 us -> 15.4 us  [run(): pl.pallas_call(body, out_shape=out_shape, in_specs=specs, out_specs=out_s...]
  transfers between devices with their start and end apart: 35 -> 35, of which waited for: 18 -> 19; matrix products, arithmetic and copies ran while one was open for 0% -> 0% of each run, Pallas kernels for 18% -> 21%
where the time goes in v5:
time: 64.8 us; the launch traced here: 63.7 us
  starting transfers between devices  29.7 us (46%)
  waiting for transfers between devices  17.7 us (27%)
  Pallas kernels  15.4 us (24%)
  between operations  0.97 us (1%)
    ppermute x16, starting transfers between devices, inner(): return lax.ppermute(value, axes, inner_pairs)  19.4 us
    pallas_call x36, Pallas kernels, run(): pl.pallas_call(body, out_shape=out_shape, in_specs=specs, out_specs=out_s...  15.4 us
    ppermute x16, starting transfers between devices, outer(): return lax.ppermute(value, axes, outer_pairs)  10.1 us
    ppermute x16, waiting for transfers between devices, outer(): return lax.ppermute(value, axes, outer_pairs)  8.47 us
    ppermute x16, waiting for transfers between devices, inner(): return lax.ppermute(value, axes, inner_pairs)  5.66 us
    ppermute x3, waiting for transfers between devices, on_line(): handed = [lax.ppermute(part, 'section', ring) for part in parts]  3.55 us
  transfers between devices with their start and end apart: 35, of which 19 were waited for; matrix products, arithmetic and copies ran while one was open for 0% of the time, Pallas kernels for 21%

profile of v5, /device:TPU:12, one launch (start us, length us, event | category | flops | bytes accessed | tf_op | source)
XLA Modules:
  0.0 63.7 jit_solution(18128313769319237472)
XLA Ops:
  0.6 1.2 %prepare.1 = (bf16[32,2176]{1,0:T(8,128)(2,1)S(1)}, bf16[32,2048]{1,0:T(8,128)(2,1)S(1)}, bf16[32,2176]{1,0:T(8,128)(2,1)S(1)}, bf16[32,2048]{1,0:T(8,128)(2,1)S(1)}) custom-call(bf16[128,2048]{1,0:T(8,128)(2,1)} %bitcast.15, s32[2,128]{1,0:T(2,128)} %bitcast.18, f32[2,128]{1,0:T(2,128)} %bitcast.19), custom_call_target="tpu_custom_call" | custom-call | tf_op jit(solution)/shard_map/prepare/pallas_call | solution.py:87
  1.8 1.6 %collective-permute-start.2 = (bf16[32,2176]{1,0:T(8,128)(2,1)S(1)}, bf16[32,2176]{1,0:T(8,128)(2,1)S(1)}, u32[]{:S(2)}, u32[]{:S(2)}) collective-permute-start(bf16[32,2176]{1,0:T(8,128)(2,1)S(1)} %get-tuple-element.36.refs_0_), channel_id=1, source_target_pairs={{0,8},{2,4},{4,2},{6,14},{8,0},{10,12},{12,10},{14,6},{16,24},{18,... | collective-permute-start | bytes 417800 | tf_op jit(solution)/shard_map/ppermute | solution.py:265
  3.5 1.7 %collective-permute-start.13 = (bf16[32,2176]{1,0:T(8,128)(2,1)S(1)}, bf16[32,2176]{1,0:T(8,128)(2,1)S(1)}, u32[]{:S(2)}, u32[]{:S(2)}) collective-permute-start(bf16[32,2176]{1,0:T(8,128)(2,1)S(1)} %get-tuple-element.37.refs_2_), channel_id=1, source_target_pairs={{0,8},{2,4},{4,2},{6,14},{8,0},{10,12},{12,10},{14,6},{16,24},{18,... | collective-permute-start | bytes 417800 | tf_op jit(solution)/shard_map/ppermute | solution.py:265
  5.5 2.9 %load.1 = (bf16[2048,512]{1,0:T(8,128)(2,1)S(1)}, bf16[2048,512]{1,0:T(8,128)(2,1)S(1)}, bf16[512,2048]{1,0:T(8,128)(2,1)S(1)}) custom-call(bf16[2048,512]{1,0:T(8,128)(2,1)} %bitcast.12, bf16[2048,512]{1,0:T(8,128)(2,1)} %bitcast.13, bf16[512,2048]{1,0:T(8,128)(2,1)} %bitcast.14), custom_call_target="tpu_custom_call" | custom-call | bytes 6291456 | tf_op jit(solution)/shard_map/load/pallas_call | solution.py:87
  8.4 1.2 %collective-permute-done.refs_0_.refs_1_.refs_2_.refs_3_ = bf16[32,2176]{1,0:T(8,128)(2,1)S(1)} collective-permute-done((bf16[32,2176]{1,0:T(8,128)(2,1)S(1)}, bf16[32,2176]{1,0:T(8,128)(2,1)S(1)}, u32[]{:S(2)}, u32[]{:S(2)}) %collective-permute-start) | collective-permute-done | bytes 139296 | tf_op jit(solution)/shard_map/ppermute | solution.py:262
  10.6 2.1 %collective-permute-start.14 = (bf16[32,2176]{1,0:T(8,128)(2,1)S(1)}, bf16[32,2176]{1,0:T(8,128)(2,1)S(1)}, u32[]{:S(2)}, u32[]{:S(2)}) collective-permute-start(bf16[32,2176]{1,0:T(8,128)(2,1)S(1)} %choose.15), channel_id=1, source_target_pairs={{0,2},{2,0},{4,6},{6,4},{8,10},{10,8},{12,14},{14,12},{16,18},{18,... | collective-permute-start | bytes 417800 | tf_op jit(solution)/shard_map/ppermute | solution.py:262
  12.7 1.2 %collective-permute-start.7 = (bf16[32,2176]{1,0:T(8,128)(2,1)S(1)}, bf16[32,2176]{1,0:T(8,128)(2,1)S(1)}, u32[]{:S(2)}, u32[]{:S(2)}) collective-permute-start(bf16[32,2176]{1,0:T(8,128)(2,1)S(1)} %collective-permute-done.1.refs_4_.refs_5_.refs_6_.refs_7_), channel_id=1, source_target_pairs={{0,8},{2,4},{4,2},{6,14},{8,0},{10,12},{12,10},{14,6},{16,24},{18,... | collective-permute-start | bytes 417800 | tf_op jit(solution)/shard_map/ppermute | solution.py:265
  13.9 1.3 %expert_pass.6 = (bf16[32,2048]{1,0:T(8,128)(2,1)S(1)}, bf16[32,2048]{1,0:T(8,128)(2,1)S(1)}) custom-call(bf16[32,2176]{1,0:T(8,128)(2,1)S(1)} %collective-permute-done.refs_0_.refs_1_.refs_2_.refs_3_, bf16[32,2176]{1,0:T(8,128)(2,1)S(1)} %collective-permute-done.refs_0_.refs_1_.refs_2_.refs_3_, ...), custom_call_target="tpu_custom_call" | custom-call | flops 402653184 | bytes 6291456 | tf_op jit(solution)/shard_map/expert_pass/pallas_call | solution.py:87
  15.2 1.0 %collective-permute-done.3.at_mid.refs_1_.refs_3_ = bf16[32,2176]{1,0:T(8,128)(2,1)S(1)} collective-permute-done((bf16[32,2176]{1,0:T(8,128)(2,1)S(1)}, bf16[32,2176]{1,0:T(8,128)(2,1)S(1)}, u32[]{:S(2)}, u32[]{:S(2)}) %collective-permute-start.3) | collective-permute-done | bytes 139296 | tf_op jit(solution)/shard_map/ppermute | solution.py:265
  16.4 1.9 %collective-permute-start.6 = (bf16[32,2176]{1,0:T(8,128)(2,1)S(1)}, bf16[32,2176]{1,0:T(8,128)(2,1)S(1)}, u32[]{:S(2)}, u32[]{:S(2)}) collective-permute-start(bf16[32,2176]{1,0:T(8,128)(2,1)S(1)} %collective-permute-done.5.refs_2_.refs_0_.refs_1_), channel_id=1, source_target_pairs={{0,8},{2,4},{4,2},{6,14},{8,0},{10,12},{12,10},{14,6},{16,24},{18,... | collective-permute-start | bytes 417800 | tf_op jit(solution)/shard_map/ppermute | solution.py:265
  19.1 1.5 %collective-permute-start.19 = (bf16[32,2176]{1,0:T(8,128)(2,1)S(1)}, bf16[32,2176]{1,0:T(8,128)(2,1)S(1)}, u32[]{:S(2)}, u32[]{:S(2)}) collective-permute-start(bf16[32,2176]{1,0:T(8,128)(2,1)S(1)} %collective-permute-done.14.refs_6_.refs_4_.refs_5_), channel_id=1, source_target_pairs={{0,8},{2,4},{4,2},{6,14},{8,0},{10,12},{12,10},{14,6},{16,24},{18,... | collective-permute-start | bytes 417800 | tf_op jit(solution)/shard_map/ppermute | solution.py:265
  21.2 1.1 %own_pass.1.total = f32[128,2048]{1,0:T(8,128)S(1)} custom-call(bf16[32,2176]{1,0:T(8,128)(2,1)S(1)} %get-tuple-element.36.refs_0_, bf16[32,2048]{1,0:T(8,128)(2,1)S(1)} %get-tuple-element.45.at_end.refs_1_.at_mid, bf16[32,2176]{1,0:T(8,128)(2,1)S(1)} %get-tuple-element.37.refs_2_, bf16[32,2048]{1,0:T(8,128)(2,1)S(1)} %get-tuple-element.47.refs_3_.at_end.at_mid, ...), custom_call_target="tpu_custom_call" | custom-call | flops 805306368 | bytes 6291456 | tf_op jit(solution)/shard_map/own_pass/pallas_call | solution.py:87
  22.4 1.3 %expert_pass.9 = (bf16[32,2048]{1,0:T(8,128)(2,1)S(1)}, bf16[32,2048]{1,0:T(8,128)(2,1)S(1)}) custom-call(bf16[32,2176]{1,0:T(8,128)(2,1)S(1)} %collective-permute-done.5.refs_2_.refs_0_.refs_1_, bf16[32,2176]{1,0:T(8,128)(2,1)S(1)} %collective-permute-done.2.at_mid.refs_3_.refs_1_, bf16[32,2176]{1,0:T(8,128)(2,1)S(1)} %collective-permute-done.5.refs_2_.refs_0_.refs_1_, ...), custom_call_target="tpu_custom_call" | custom-call | flops 402653184 | bytes 6291456 | tf_op jit(solution)/shard_map/expert_pass/pallas_call | solution.py:87
  23.7 2.1 %collective-permute-start.15 = (bf16[32,2048]{1,0:T(8,128)(2,1)S(1)}, bf16[32,2048]{1,0:T(8,128)(2,1)S(1)}, u32[]{:S(2)}, u32[]{:S(2)}) collective-permute-start(bf16[32,2048]{1,0:T(8,128)(2,1)S(1)} %choose.16), channel_id=1, source_target_pairs={{0,2},{2,0},{4,6},{6,4},{8,10},{10,8},{12,14},{14,12},{16,18},{18,... | collective-permute-start | bytes 393224 | tf_op jit(solution)/shard_map/ppermute | solution.py:262
  25.8 1.5 %collective-permute-start.11 = (bf16[32,2048]{1,0:T(8,128)(2,1)S(1)}, bf16[32,2048]{1,0:T(8,128)(2,1)S(1)}, u32[]{:S(2)}, u32[]{:S(2)}) collective-permute-start(bf16[32,2048]{1,0:T(8,128)(2,1)S(1)} %get-tuple-element.47.refs_3_.at_end.at_mid), channel_id=1, source_target_pairs={{0,8},{2,4},{4,2},{6,14},{8,0},{10,12},{12,10},{14,6},{16,24},{18,... | collective-permute-start | bytes 393224 | tf_op jit(solution)/shard_map/ppermute | solution.py:265
  27.4 1.3 %expert_pass.7 = (bf16[32,2048]{1,0:T(8,128)(2,1)S(1)}, bf16[32,2048]{1,0:T(8,128)(2,1)S(1)}) custom-call(bf16[32,2176]{1,0:T(8,128)(2,1)S(1)} %collective-permute-done.4.refs_0_.refs_2_.refs_1_, bf16[32,2176]{1,0:T(8,128)(2,1)S(1)} %collective-permute-done.3.at_mid.refs_1_.refs_3_, bf16[32,2176]{1,0:T(8,128)(2,1)S(1)} %collective-permute-done.4.refs_0_.refs_2_.refs_1_, ...), custom_call_target="tpu_custom_call" | custom-call | flops 402653184 | bytes 6291456 | tf_op jit(solution)/shard_map/expert_pass/pallas_call | solution.py:87
  28.7 2.1 %collective-permute-start.10 = (bf16[32,2048]{1,0:T(8,128)(2,1)S(1)}, bf16[32,2048]{1,0:T(8,128)(2,1)S(1)}, u32[]{:S(2)}, u32[]{:S(2)}) collective-permute-start(bf16[32,2048]{1,0:T(8,128)(2,1)S(1)} %choose.13), channel_id=1, source_target_pairs={{0,2},{2,0},{4,6},{6,4},{8,10},{10,8},{12,14},{14,12},{16,18},{18,... | collective-permute-start | bytes 393224 | tf_op jit(solution)/shard_map/ppermute | solution.py:262
  30.9 1.0 %collective-permute-start.16 = (bf16[32,2048]{1,0:T(8,128)(2,1)S(1)}, bf16[32,2048]{1,0:T(8,128)(2,1)S(1)}, u32[]{:S(2)}, u32[]{:S(2)}) collective-permute-start(bf16[32,2048]{1,0:T(8,128)(2,1)S(1)} %add.8), channel_id=1, source_target_pairs={{0,8},{2,4},{4,2},{6,14},{8,0},{10,12},{12,10},{14,6},{16,24},{18,... | collective-permute-start | bytes 393224 | tf_op jit(solution)/shard_map/ppermute | solution.py:265
  33.3 1.3 %collective-permute-start.21 = (bf16[32,2048]{1,0:T(8,128)(2,1)S(1)}, bf16[32,2048]{1,0:T(8,128)(2,1)S(1)}, u32[]{:S(2)}, u32[]{:S(2)}) collective-permute-start(bf16[32,2048]{1,0:T(8,128)(2,1)S(1)} %add.10), channel_id=1, source_target_pairs={{0,8},{2,4},{4,2},{6,14},{8,0},{10,12},{12,10},{14,6},{16,24},{18,... | collective-permute-start | bytes 393224 | tf_op jit(solution)/shard_map/ppermute | solution.py:265
  34.6 1.3 %expert_pass.10 = (bf16[32,2048]{1,0:T(8,128)(2,1)S(1)}, bf16[32,2048]{1,0:T(8,128)(2,1)S(1)}) custom-call(bf16[32,2048]{1,0:T(8,128)(2,1)S(1)} %collective-permute-done.15.a.refs_0_, bf16[32,2176]{1,0:T(8,128)(2,1)S(1)} %collective-permute-done.6.at_mid.refs_1_, bf16[32,2176]{1,0:T(8,128)(2,1)S(1)} %collective-permute-done.4.refs_0_.refs_2_.refs_1_, ...), custom_call_target="tpu_custom_call" | custom-call | flops 402653184 | bytes 6291456 | tf_op jit(solution)/shard_map/expert_pass/pallas_call | solution.py:87
  36.5 1.3 %collective-permute-start.17 = (bf16[32,2048]{1,0:T(8,128)(2,1)S(1)}, bf16[32,2048]{1,0:T(8,128)(2,1)S(1)}, u32[]{:S(2)}, u32[]{:S(2)}) collective-permute-start(bf16[32,2048]{1,0:T(8,128)(2,1)S(1)} %add.9), channel_id=1, source_target_pairs={{0,8},{2,4},{4,2},{6,14},{8,0},{10,12},{12,10},{14,6},{16,24},{18,... | collective-permute-start | bytes 393224 | tf_op jit(solution)/shard_map/ppermute | solution.py:265
  39.6 1.3 %expert_pass.8 = (bf16[32,2048]{1,0:T(8,128)(2,1)S(1)}, bf16[32,2048]{1,0:T(8,128)(2,1)S(1)}) custom-call(bf16[32,2048]{1,0:T(8,128)(2,1)S(1)} %collective-permute-done.10.refs_0_.a, bf16[32,2048]{1,0:T(8,128)(2,1)S(1)} %collective-permute-done.9.at_mid.refs_1_, bf16[32,2176]{1,0:T(8,128)(2,1)S(1)} %collective-permute-done.5.refs_2_.refs_0_.refs_1_, ...), custom_call_target="tpu_custom_call" | custom-call | flops 402653184 | bytes 6291456 | tf_op jit(solution)/shard_map/expert_pass/pallas_call | solution.py:87
  41.6 1.1 %collective-permute-done.17.mid_a = bf16[32,2048]{1,0:T(8,128)(2,1)S(1)} collective-permute-done((bf16[32,2048]{1,0:T(8,128)(2,1)S(1)}, bf16[32,2048]{1,0:T(8,128)(2,1)S(1)}, u32[]{:S(2)}, u32[]{:S(2)}) %collective-permute-start.17) | collective-permute-done | bytes 131104 | tf_op jit(solution)/shard_map/ppermute | solution.py:265
  42.7 1.5 %collective-permute-start.26 = (bf16[32,2048]{1,0:T(8,128)(2,1)S(1)}, bf16[32,2048]{1,0:T(8,128)(2,1)S(1)}, u32[]{:S(2)}, u32[]{:S(2)}) collective-permute-start(bf16[32,2048]{1,0:T(8,128)(2,1)S(1)} %add.12), channel_id=1, source_target_pairs={{0,8},{2,4},{4,2},{6,14},{8,0},{10,12},{12,10},{14,6},{16,24},{18,... | collective-permute-start | bytes 393224 | tf_op jit(solution)/shard_map/ppermute | solution.py:265
  44.3 1.2 %collective-permute-done.22.mid_a = bf16[32,2048]{1,0:T(8,128)(2,1)S(1)} collective-permute-done((bf16[32,2048]{1,0:T(8,128)(2,1)S(1)}, bf16[32,2048]{1,0:T(8,128)(2,1)S(1)}, u32[]{:S(2)}, u32[]{:S(2)}) %collective-permute-start.22) | collective-permute-done | bytes 131104 | tf_op jit(solution)/shard_map/ppermute | solution.py:265
  45.5 1.5 %collective-permute-start.29 = (bf16[32,2048]{1,0:T(8,128)(2,1)S(1)}, bf16[32,2048]{1,0:T(8,128)(2,1)S(1)}, u32[]{:S(2)}, u32[]{:S(2)}) collective-permute-start(bf16[32,2048]{1,0:T(8,128)(2,1)S(1)} %add.14), channel_id=1, source_target_pairs={{0,8},{2,4},{4,2},{6,14},{8,0},{10,12},{12,10},{14,6},{16,24},{18,... | collective-permute-start | bytes 393224 | tf_op jit(solution)/shard_map/ppermute | solution.py:265
  47.1 1.3 %expert_pass.11 = (bf16[32,2048]{1,0:T(8,128)(2,1)S(1)}, bf16[32,2048]{1,0:T(8,128)(2,1)S(1)}) custom-call(bf16[32,2048]{1,0:T(8,128)(2,1)S(1)} %collective-permute-done.24.refs_0_.a, bf16[32,2176]{1,0:T(8,128)(2,1)S(1)} %collective-permute-done.5.refs_2_.refs_0_.refs_1_, bf16[32,2176]{1,0:T(8,128)(2,1)S(1)} %collective-permute-done.refs_0_.refs_1_.refs_2_.refs_3_, ...), custom_call_target="tpu_custom_call" | custom-call | flops 402653184 | bytes 6291456 | tf_op jit(solution)/shard_map/expert_pass/pallas_call | solution.py:87
  48.7 1.8 %collective-permute-start.27 = (bf16[32,2048]{1,0:T(8,128)(2,1)S(1)}, bf16[32,2048]{1,0:T(8,128)(2,1)S(1)}, u32[]{:S(2)}, u32[]{:S(2)}) collective-permute-start(bf16[32,2048]{1,0:T(8,128)(2,1)S(1)} %choose_sum.6), channel_id=1, source_target_pairs={{0,2},{2,0},{4,6},{6,4},{8,10},{10,8},{12,14},{14,12},{16,18},{18,... | collective-permute-start | bytes 393224 | tf_op jit(solution)/shard_map/ppermute | solution.py:262
  51.3 2.0 %collective-permute-done.23.refs_3_.a = bf16[32,2048]{1,0:T(8,128)(2,1)S(1)} collective-permute-done((bf16[32,2048]{1,0:T(8,128)(2,1)S(1)}, bf16[32,2048]{1,0:T(8,128)(2,1)S(1)}, u32[]{:S(2)}, u32[]{:S(2)}) %collective-permute-start.23) | collective-permute-done | bytes 131104 | tf_op jit(solution)/shard_map/ppermute | solution.py:262
  54.2 1.9 %collective-permute-done.27.outer = bf16[32,2048]{1,0:T(8,128)(2,1)S(1)} collective-permute-done((bf16[32,2048]{1,0:T(8,128)(2,1)S(1)}, bf16[32,2048]{1,0:T(8,128)(2,1)S(1)}, u32[]{:S(2)}, u32[]{:S(2)}) %collective-permute-start.27) | collective-permute-done | bytes 131104 | tf_op jit(solution)/shard_map/ppermute | solution.py:262
  59.4 2.0 %collective-permute-done.33.refs_1_ = bf16[32,2048]{1,0:T(8,128)(2,1)S(1)} collective-permute-done((bf16[32,2048]{1,0:T(8,128)(2,1)S(1)}, bf16[32,2048]{1,0:T(8,128)(2,1)S(1)}, u32[]{:S(2)}, u32[]{:S(2)}) %collective-permute-start.33) | collective-permute-done | bytes 131104 | tf_op jit(solution)/shard_map/ppermute | solution.py:371
  61.4 1.5 %collective-permute-done.34.refs_2_ = bf16[32,2048]{1,0:T(8,128)(2,1)S(1)} collective-permute-done((bf16[32,2048]{1,0:T(8,128)(2,1)S(1)}, bf16[32,2048]{1,0:T(8,128)(2,1)S(1)}, u32[]{:S(2)}, u32[]{:S(2)}) %collective-permute-start.34) | collective-permute-done | bytes 131104 | tf_op jit(solution)/shard_map/ppermute | solution.py:371
  (74 shorter events, 14.0 us)
Async XLA Ops:
  1.8 6.6 %collective-permute-start.2 = (bf16[32,2176]{1,0:T(8,128)(2,1)S(1)}, bf16[32,2176]{1,0:T(8,128)(2,1)S(1)}, u32[]{:S(2)}, u32[]{:S(2)}) collective-permute-start(bf16[32,2176]{1,0:T(8,128)(2,1)S(1)} %get-tuple-element.36.refs_0_), channel_id=1, source_target_pairs={{0,8},{2,4},{4,2},{6,14},{8,0},{10,12},{12,10},{14,6},{16,24},{18,... | collective-permute-start | bytes 417800 | tf_op jit(solution)/shard_map/ppermute | solution.py:265
  3.5 6.2 %collective-permute-start = (bf16[32,2176]{1,0:T(8,128)(2,1)S(1)}, bf16[32,2176]{1,0:T(8,128)(2,1)S(1)}, u32[]{:S(2)}, u32[]{:S(2)}) collective-permute-start(bf16[32,2176]{1,0:T(8,128)(2,1)S(1)} %get-tuple-element.36.refs_0_), channel_id=1, source_target_pairs={{0,2},{2,0},{4,6},{6,4},{8,10},{10,8},{12,14},{14,12},{16,18},{18,... | collective-permute-start | bytes 417800 | tf_op jit(solution)/shard_map/ppermute | solution.py:262
  3.5 7.1 %collective-permute-start.13 = (bf16[32,2176]{1,0:T(8,128)(2,1)S(1)}, bf16[32,2176]{1,0:T(8,128)(2,1)S(1)}, u32[]{:S(2)}, u32[]{:S(2)}) collective-permute-start(bf16[32,2176]{1,0:T(8,128)(2,1)S(1)} %get-tuple-element.37.refs_2_), channel_id=1, source_target_pairs={{0,8},{2,4},{4,2},{6,14},{8,0},{10,12},{12,10},{14,6},{16,24},{18,... | collective-permute-start | bytes 417800 | tf_op jit(solution)/shard_map/ppermute | solution.py:265
  5.1 7.6 %collective-permute-start.1 = (bf16[32,2176]{1,0:T(8,128)(2,1)S(1)}, bf16[32,2176]{1,0:T(8,128)(2,1)S(1)}, u32[]{:S(2)}, u32[]{:S(2)}) collective-permute-start(bf16[32,2176]{1,0:T(8,128)(2,1)S(1)} %get-tuple-element.37.refs_2_), channel_id=1, source_target_pairs={{0,2},{2,0},{4,6},{6,4},{8,10},{10,8},{12,14},{14,12},{16,18},{18,... | collective-permute-start | bytes 417800 | tf_op jit(solution)/shard_map/ppermute | solution.py:262
  9.6 6.5 %collective-permute-start.3 = (bf16[32,2176]{1,0:T(8,128)(2,1)S(1)}, bf16[32,2176]{1,0:T(8,128)(2,1)S(1)}, u32[]{:S(2)}, u32[]{:S(2)}) collective-permute-start(bf16[32,2176]{1,0:T(8,128)(2,1)S(1)} %collective-permute-done.refs_0_.refs_1_.refs_2_.refs_3_), channel_id=1, source_target_pairs={{0,8},{2,4},{4,2},{6,14},{8,0},{10,12},{12,10},{14,6},{16,24},{18,... | collective-permute-start | bytes 417800 | tf_op jit(solution)/shard_map/ppermute | solution.py:265
  10.5 5.9 %collective-permute-start.5 = (bf16[32,2176]{1,0:T(8,128)(2,1)S(1)}, bf16[32,2176]{1,0:T(8,128)(2,1)S(1)}, u32[]{:S(2)}, u32[]{:S(2)}) collective-permute-start(bf16[32,2176]{1,0:T(8,128)(2,1)S(1)} %choose.11), channel_id=1, source_target_pairs={{0,2},{2,0},{4,6},{6,4},{8,10},{10,8},{12,14},{14,12},{16,18},{18,... | collective-permute-start | bytes 417800 | tf_op jit(solution)/shard_map/ppermute | solution.py:262
  10.6 8.5 %collective-permute-start.14 = (bf16[32,2176]{1,0:T(8,128)(2,1)S(1)}, bf16[32,2176]{1,0:T(8,128)(2,1)S(1)}, u32[]{:S(2)}, u32[]{:S(2)}) collective-permute-start(bf16[32,2176]{1,0:T(8,128)(2,1)S(1)} %choose.15), channel_id=1, source_target_pairs={{0,2},{2,0},{4,6},{6,4},{8,10},{10,8},{12,14},{14,12},{16,18},{18,... | collective-permute-start | bytes 417800 | tf_op jit(solution)/shard_map/ppermute | solution.py:262
  12.7 8.4 %collective-permute-start.7 = (bf16[32,2176]{1,0:T(8,128)(2,1)S(1)}, bf16[32,2176]{1,0:T(8,128)(2,1)S(1)}, u32[]{:S(2)}, u32[]{:S(2)}) collective-permute-start(bf16[32,2176]{1,0:T(8,128)(2,1)S(1)} %collective-permute-done.1.refs_4_.refs_5_.refs_6_.refs_7_), channel_id=1, source_target_pairs={{0,8},{2,4},{4,2},{6,14},{8,0},{10,12},{12,10},{14,6},{16,24},{18,... | collective-permute-start | bytes 417800 | tf_op jit(solution)/shard_map/ppermute | solution.py:265
  16.2 7.5 %collective-permute-start.4 = (bf16[32,2176]{1,0:T(8,128)(2,1)S(1)}, bf16[32,2176]{1,0:T(8,128)(2,1)S(1)}, u32[]{:S(2)}, u32[]{:S(2)}) collective-permute-start(bf16[32,2176]{1,0:T(8,128)(2,1)S(1)} %choose.10), channel_id=1, source_target_pairs={{0,2},{2,0},{4,6},{6,4},{8,10},{10,8},{12,14},{14,12},{16,18},{18,... | collective-permute-start | bytes 417800 | tf_op jit(solution)/shard_map/ppermute | solution.py:262
  16.4 7.3 %collective-permute-start.6 = (bf16[32,2176]{1,0:T(8,128)(2,1)S(1)}, bf16[32,2176]{1,0:T(8,128)(2,1)S(1)}, u32[]{:S(2)}, u32[]{:S(2)}) collective-permute-start(bf16[32,2176]{1,0:T(8,128)(2,1)S(1)} %collective-permute-done.5.refs_2_.refs_0_.refs_1_), channel_id=1, source_target_pairs={{0,8},{2,4},{4,2},{6,14},{8,0},{10,12},{12,10},{14,6},{16,24},{18,... | collective-permute-start | bytes 417800 | tf_op jit(solution)/shard_map/ppermute | solution.py:265
  19.1 8.2 %collective-permute-start.19 = (bf16[32,2176]{1,0:T(8,128)(2,1)S(1)}, bf16[32,2176]{1,0:T(8,128)(2,1)S(1)}, u32[]{:S(2)}, u32[]{:S(2)}) collective-permute-start(bf16[32,2176]{1,0:T(8,128)(2,1)S(1)} %collective-permute-done.14.refs_6_.refs_4_.refs_5_), channel_id=1, source_target_pairs={{0,8},{2,4},{4,2},{6,14},{8,0},{10,12},{12,10},{14,6},{16,24},{18,... | collective-permute-start | bytes 417800 | tf_op jit(solution)/shard_map/ppermute | solution.py:265
  20.6 8.1 %collective-permute-start.9 = (bf16[32,2048]{1,0:T(8,128)(2,1)S(1)}, bf16[32,2048]{1,0:T(8,128)(2,1)S(1)}, u32[]{:S(2)}, u32[]{:S(2)}) collective-permute-start(bf16[32,2048]{1,0:T(8,128)(2,1)S(1)} %get-tuple-element.45.at_end.refs_1_.at_mid), channel_id=1, source_target_pairs={{0,8},{2,4},{4,2},{6,14},{8,0},{10,12},{12,10},{14,6},{16,24},{18,... | collective-permute-start | bytes 393224 | tf_op jit(solution)/shard_map/ppermute | solution.py:265
  21.2 6.2 %collective-permute-start.8 = (bf16[32,2176]{1,0:T(8,128)(2,1)S(1)}, bf16[32,2176]{1,0:T(8,128)(2,1)S(1)}, u32[]{:S(2)}, u32[]{:S(2)}) collective-permute-start(bf16[32,2176]{1,0:T(8,128)(2,1)S(1)} %choose.12), channel_id=1, source_target_pairs={{0,2},{2,0},{4,6},{6,4},{8,10},{10,8},{12,14},{14,12},{16,18},{18,... | collective-permute-start | bytes 417800 | tf_op jit(solution)/shard_map/ppermute | solution.py:262
  23.7 7.1 %collective-permute-start.15 = (bf16[32,2048]{1,0:T(8,128)(2,1)S(1)}, bf16[32,2048]{1,0:T(8,128)(2,1)S(1)}, u32[]{:S(2)}, u32[]{:S(2)}) collective-permute-start(bf16[32,2048]{1,0:T(8,128)(2,1)S(1)} %choose.16), channel_id=1, source_target_pairs={{0,2},{2,0},{4,6},{6,4},{8,10},{10,8},{12,14},{14,12},{16,18},{18,... | collective-permute-start | bytes 393224 | tf_op jit(solution)/shard_map/ppermute | solution.py:262
  25.8 6.0 %collective-permute-start.11 = (bf16[32,2048]{1,0:T(8,128)(2,1)S(1)}, bf16[32,2048]{1,0:T(8,128)(2,1)S(1)}, u32[]{:S(2)}, u32[]{:S(2)}) collective-permute-start(bf16[32,2048]{1,0:T(8,128)(2,1)S(1)} %get-tuple-element.47.refs_3_.at_end.at_mid), channel_id=1, source_target_pairs={{0,8},{2,4},{4,2},{6,14},{8,0},{10,12},{12,10},{14,6},{16,24},{18,... | collective-permute-start | bytes 393224 | tf_op jit(solution)/shard_map/ppermute | solution.py:265
  27.3 6.0 %collective-permute-start.20 = (bf16[32,2048]{1,0:T(8,128)(2,1)S(1)}, bf16[32,2048]{1,0:T(8,128)(2,1)S(1)}, u32[]{:S(2)}, u32[]{:S(2)}) collective-permute-start(bf16[32,2048]{1,0:T(8,128)(2,1)S(1)} %choose.17), channel_id=1, source_target_pairs={{0,2},{2,0},{4,6},{6,4},{8,10},{10,8},{12,14},{14,12},{16,18},{18,... | collective-permute-start | bytes 393224 | tf_op jit(solution)/shard_map/ppermute | solution.py:262
  28.7 7.5 %collective-permute-start.10 = (bf16[32,2048]{1,0:T(8,128)(2,1)S(1)}, bf16[32,2048]{1,0:T(8,128)(2,1)S(1)}, u32[]{:S(2)}, u32[]{:S(2)}) collective-permute-start(bf16[32,2048]{1,0:T(8,128)(2,1)S(1)} %choose.13), channel_id=1, source_target_pairs={{0,2},{2,0},{4,6},{6,4},{8,10},{10,8},{12,14},{14,12},{16,18},{18,... | collective-permute-start | bytes 393224 | tf_op jit(solution)/shard_map/ppermute | solution.py:262
  30.9 5.6 %collective-permute-start.16 = (bf16[32,2048]{1,0:T(8,128)(2,1)S(1)}, bf16[32,2048]{1,0:T(8,128)(2,1)S(1)}, u32[]{:S(2)}, u32[]{:S(2)}) collective-permute-start(bf16[32,2048]{1,0:T(8,128)(2,1)S(1)} %add.8), channel_id=1, source_target_pairs={{0,8},{2,4},{4,2},{6,14},{8,0},{10,12},{12,10},{14,6},{16,24},{18,... | collective-permute-start | bytes 393224 | tf_op jit(solution)/shard_map/ppermute | solution.py:265
  31.8 6.4 %collective-permute-start.12 = (bf16[32,2048]{1,0:T(8,128)(2,1)S(1)}, bf16[32,2048]{1,0:T(8,128)(2,1)S(1)}, u32[]{:S(2)}, u32[]{:S(2)}) collective-permute-start(bf16[32,2048]{1,0:T(8,128)(2,1)S(1)} %choose.14), channel_id=1, source_target_pairs={{0,2},{2,0},{4,6},{6,4},{8,10},{10,8},{12,14},{14,12},{16,18},{18,... | collective-permute-start | bytes 393224 | tf_op jit(solution)/shard_map/ppermute | solution.py:262
  33.3 5.3 %collective-permute-start.21 = (bf16[32,2048]{1,0:T(8,128)(2,1)S(1)}, bf16[32,2048]{1,0:T(8,128)(2,1)S(1)}, u32[]{:S(2)}, u32[]{:S(2)}) collective-permute-start(bf16[32,2048]{1,0:T(8,128)(2,1)S(1)} %add.10), channel_id=1, source_target_pairs={{0,8},{2,4},{4,2},{6,14},{8,0},{10,12},{12,10},{14,6},{16,24},{18,... | collective-permute-start | bytes 393224 | tf_op jit(solution)/shard_map/ppermute | solution.py:265
  35.9 5.6 %collective-permute-start.24 = (bf16[32,2048]{1,0:T(8,128)(2,1)S(1)}, bf16[32,2048]{1,0:T(8,128)(2,1)S(1)}, u32[]{:S(2)}, u32[]{:S(2)}) collective-permute-start(bf16[32,2048]{1,0:T(8,128)(2,1)S(1)} %choose.18), channel_id=1, source_target_pairs={{0,2},{2,0},{4,6},{6,4},{8,10},{10,8},{12,14},{14,12},{16,18},{18,... | collective-permute-start | bytes 393224 | tf_op jit(solution)/shard_map/ppermute | solution.py:262
  36.5 6.2 %collective-permute-start.17 = (bf16[32,2048]{1,0:T(8,128)(2,1)S(1)}, bf16[32,2048]{1,0:T(8,128)(2,1)S(1)}, u32[]{:S(2)}, u32[]{:S(2)}) collective-permute-start(bf16[32,2048]{1,0:T(8,128)(2,1)S(1)} %add.9), channel_id=1, source_target_pairs={{0,8},{2,4},{4,2},{6,14},{8,0},{10,12},{12,10},{14,6},{16,24},{18,... | collective-permute-start | bytes 393224 | tf_op jit(solution)/shard_map/ppermute | solution.py:265
  37.8 6.4 %collective-permute-start.25 = (bf16[32,2048]{1,0:T(8,128)(2,1)S(1)}, bf16[32,2048]{1,0:T(8,128)(2,1)S(1)}, u32[]{:S(2)}, u32[]{:S(2)}) collective-permute-start(bf16[32,2048]{1,0:T(8,128)(2,1)S(1)} %choose.19), channel_id=1, source_target_pairs={{0,2},{2,0},{4,6},{6,4},{8,10},{10,8},{12,14},{14,12},{16,18},{18,... | collective-permute-start | bytes 393224 | tf_op jit(solution)/shard_map/ppermute | solution.py:262
  38.7 6.8 %collective-permute-start.22 = (bf16[32,2048]{1,0:T(8,128)(2,1)S(1)}, bf16[32,2048]{1,0:T(8,128)(2,1)S(1)}, u32[]{:S(2)}, u32[]{:S(2)}) collective-permute-start(bf16[32,2048]{1,0:T(8,128)(2,1)S(1)} %add.11), channel_id=1, source_target_pairs={{0,8},{2,4},{4,2},{6,14},{8,0},{10,12},{12,10},{14,6},{16,24},{18,... | collective-permute-start | bytes 393224 | tf_op jit(solution)/shard_map/ppermute | solution.py:265
  42.7 6.0 %collective-permute-start.26 = (bf16[32,2048]{1,0:T(8,128)(2,1)S(1)}, bf16[32,2048]{1,0:T(8,128)(2,1)S(1)}, u32[]{:S(2)}, u32[]{:S(2)}) collective-permute-start(bf16[32,2048]{1,0:T(8,128)(2,1)S(1)} %add.12), channel_id=1, source_target_pairs={{0,8},{2,4},{4,2},{6,14},{8,0},{10,12},{12,10},{14,6},{16,24},{18,... | collective-permute-start | bytes 393224 | tf_op jit(solution)/shard_map/ppermute | solution.py:265
  44.2 6.3 %collective-permute-start.18 = (bf16[32,2048]{1,0:T(8,128)(2,1)S(1)}, bf16[32,2048]{1,0:T(8,128)(2,1)S(1)}, u32[]{:S(2)}, u32[]{:S(2)}) collective-permute-start(bf16[32,2048]{1,0:T(8,128)(2,1)S(1)} %choose_sum.4), channel_id=1, source_target_pairs={{0,2},{2,0},{4,6},{6,4},{8,10},{10,8},{12,14},{14,12},{16,18},{18,... | collective-permute-start | bytes 393224 | tf_op jit(solution)/shard_map/ppermute | solution.py:262
  45.5 5.7 %collective-permute-start.29 = (bf16[32,2048]{1,0:T(8,128)(2,1)S(1)}, bf16[32,2048]{1,0:T(8,128)(2,1)S(1)}, u32[]{:S(2)}, u32[]{:S(2)}) collective-permute-start(bf16[32,2048]{1,0:T(8,128)(2,1)S(1)} %add.14), channel_id=1, source_target_pairs={{0,8},{2,4},{4,2},{6,14},{8,0},{10,12},{12,10},{14,6},{16,24},{18,... | collective-permute-start | bytes 393224 | tf_op jit(solution)/shard_map/ppermute | solution.py:265
  47.0 6.3 %collective-permute-start.23 = (bf16[32,2048]{1,0:T(8,128)(2,1)S(1)}, bf16[32,2048]{1,0:T(8,128)(2,1)S(1)}, u32[]{:S(2)}, u32[]{:S(2)}) collective-permute-start(bf16[32,2048]{1,0:T(8,128)(2,1)S(1)} %choose_sum.5), channel_id=1, source_target_pairs={{0,2},{2,0},{4,6},{6,4},{8,10},{10,8},{12,14},{14,12},{16,18},{18,... | collective-permute-start | bytes 393224 | tf_op jit(solution)/shard_map/ppermute | solution.py:262
  48.7 7.4 %collective-permute-start.27 = (bf16[32,2048]{1,0:T(8,128)(2,1)S(1)}, bf16[32,2048]{1,0:T(8,128)(2,1)S(1)}, u32[]{:S(2)}, u32[]{:S(2)}) collective-permute-start(bf16[32,2048]{1,0:T(8,128)(2,1)S(1)} %choose_sum.6), channel_id=1, source_target_pairs={{0,2},{2,0},{4,6},{6,4},{8,10},{10,8},{12,14},{14,12},{16,18},{18,... | collective-permute-start | bytes 393224 | tf_op jit(solution)/shard_map/ppermute | solution.py:262
  50.5 6.2 %collective-permute-start.28 = (bf16[32,2048]{1,0:T(8,128)(2,1)S(1)}, bf16[32,2048]{1,0:T(8,128)(2,1)S(1)}, u32[]{:S(2)}, u32[]{:S(2)}) collective-permute-start(bf16[32,2048]{1,0:T(8,128)(2,1)S(1)} %add.13), channel_id=1, source_target_pairs={{0,8},{2,4},{4,2},{6,14},{8,0},{10,12},{12,10},{14,6},{16,24},{18,... | collective-permute-start | bytes 393224 | tf_op jit(solution)/shard_map/ppermute | solution.py:265
  51.2 6.4 %collective-permute-start.30 = (bf16[32,2048]{1,0:T(8,128)(2,1)S(1)}, bf16[32,2048]{1,0:T(8,128)(2,1)S(1)}, u32[]{:S(2)}, u32[]{:S(2)}) collective-permute-start(bf16[32,2048]{1,0:T(8,128)(2,1)S(1)} %choose_sum.7), channel_id=1, source_target_pairs={{0,2},{2,0},{4,6},{6,4},{8,10},{10,8},{12,14},{14,12},{16,18},{18,... | collective-permute-start | bytes 393224 | tf_op jit(solution)/shard_map/ppermute | solution.py:262
  54.1 8.8 %collective-permute-start.32 = (bf16[64,2048]{1,0:T(8,128)(2,1)S(1)}, bf16[64,2048]{1,0:T(8,128)(2,1)S(1)}, u32[]{:S(2)}, u32[]{:S(2)}) collective-permute-start(bf16[64,2048]{1,0:T(8,128)(2,1)S(1)} %finish_first.1.firsts), channel_id=1, source_target_pairs={{0,8},{8,16},{16,24},{24,0},{1,9},{9,17},{17,25},{25,1},{2,10},{10... | collective-permute-start | bytes 786440 | tf_op jit(solution)/shard_map/ppermute | solution.py:371
  (3 other events, 14.0 us)

commit v6 on v5

--- a/solution.py
+++ b/solution.py
@@ -141,16 +141,6 @@
     return narrow(out).astype(jnp.float32)
 
 
-def own_pass(*refs):
-    pieces, (gate_w, up_w, down_w, total) = refs[: 2 * STREAMS], refs[2 * STREAMS :]
-    width = total.shape[1]
-    rows = jnp.concatenate([piece[:, :width] for piece in pieces], axis=0)
-    weight = jnp.concatenate(
-        [weight_of(pieces[i // 2 * 2][:, width:], i % 2) for i in range(2 * STREAMS)], axis=0
-    )
-    total[...] = rows.astype(jnp.float32) + expert_of(rows, gate_w, up_w, down_w) * weight
-
-
 def load(*refs):
     sems = refs[6]
     copies = [pltpu.make_async_copy(refs[i], refs[3 + i], sems.at[i]) for i in range(3)]
@@ -163,17 +153,26 @@
 def pass_of(late):
     def body(*refs):
         _, end = position()
-        given, (gate_w, up_w, down_w), results = refs[: -3 - STREAMS], refs[-3 - STREAMS : -STREAMS], refs[-STREAMS:]
+        given, refs = refs[: 4 * STREAMS], refs[4 * STREAMS :]
+        pieces = refs[: 2 * STREAMS] if len(refs) > 3 + STREAMS else ()
+        refs = refs[len(pieces) :]
+        weights, results, totals = refs[:3], refs[3 : 3 + STREAMS], refs[3 + STREAMS :]
         piece, width = results[0].shape
         rows, weight = [], []
         for s in range(STREAMS):
             at_end, at_mid, tag_end, tag_mid = given[4 * s : 4 * s + 4]
             rows.append(jnp.where(end, at_end[:, :width], at_mid[:, :width]))
             weight.append(weight_of(jnp.where(end, tag_end[:, width:], tag_mid[:, width:]), late))
-        out = expert_of(jnp.concatenate(rows, axis=0), gate_w, up_w, down_w)
-        out = narrow(out * jnp.concatenate(weight, axis=0))
+        for i, ref in enumerate(pieces):
+            rows.append(ref[:, :width])
+            weight.append(weight_of(pieces[i // 2 * 2][:, width:], i % 2))
+        rows, weight = jnp.concatenate(rows, axis=0), jnp.concatenate(weight, axis=0)
+        out = expert_of(rows, *weights) * weight
         for s in range(STREAMS):
-            results[s][...] = out[s * piece : (s + 1) * piece]
+            results[s][...] = narrow(out[s * piece : (s + 1) * piece])
+        for total in totals:
+            start = STREAMS * piece
+            total[...] = rows[start:].astype(jnp.float32) + out[start:]
 
     return body
 
@@ -197,15 +196,15 @@
     result[...] = narrow(wide(a) + wide(b))
 
 
-def finish_first(total, *refs):
-    _, end = position()
-    given, result = refs[:-1], refs[-1]
-    (rows, width), piece = result.shape, result.shape[0] // STREAMS
-    for s in range(STREAMS):
-        far, near, inner = given[3 * s : 3 * s + 3]
+def finish_first(stream):
+    def body(total, far, near, inner, result):
+        _, end = position()
+        piece, width = result.shape
+        own = total[2 * stream * piece : (2 * stream + 1) * piece]
         at_mid = near[:, :width].astype(jnp.float32) + wide(inner)
-        own = total[2 * s * piece : (2 * s + 1) * piece]
-        result[s * piece : (s + 1) * piece] = narrow(own + jnp.where(end, wide(far), at_mid))
+        result[...] = narrow(own + jnp.where(end, wide(far), at_mid))
+
+    return body
 
 
 def finish_second(stream):
@@ -218,25 +217,34 @@
     return body
 
 
-def join(firsts, *refs):
-    seconds, whole, sems = refs[:STREAMS], refs[STREAMS], refs[STREAMS + 1]
-    piece = seconds[0].shape[0]
-    copies = []
-    for s in range(STREAMS):
-        for i, part in enumerate((firsts.at[pl.ds(s * piece, piece)], seconds[s])):
-            place = 2 * s + i
-            there = whole.at[pl.ds(place * piece, piece)]
-            copies.append(pltpu.make_async_copy(part, there, sems.at[place]))
+def join(*refs):
+    parts, whole, sems = refs[:-2], refs[-2], refs[-1]
+    copies, row = [], 0
+    for i, part in enumerate(parts):
+        there = whole.at[pl.ds(row, part.shape[0])]
+        copies.append(pltpu.make_async_copy(part, there, sems.at[i]))
+        row += part.shape[0]
     for copy in copies:
         copy.start()
     for copy in copies:
         copy.wait()
 
 
+def join_two(a, b, result):
+    half = a.shape[0]
+    result[:half] = a[...]
+    result[half:] = b[...]
+
+
+def join_apart(firsts, *refs):
+    half = firsts.shape[0] // 2
+    join_handed(firsts.at[:half], refs[0], firsts.at[half:], *refs[1:])
+
+
 def join_handed(*refs):
     @pl.when(lax.axis_index("section") == 0)
     def _():
-        for ref in refs[: 1 + STREAMS]:
+        for ref in refs[:-2]:
             ref[...] = jnp.zeros_like(ref)
 
     join(*refs)
@@ -282,9 +290,16 @@
     first, second = pieces[::2], pieces[1::2]
     o, i, p = [[None] * 8 for _ in both], [[None] * 8 for _ in both], [None] * 8
 
+    sent = [None, None]
+
     def swap(k, s, to_outer, to_inner):
-        if 5 <= k <= 7:
+        if k == 3:
+            o[s][k - 1], to_outer = lax.optimization_barrier((o[s][k - 1], to_outer))
+        if k in (5, 6):
             i[s][k - 1], to_inner = lax.optimization_barrier((i[s][k - 1], to_inner))
+        if s == 1 and k == 4:
+            to_outer, _ = lax.optimization_barrier((to_outer, sent[0]))
+        sent[:] = [to_outer, to_inner]
         o[s][k], i[s][k] = outer(to_outer), inner(to_inner)
 
     for s in both:
@@ -300,14 +315,16 @@
     )
     i[0][0], *weights = lax.optimization_barrier((i[0][0], *weights))
 
-    def expert(late, given):
+    def expert(late, given, *own):
+        count_all = piece * (STREAMS + len(own))
         return run(
             pass_of(late),
             "expert_pass",
-            [held(block)] * STREAMS,
+            [held(block)] * STREAMS + ([held((count, width), jnp.float32)] if own else []),
             *(x for s in both for x in given(s)),
+            *own,
             *weights,
-            work=(6 * piece * STREAMS * weights[0].size, 6 * weights[0].size),
+            work=(6 * count_all * weights[0].size, 6 * weights[0].size),
         )
 
     def mixed(body, *operands, shape=block):
@@ -319,41 +336,32 @@
     for s in both:
         swap(2, s, mixed(choose, p[1][s], i[s][1], shape=tagged), o[s][1])
     p[2] = expert(False, lambda s: (o[s][1], i[s][0]) * 2)
-    total = run(
-        own_pass,
-        "own_pass",
-        held((count, width), jnp.float32),
-        *pieces,
-        *weights,
-        work=(6 * count * weights[0].size, 6 * weights[0].size),
-    )
-    o[0][2], i[0][2], total = lax.optimization_barrier((o[0][2], i[0][2], total))
     for s in both:
         swap(3, s, mixed(choose, p[2][s], i[s][2]), second[s])
     p[3] = expert(False, lambda s: (o[s][2], i[s][1]) * 2)
     for s in both:
         swap(4, s, mixed(choose, p[3][s], i[s][3]), mixed(add, o[s][3], p[2][s]))
-    p[4] = expert(True, lambda s: (o[s][3], i[s][2], o[s][2], i[s][1]))
+    *p[4], total = expert(True, lambda s: (o[s][3], i[s][2], o[s][2], i[s][1]), *pieces)
     for s in both:
         swap(5, s, mixed(choose, p[4][s], second[s]), mixed(add, o[s][4], p[3][s]))
     p[5] = expert(True, lambda s: (o[s][4], i[s][3], o[s][1], i[s][0]))
     for s in both:
         at_outer = mixed(choose_sum, p[5][s], i[s][5], p[1][s])
         swap(6, s, at_outer, mixed(add, o[s][5], p[4][s]))
+    firsts = [
+        run(finish_first(s), "finish_first", held(block), total, o[s][6], o[s][2], i[s][4])
+        for s in both
+    ]
     p[6] = expert(True, lambda s: (o[s][5], o[s][1], o[s][0], o[s][0]))
     for s in both:
         at_outer = mixed(choose_sum, p[6][s], i[s][6], p[6][s])
         swap(7, s, at_outer, mixed(add, o[s][6], p[5][s]))
-    firsts = run(
-        finish_first,
-        "finish_first",
-        held((STREAMS * piece, width)),
-        total,
-        *(x for s in both for x in (o[s][6], o[s][2], i[s][4])),
-    )
-    seconds = [
-        run(finish_second(s), "finish_second", held(block), total, o[s][7], i[s][7]) for s in both
-    ]
+    done = [None] * 4
+    for s in both:
+        done[2 * s + 1] = run(
+            finish_second(s), "finish_second", held(block), total, o[s][7], i[s][7]
+        )
+        done[2 * s] = firsts[s]
 
     def joined(body, parts):
         return run(
@@ -365,11 +373,13 @@
             out_specs=ANYWHERE,
         )
 
-    parts = [firsts, *seconds]
     count_s = lax.axis_size("section")
     ring = [(s, (s + 1) % count_s) for s in range(count_s)]
-    handed = [lax.ppermute(part, "section", ring) for part in parts]
-    return (joined(join, parts)[None], joined(join_handed, handed)[None])
+    one = run(join_two, "join_two", held((2 * piece, width)), firsts[0], firsts[1])
+    back = lax.ppermute(one, "section", ring)
+    given = [back, *(lax.ppermute(done[k], "section", ring) for k in (1, 3))]
+    handed = joined(join_apart, given)
+    return (joined(join, done)[None], handed[None])
 
 
 def solution(mesh):

time: 64.8 us -> 63.9 us (0.986)
  waiting for transfers between devices: 17.7 us -> 24.6 us
  starting transfers between devices: 29.7 us -> 23.1 us
  Pallas kernels: 15.4 us -> 14.5 us
    ppermute x16, waiting for transfers between devices: 8.47 us -> 14.4 us  [outer(): return lax.ppermute(value, axes, outer_pairs)]
    ppermute x16, starting transfers between devices: 10.1 us -> 6.64 us  [outer(): return lax.ppermute(value, axes, outer_pairs)]
    ppermute x16, starting transfers between devices: 19.4 us -> 16.3 us  [inner(): return lax.ppermute(value, axes, inner_pairs)]
    pallas_call x36 -> x37, Pallas kernels: 15.4 us -> 14.5 us  [run(): pl.pallas_call(body, out_shape=out_shape, in_specs=specs, out_specs=out_s...]
  transfers between devices with their start and end apart: 35 -> 35, of which waited for: 19 -> 22; matrix products, arithmetic and copies ran while one was open for 0% -> 0% of each run, Pallas kernels for 21% -> 20%
where the time goes in v6:
time: 63.9 us; the launch traced here: 63.1 us
  waiting for transfers between devices  24.6 us (38%)
  starting transfers between devices  23.1 us (36%)
  Pallas kernels  14.5 us (23%)
  between operations  0.94 us (1%)
    ppermute x16, starting transfers between devices, inner(): return lax.ppermute(value, axes, inner_pairs)  16.3 us
    pallas_call x37, Pallas kernels, run(): pl.pallas_call(body, out_shape=out_shape, in_specs=specs, out_specs=out_s...  14.5 us
    ppermute x16, waiting for transfers between devices, outer(): return lax.ppermute(value, axes, outer_pairs)  14.4 us
    ppermute x16, starting transfers between devices, outer(): return lax.ppermute(value, axes, outer_pairs)  6.64 us
    ppermute x16, waiting for transfers between devices, inner(): return lax.ppermute(value, axes, inner_pairs)  6.15 us
    ppermute x2, waiting for transfers between devices, on_line(): given = [back, *(lax.ppermute(done[k], 'section', ring) for k in (1, 3))]  4.07 us
  transfers between devices with their start and end apart: 35, of which 22 were waited for; matrix products, arithmetic and copies ran while one was open for 0% of the time, Pallas kernels for 20%

profile of v6, /device:TPU:12, one launch (start us, length us, event | category | flops | bytes accessed | tf_op | source)
XLA Modules:
  0.0 63.1 jit_solution(12676158853242002718)
XLA Ops:
  0.6 1.2 %prepare.1 = (bf16[32,2176]{1,0:T(8,128)(2,1)S(1)}, bf16[32,2048]{1,0:T(8,128)(2,1)S(1)}, bf16[32,2176]{1,0:T(8,128)(2,1)S(1)}, bf16[32,2048]{1,0:T(8,128)(2,1)S(1)}) custom-call(bf16[128,2048]{1,0:T(8,128)(2,1)} %bitcast.15, s32[2,128]{1,0:T(2,128)} %bitcast.18, f32[2,128]{1,0:T(2,128)} %bitcast.19), custom_call_target="tpu_custom_call" | custom-call | tf_op jit(solution)/shard_map/prepare/pallas_call | solution.py:87
  1.8 1.6 %collective-permute-start.2 = (bf16[32,2176]{1,0:T(8,128)(2,1)S(1)}, bf16[32,2176]{1,0:T(8,128)(2,1)S(1)}, u32[]{:S(2)}, u32[]{:S(2)}) collective-permute-start(bf16[32,2176]{1,0:T(8,128)(2,1)S(1)} %get-tuple-element.37.refs_8_), channel_id=1, source_target_pairs={{0,8},{2,4},{4,2},{6,14},{8,0},{10,12},{12,10},{14,6},{16,24},{18,... | collective-permute-start | bytes 417800 | tf_op jit(solution)/shard_map/ppermute | solution.py:273
  3.5 1.7 %collective-permute-start.6 = (bf16[32,2176]{1,0:T(8,128)(2,1)S(1)}, bf16[32,2176]{1,0:T(8,128)(2,1)S(1)}, u32[]{:S(2)}, u32[]{:S(2)}) collective-permute-start(bf16[32,2176]{1,0:T(8,128)(2,1)S(1)} %get-tuple-element.38.refs_10_), channel_id=1, source_target_pairs={{0,8},{2,4},{4,2},{6,14},{8,0},{10,12},{12,10},{14,6},{16,24},{18,... | collective-permute-start | bytes 417800 | tf_op jit(solution)/shard_map/ppermute | solution.py:273
  5.5 2.9 %load.1 = (bf16[2048,512]{1,0:T(8,128)(2,1)S(1)}, bf16[2048,512]{1,0:T(8,128)(2,1)S(1)}, bf16[512,2048]{1,0:T(8,128)(2,1)S(1)}) custom-call(bf16[2048,512]{1,0:T(8,128)(2,1)} %bitcast.12, bf16[2048,512]{1,0:T(8,128)(2,1)} %bitcast.13, bf16[512,2048]{1,0:T(8,128)(2,1)} %bitcast.14), custom_call_target="tpu_custom_call" | custom-call | bytes 6291456 | tf_op jit(solution)/shard_map/load/pallas_call | solution.py:87
  8.5 1.7 %collective-permute-start.5 = (bf16[32,2176]{1,0:T(8,128)(2,1)S(1)}, bf16[32,2176]{1,0:T(8,128)(2,1)S(1)}, u32[]{:S(2)}, u32[]{:S(2)}) collective-permute-start(bf16[32,2176]{1,0:T(8,128)(2,1)S(1)} %choose.11), channel_id=1, source_target_pairs={{0,2},{2,0},{4,6},{6,4},{8,10},{10,8},{12,14},{14,12},{16,18},{18,... | collective-permute-start | bytes 417800 | tf_op jit(solution)/shard_map/ppermute | solution.py:270
  10.7 1.1 %collective-permute-done.1.refs_4_.refs_5_.refs_6_.refs_7_ = bf16[32,2176]{1,0:T(8,128)(2,1)S(1)} collective-permute-done((bf16[32,2176]{1,0:T(8,128)(2,1)S(1)}, bf16[32,2176]{1,0:T(8,128)(2,1)S(1)}, u32[]{:S(2)}, u32[]{:S(2)}) %collective-permute-start.1) | collective-permute-done | bytes 139296 | tf_op jit(solution)/shard_map/ppermute | solution.py:270
  11.8 1.1 %collective-permute-start.10 = (bf16[32,2176]{1,0:T(8,128)(2,1)S(1)}, bf16[32,2176]{1,0:T(8,128)(2,1)S(1)}, u32[]{:S(2)}, u32[]{:S(2)}) collective-permute-start(bf16[32,2176]{1,0:T(8,128)(2,1)S(1)} %collective-permute-done.1.refs_4_.refs_5_.refs_6_.refs_7_), channel_id=1, source_target_pairs={{0,8},{2,4},{4,2},{6,14},{8,0},{10,12},{12,10},{14,6},{16,24},{18,... | collective-permute-start | bytes 417800 | tf_op jit(solution)/shard_map/ppermute | solution.py:273
  12.9 1.3 %expert_pass.6 = (bf16[32,2048]{1,0:T(8,128)(2,1)S(1)}, bf16[32,2048]{1,0:T(8,128)(2,1)S(1)}) custom-call(bf16[32,2176]{1,0:T(8,128)(2,1)S(1)} %collective-permute-done.refs_0_.refs_1_.refs_2_.refs_3_, bf16[32,2176]{1,0:T(8,128)(2,1)S(1)} %collective-permute-done.refs_0_.refs_1_.refs_2_.refs_3_, ...), custom_call_target="tpu_custom_call" | custom-call | flops 402653184 | bytes 6291456 | tf_op jit(solution)/shard_map/expert_pass/pallas_call | solution.py:87
  15.1 1.5 %collective-permute-start.8 = (bf16[32,2176]{1,0:T(8,128)(2,1)S(1)}, bf16[32,2176]{1,0:T(8,128)(2,1)S(1)}, u32[]{:S(2)}, u32[]{:S(2)}) collective-permute-start(bf16[32,2176]{1,0:T(8,128)(2,1)S(1)} %collective-permute-done.5.refs_0_.refs_2_.refs_1_), channel_id=1, source_target_pairs={{0,8},{2,4},{4,2},{6,14},{8,0},{10,12},{12,10},{14,6},{16,24},{18,... | collective-permute-start | bytes 417800 | tf_op jit(solution)/shard_map/ppermute | solution.py:273
  18.3 0.9 %collective-permute-done.10.at_mid.refs_7_.refs_5_ = bf16[32,2176]{1,0:T(8,128)(2,1)S(1)} collective-permute-done((bf16[32,2176]{1,0:T(8,128)(2,1)S(1)}, bf16[32,2176]{1,0:T(8,128)(2,1)S(1)}, u32[]{:S(2)}, u32[]{:S(2)}) %collective-permute-start.10) | collective-permute-done | bytes 139296 | tf_op jit(solution)/shard_map/ppermute | solution.py:273
  20.2 1.3 %expert_pass.7 = (bf16[32,2048]{1,0:T(8,128)(2,1)S(1)}, bf16[32,2048]{1,0:T(8,128)(2,1)S(1)}) custom-call(bf16[32,2176]{1,0:T(8,128)(2,1)S(1)} %collective-permute-done.5.refs_0_.refs_2_.refs_1_, bf16[32,2176]{1,0:T(8,128)(2,1)S(1)} %collective-permute-done.2.at_mid.refs_1_.refs_3_, bf16[32,2176]{1,0:T(8,128)(2,1)S(1)} %collective-permute-done.5.refs_0_.refs_2_.refs_1_, ...), custom_call_target="tpu_custom_call" | custom-call | flops 402653184 | bytes 6291456 | tf_op jit(solution)/shard_map/expert_pass/pallas_call | solution.py:87
  22.2 0.9 %collective-permute-done.4.refs_2_.refs_0_.near = bf16[32,2176]{1,0:T(8,128)(2,1)S(1)} collective-permute-done((bf16[32,2176]{1,0:T(8,128)(2,1)S(1)}, bf16[32,2176]{1,0:T(8,128)(2,1)S(1)}, u32[]{:S(2)}, u32[]{:S(2)}) %collective-permute-start.4) | collective-permute-done | bytes 139296 | tf_op jit(solution)/shard_map/ppermute | solution.py:270
  24.1 1.1 %collective-permute-done.12.at_mid.refs_5_ = bf16[32,2176]{1,0:T(8,128)(2,1)S(1)} collective-permute-done((bf16[32,2176]{1,0:T(8,128)(2,1)S(1)}, bf16[32,2176]{1,0:T(8,128)(2,1)S(1)}, u32[]{:S(2)}, u32[]{:S(2)}) %collective-permute-start.12) | collective-permute-done | bytes 139296 | tf_op jit(solution)/shard_map/ppermute | solution.py:273
  25.9 1.3 %expert_pass.9 = (bf16[32,2048]{1,0:T(8,128)(2,1)S(1)}, bf16[32,2048]{1,0:T(8,128)(2,1)S(1)}) custom-call(bf16[32,2176]{1,0:T(8,128)(2,1)S(1)} %collective-permute-done.4.refs_2_.refs_0_.near, bf16[32,2176]{1,0:T(8,128)(2,1)S(1)} %collective-permute-done.3.at_mid.refs_3_.refs_1_, bf16[32,2176]{1,0:T(8,128)(2,1)S(1)} %collective-permute-done.4.refs_2_.refs_0_.near, ...), custom_call_target="tpu_custom_call" | custom-call | flops 402653184 | bytes 6291456 | tf_op jit(solution)/shard_map/expert_pass/pallas_call | solution.py:87
  30.3 1.8 %collective-permute-done.13.refs_4_.a = bf16[32,2048]{1,0:T(8,128)(2,1)S(1)} collective-permute-done((bf16[32,2048]{1,0:T(8,128)(2,1)S(1)}, bf16[32,2048]{1,0:T(8,128)(2,1)S(1)}, u32[]{:S(2)}, u32[]{:S(2)}) %collective-permute-start.13) | collective-permute-done | bytes 131104 | tf_op jit(solution)/shard_map/ppermute | solution.py:270
  32.3 1.5 %expert_pass.8 = (bf16[32,2048]{1,0:T(8,128)(2,1)S(1)}, bf16[32,2048]{1,0:T(8,128)(2,1)S(1)}, f32[128,2048]{1,0:T(8,128)S(1)}) custom-call(bf16[32,2048]{1,0:T(8,128)(2,1)S(1)} %collective-permute-done.9.refs_0_.a, bf16[32,2176]{1,0:T(8,128)(2,1)S(1)} %collective-permute-done.8.at_mid.refs_1_, ...), custom_call_target="tpu_custom_call" | custom-call | flops 1207959552 | bytes 6291456 | tf_op jit(solution)/shard_map/expert_pass/pallas_call | solution.py:87
  34.1 0.9 %collective-permute-done.15.refs_0_.a = bf16[32,2048]{1,0:T(8,128)(2,1)S(1)} collective-permute-done((bf16[32,2048]{1,0:T(8,128)(2,1)S(1)}, bf16[32,2048]{1,0:T(8,128)(2,1)S(1)}, u32[]{:S(2)}, u32[]{:S(2)}) %collective-permute-start.15) | collective-permute-done | bytes 131104 | tf_op jit(solution)/shard_map/ppermute | solution.py:270
  35.0 1.1 %collective-permute-start.22 = (bf16[32,2048]{1,0:T(8,128)(2,1)S(1)}, bf16[32,2048]{1,0:T(8,128)(2,1)S(1)}, u32[]{:S(2)}, u32[]{:S(2)}) collective-permute-start(bf16[32,2048]{1,0:T(8,128)(2,1)S(1)} %choose.19), channel_id=1, source_target_pairs={{0,2},{2,0},{4,6},{6,4},{8,10},{10,8},{12,14},{14,12},{16,18},{18,... | collective-permute-start | bytes 393224 | tf_op jit(solution)/shard_map/ppermute | solution.py:270
  36.1 2.1 %collective-permute-start.19 = (bf16[32,2048]{1,0:T(8,128)(2,1)S(1)}, bf16[32,2048]{1,0:T(8,128)(2,1)S(1)}, u32[]{:S(2)}, u32[]{:S(2)}) collective-permute-start(bf16[32,2048]{1,0:T(8,128)(2,1)S(1)} %add.9), channel_id=1, source_target_pairs={{0,8},{2,4},{4,2},{6,14},{8,0},{10,12},{12,10},{14,6},{16,24},{18,... | collective-permute-start | bytes 393224 | tf_op jit(solution)/shard_map/ppermute | solution.py:273
  38.3 1.3 %expert_pass.10 = (bf16[32,2048]{1,0:T(8,128)(2,1)S(1)}, bf16[32,2048]{1,0:T(8,128)(2,1)S(1)}) custom-call(bf16[32,2048]{1,0:T(8,128)(2,1)S(1)} %collective-permute-done.15.refs_0_.a, bf16[32,2048]{1,0:T(8,128)(2,1)S(1)} %collective-permute-done.14.at_mid.refs_1_, bf16[32,2176]{1,0:T(8,128)(2,1)S(1)} %collective-permute-done.5.refs_0_.refs_2_.refs_1_, ...), custom_call_target="tpu_custom_call" | custom-call | flops 402653184 | bytes 6291456 | tf_op jit(solution)/shard_map/expert_pass/pallas_call | solution.py:87
  40.4 1.7 %collective-permute-done.22.refs_4_.a = bf16[32,2048]{1,0:T(8,128)(2,1)S(1)} collective-permute-done((bf16[32,2048]{1,0:T(8,128)(2,1)S(1)}, bf16[32,2048]{1,0:T(8,128)(2,1)S(1)}, u32[]{:S(2)}, u32[]{:S(2)}) %collective-permute-start.22) | collective-permute-done | bytes 131104 | tf_op jit(solution)/shard_map/ppermute | solution.py:270
  42.2 1.0 %collective-permute-start.23 = (bf16[32,2048]{1,0:T(8,128)(2,1)S(1)}, bf16[32,2048]{1,0:T(8,128)(2,1)S(1)}, u32[]{:S(2)}, u32[]{:S(2)}) collective-permute-start(bf16[32,2048]{1,0:T(8,128)(2,1)S(1)} %add.10), channel_id=1, source_target_pairs={{0,8},{2,4},{4,2},{6,14},{8,0},{10,12},{12,10},{14,6},{16,24},{18,... | collective-permute-start | bytes 393224 | tf_op jit(solution)/shard_map/ppermute | solution.py:273
  43.3 1.6 %collective-permute-start.29 = (bf16[32,2048]{1,0:T(8,128)(2,1)S(1)}, bf16[32,2048]{1,0:T(8,128)(2,1)S(1)}, u32[]{:S(2)}, u32[]{:S(2)}) collective-permute-start(bf16[32,2048]{1,0:T(8,128)(2,1)S(1)} %add.14), channel_id=1, source_target_pairs={{0,8},{2,4},{4,2},{6,14},{8,0},{10,12},{12,10},{14,6},{16,24},{18,... | collective-permute-start | bytes 393224 | tf_op jit(solution)/shard_map/ppermute | solution.py:273
  45.4 1.3 %expert_pass.11 = (bf16[32,2048]{1,0:T(8,128)(2,1)S(1)}, bf16[32,2048]{1,0:T(8,128)(2,1)S(1)}) custom-call(bf16[32,2048]{1,0:T(8,128)(2,1)S(1)} %collective-permute-done.21.refs_0_.a, bf16[32,2176]{1,0:T(8,128)(2,1)S(1)} %collective-permute-done.5.refs_0_.refs_2_.refs_1_, bf16[32,2176]{1,0:T(8,128)(2,1)S(1)} %collective-permute-done.refs_0_.refs_1_.refs_2_.refs_3_, ...), custom_call_target="tpu_custom_call" | custom-call | flops 402653184 | bytes 6291456 | tf_op jit(solution)/shard_map/expert_pass/pallas_call | solution.py:87
  46.7 1.9 %collective-permute-done.23.mid_a = bf16[32,2048]{1,0:T(8,128)(2,1)S(1)} collective-permute-done((bf16[32,2048]{1,0:T(8,128)(2,1)S(1)}, bf16[32,2048]{1,0:T(8,128)(2,1)S(1)}, u32[]{:S(2)}, u32[]{:S(2)}) %collective-permute-start.23) | collective-permute-done | bytes 131104 | tf_op jit(solution)/shard_map/ppermute | solution.py:273
  49.4 1.4 %collective-permute-start.25 = (bf16[32,2048]{1,0:T(8,128)(2,1)S(1)}, bf16[32,2048]{1,0:T(8,128)(2,1)S(1)}, u32[]{:S(2)}, u32[]{:S(2)}) collective-permute-start(bf16[32,2048]{1,0:T(8,128)(2,1)S(1)} %add.11), channel_id=1, source_target_pairs={{0,8},{2,4},{4,2},{6,14},{8,0},{10,12},{12,10},{14,6},{16,24},{18,... | collective-permute-start | bytes 393224 | tf_op jit(solution)/shard_map/ppermute | solution.py:273
  51.0 1.2 %collective-permute-done.28.far.a = bf16[32,2048]{1,0:T(8,128)(2,1)S(1)} collective-permute-done((bf16[32,2048]{1,0:T(8,128)(2,1)S(1)}, bf16[32,2048]{1,0:T(8,128)(2,1)S(1)}, u32[]{:S(2)}, u32[]{:S(2)}) %collective-permute-start.28) | collective-permute-done | bytes 131104 | tf_op jit(solution)/shard_map/ppermute | solution.py:270
  52.2 1.2 %collective-permute-start.31 = (bf16[32,2048]{1,0:T(8,128)(2,1)S(1)}, bf16[32,2048]{1,0:T(8,128)(2,1)S(1)}, u32[]{:S(2)}, u32[]{:S(2)}) collective-permute-start(bf16[32,2048]{1,0:T(8,128)(2,1)S(1)} %add.15), channel_id=1, source_target_pairs={{0,8},{2,4},{4,2},{6,14},{8,0},{10,12},{12,10},{14,6},{16,24},{18,... | collective-permute-start | bytes 393224 | tf_op jit(solution)/shard_map/ppermute | solution.py:273
  53.7 1.5 %collective-permute-done.24.outer = bf16[32,2048]{1,0:T(8,128)(2,1)S(1)} collective-permute-done((bf16[32,2048]{1,0:T(8,128)(2,1)S(1)}, bf16[32,2048]{1,0:T(8,128)(2,1)S(1)}, u32[]{:S(2)}, u32[]{:S(2)}) %collective-permute-start.24) | collective-permute-done | bytes 131104 | tf_op jit(solution)/shard_map/ppermute | solution.py:270
  55.3 1.4 %collective-permute-done.30.outer = bf16[32,2048]{1,0:T(8,128)(2,1)S(1)} collective-permute-done((bf16[32,2048]{1,0:T(8,128)(2,1)S(1)}, bf16[32,2048]{1,0:T(8,128)(2,1)S(1)}, u32[]{:S(2)}, u32[]{:S(2)}) %collective-permute-start.30) | collective-permute-done | bytes 131104 | tf_op jit(solution)/shard_map/ppermute | solution.py:270
  58.2 2.7 %collective-permute-done.33.refs_0_ = bf16[32,2048]{1,0:T(8,128)(2,1)S(1)} collective-permute-done((bf16[32,2048]{1,0:T(8,128)(2,1)S(1)}, bf16[32,2048]{1,0:T(8,128)(2,1)S(1)}, u32[]{:S(2)}, u32[]{:S(2)}) %collective-permute-start.33) | collective-permute-done | bytes 131104 | tf_op jit(solution)/shard_map/ppermute | solution.py:380
  60.9 1.4 %collective-permute-done.34.refs_1_ = bf16[32,2048]{1,0:T(8,128)(2,1)S(1)} collective-permute-done((bf16[32,2048]{1,0:T(8,128)(2,1)S(1)}, bf16[32,2048]{1,0:T(8,128)(2,1)S(1)}, u32[]{:S(2)}, u32[]{:S(2)}) %collective-permute-start.34) | collective-permute-done | bytes 131104 | tf_op jit(solution)/shard_map/ppermute | solution.py:380
  (75 shorter events, 15.8 us)
Async XLA Ops:
  1.8 6.6 %collective-permute-start.2 = (bf16[32,2176]{1,0:T(8,128)(2,1)S(1)}, bf16[32,2176]{1,0:T(8,128)(2,1)S(1)}, u32[]{:S(2)}, u32[]{:S(2)}) collective-permute-start(bf16[32,2176]{1,0:T(8,128)(2,1)S(1)} %get-tuple-element.37.refs_8_), channel_id=1, source_target_pairs={{0,8},{2,4},{4,2},{6,14},{8,0},{10,12},{12,10},{14,6},{16,24},{18,... | collective-permute-start | bytes 417800 | tf_op jit(solution)/shard_map/ppermute | solution.py:273
  3.5 6.7 %collective-permute-start = (bf16[32,2176]{1,0:T(8,128)(2,1)S(1)}, bf16[32,2176]{1,0:T(8,128)(2,1)S(1)}, u32[]{:S(2)}, u32[]{:S(2)}) collective-permute-start(bf16[32,2176]{1,0:T(8,128)(2,1)S(1)} %get-tuple-element.37.refs_8_), channel_id=1, source_target_pairs={{0,2},{2,0},{4,6},{6,4},{8,10},{10,8},{12,14},{14,12},{16,18},{18,... | collective-permute-start | bytes 417800 | tf_op jit(solution)/shard_map/ppermute | solution.py:270
  3.5 7.1 %collective-permute-start.6 = (bf16[32,2176]{1,0:T(8,128)(2,1)S(1)}, bf16[32,2176]{1,0:T(8,128)(2,1)S(1)}, u32[]{:S(2)}, u32[]{:S(2)}) collective-permute-start(bf16[32,2176]{1,0:T(8,128)(2,1)S(1)} %get-tuple-element.38.refs_10_), channel_id=1, source_target_pairs={{0,8},{2,4},{4,2},{6,14},{8,0},{10,12},{12,10},{14,6},{16,24},{18,... | collective-permute-start | bytes 417800 | tf_op jit(solution)/shard_map/ppermute | solution.py:273
  5.1 6.7 %collective-permute-start.1 = (bf16[32,2176]{1,0:T(8,128)(2,1)S(1)}, bf16[32,2176]{1,0:T(8,128)(2,1)S(1)}, u32[]{:S(2)}, u32[]{:S(2)}) collective-permute-start(bf16[32,2176]{1,0:T(8,128)(2,1)S(1)} %get-tuple-element.38.refs_10_), channel_id=1, source_target_pairs={{0,2},{2,0},{4,6},{6,4},{8,10},{10,8},{12,14},{14,12},{16,18},{18,... | collective-permute-start | bytes 417800 | tf_op jit(solution)/shard_map/ppermute | solution.py:270
  8.5 6.6 %collective-permute-start.5 = (bf16[32,2176]{1,0:T(8,128)(2,1)S(1)}, bf16[32,2176]{1,0:T(8,128)(2,1)S(1)}, u32[]{:S(2)}, u32[]{:S(2)}) collective-permute-start(bf16[32,2176]{1,0:T(8,128)(2,1)S(1)} %choose.11), channel_id=1, source_target_pairs={{0,2},{2,0},{4,6},{6,4},{8,10},{10,8},{12,14},{14,12},{16,18},{18,... | collective-permute-start | bytes 417800 | tf_op jit(solution)/shard_map/ppermute | solution.py:270
  10.1 6.4 %collective-permute-start.3 = (bf16[32,2176]{1,0:T(8,128)(2,1)S(1)}, bf16[32,2176]{1,0:T(8,128)(2,1)S(1)}, u32[]{:S(2)}, u32[]{:S(2)}) collective-permute-start(bf16[32,2176]{1,0:T(8,128)(2,1)S(1)} %collective-permute-done.refs_0_.refs_1_.refs_2_.refs_3_), channel_id=1, source_target_pairs={{0,8},{2,4},{4,2},{6,14},{8,0},{10,12},{12,10},{14,6},{16,24},{18,... | collective-permute-start | bytes 417800 | tf_op jit(solution)/shard_map/ppermute | solution.py:273
  10.6 7.0 %collective-permute-start.7 = (bf16[32,2176]{1,0:T(8,128)(2,1)S(1)}, bf16[32,2176]{1,0:T(8,128)(2,1)S(1)}, u32[]{:S(2)}, u32[]{:S(2)}) collective-permute-start(bf16[32,2176]{1,0:T(8,128)(2,1)S(1)} %choose.12), channel_id=1, source_target_pairs={{0,2},{2,0},{4,6},{6,4},{8,10},{10,8},{12,14},{14,12},{16,18},{18,... | collective-permute-start | bytes 417800 | tf_op jit(solution)/shard_map/ppermute | solution.py:270
  11.8 7.5 %collective-permute-start.10 = (bf16[32,2176]{1,0:T(8,128)(2,1)S(1)}, bf16[32,2176]{1,0:T(8,128)(2,1)S(1)}, u32[]{:S(2)}, u32[]{:S(2)}) collective-permute-start(bf16[32,2176]{1,0:T(8,128)(2,1)S(1)} %collective-permute-done.1.refs_4_.refs_5_.refs_6_.refs_7_), channel_id=1, source_target_pairs={{0,8},{2,4},{4,2},{6,14},{8,0},{10,12},{12,10},{14,6},{16,24},{18,... | collective-permute-start | bytes 417800 | tf_op jit(solution)/shard_map/ppermute | solution.py:273
  15.1 7.2 %collective-permute-start.8 = (bf16[32,2176]{1,0:T(8,128)(2,1)S(1)}, bf16[32,2176]{1,0:T(8,128)(2,1)S(1)}, u32[]{:S(2)}, u32[]{:S(2)}) collective-permute-start(bf16[32,2176]{1,0:T(8,128)(2,1)S(1)} %collective-permute-done.5.refs_0_.refs_2_.refs_1_), channel_id=1, source_target_pairs={{0,8},{2,4},{4,2},{6,14},{8,0},{10,12},{12,10},{14,6},{16,24},{18,... | collective-permute-start | bytes 417800 | tf_op jit(solution)/shard_map/ppermute | solution.py:273
  16.6 6.6 %collective-permute-start.4 = (bf16[32,2176]{1,0:T(8,128)(2,1)S(1)}, bf16[32,2176]{1,0:T(8,128)(2,1)S(1)}, u32[]{:S(2)}, u32[]{:S(2)}) collective-permute-start(bf16[32,2176]{1,0:T(8,128)(2,1)S(1)} %choose.10), channel_id=1, source_target_pairs={{0,2},{2,0},{4,6},{6,4},{8,10},{10,8},{12,14},{14,12},{16,18},{18,... | collective-permute-start | bytes 417800 | tf_op jit(solution)/shard_map/ppermute | solution.py:270
  17.5 7.6 %collective-permute-start.12 = (bf16[32,2176]{1,0:T(8,128)(2,1)S(1)}, bf16[32,2176]{1,0:T(8,128)(2,1)S(1)}, u32[]{:S(2)}, u32[]{:S(2)}) collective-permute-start(bf16[32,2176]{1,0:T(8,128)(2,1)S(1)} %collective-permute-done.7.refs_4_.refs_6_.refs_5_), channel_id=1, source_target_pairs={{0,8},{2,4},{4,2},{6,14},{8,0},{10,12},{12,10},{14,6},{16,24},{18,... | collective-permute-start | bytes 417800 | tf_op jit(solution)/shard_map/ppermute | solution.py:273
  19.3 6.0 %collective-permute-start.11 = (bf16[32,2176]{1,0:T(8,128)(2,1)S(1)}, bf16[32,2176]{1,0:T(8,128)(2,1)S(1)}, u32[]{:S(2)}, u32[]{:S(2)}) collective-permute-start(bf16[32,2176]{1,0:T(8,128)(2,1)S(1)} %choose.14), channel_id=1, source_target_pairs={{0,2},{2,0},{4,6},{6,4},{8,10},{10,8},{12,14},{14,12},{16,18},{18,... | collective-permute-start | bytes 417800 | tf_op jit(solution)/shard_map/ppermute | solution.py:270
  19.3 8.7 %collective-permute-start.14 = (bf16[32,2048]{1,0:T(8,128)(2,1)S(1)}, bf16[32,2048]{1,0:T(8,128)(2,1)S(1)}, u32[]{:S(2)}, u32[]{:S(2)}) collective-permute-start(bf16[32,2048]{1,0:T(8,128)(2,1)S(1)} %get-tuple-element.46.at_end.refs_9_.at_mid), channel_id=1, source_target_pairs={{0,8},{2,4},{4,2},{6,14},{8,0},{10,12},{12,10},{14,6},{16,24},{18,... | collective-permute-start | bytes 393224 | tf_op jit(solution)/shard_map/ppermute | solution.py:273
  23.2 6.3 %collective-permute-start.9 = (bf16[32,2048]{1,0:T(8,128)(2,1)S(1)}, bf16[32,2048]{1,0:T(8,128)(2,1)S(1)}, u32[]{:S(2)}, u32[]{:S(2)}) collective-permute-start(bf16[32,2048]{1,0:T(8,128)(2,1)S(1)} %choose.13), channel_id=1, source_target_pairs={{0,2},{2,0},{4,6},{6,4},{8,10},{10,8},{12,14},{14,12},{16,18},{18,... | collective-permute-start | bytes 393224 | tf_op jit(solution)/shard_map/ppermute | solution.py:270
  23.3 6.3 %collective-permute-start.16 = (bf16[32,2048]{1,0:T(8,128)(2,1)S(1)}, bf16[32,2048]{1,0:T(8,128)(2,1)S(1)}, u32[]{:S(2)}, u32[]{:S(2)}) collective-permute-start(bf16[32,2048]{1,0:T(8,128)(2,1)S(1)} %get-tuple-element.48.at_end.refs_11_.at_mid), channel_id=1, source_target_pairs={{0,8},{2,4},{4,2},{6,14},{8,0},{10,12},{12,10},{14,6},{16,24},{18,... | collective-permute-start | bytes 393224 | tf_op jit(solution)/shard_map/ppermute | solution.py:273
  25.3 6.9 %collective-permute-start.13 = (bf16[32,2048]{1,0:T(8,128)(2,1)S(1)}, bf16[32,2048]{1,0:T(8,128)(2,1)S(1)}, u32[]{:S(2)}, u32[]{:S(2)}) collective-permute-start(bf16[32,2048]{1,0:T(8,128)(2,1)S(1)} %choose.15), channel_id=1, source_target_pairs={{0,2},{2,0},{4,6},{6,4},{8,10},{10,8},{12,14},{14,12},{16,18},{18,... | collective-permute-start | bytes 393224 | tf_op jit(solution)/shard_map/ppermute | solution.py:270
  28.0 7.0 %collective-permute-start.15 = (bf16[32,2048]{1,0:T(8,128)(2,1)S(1)}, bf16[32,2048]{1,0:T(8,128)(2,1)S(1)}, u32[]{:S(2)}, u32[]{:S(2)}) collective-permute-start(bf16[32,2048]{1,0:T(8,128)(2,1)S(1)} %choose.16), channel_id=1, source_target_pairs={{0,2},{2,0},{4,6},{6,4},{8,10},{10,8},{12,14},{14,12},{16,18},{18,... | collective-permute-start | bytes 393224 | tf_op jit(solution)/shard_map/ppermute | solution.py:270
  29.5 6.6 %collective-permute-start.18 = (bf16[32,2048]{1,0:T(8,128)(2,1)S(1)}, bf16[32,2048]{1,0:T(8,128)(2,1)S(1)}, u32[]{:S(2)}, u32[]{:S(2)}) collective-permute-start(bf16[32,2048]{1,0:T(8,128)(2,1)S(1)} %add.8), channel_id=1, source_target_pairs={{0,8},{2,4},{4,2},{6,14},{8,0},{10,12},{12,10},{14,6},{16,24},{18,... | collective-permute-start | bytes 393224 | tf_op jit(solution)/shard_map/ppermute | solution.py:273
  29.6 8.5 %collective-permute-start.17 = (bf16[32,2048]{1,0:T(8,128)(2,1)S(1)}, bf16[32,2048]{1,0:T(8,128)(2,1)S(1)}, u32[]{:S(2)}, u32[]{:S(2)}) collective-permute-start(bf16[32,2048]{1,0:T(8,128)(2,1)S(1)} %choose.17), channel_id=1, source_target_pairs={{0,2},{2,0},{4,6},{6,4},{8,10},{10,8},{12,14},{14,12},{16,18},{18,... | collective-permute-start | bytes 393224 | tf_op jit(solution)/shard_map/ppermute | solution.py:270
  32.2 6.0 %collective-permute-start.26 = (bf16[32,2048]{1,0:T(8,128)(2,1)S(1)}, bf16[32,2048]{1,0:T(8,128)(2,1)S(1)}, u32[]{:S(2)}, u32[]{:S(2)}) collective-permute-start(bf16[32,2048]{1,0:T(8,128)(2,1)S(1)} %add.12), channel_id=1, source_target_pairs={{0,8},{2,4},{4,2},{6,14},{8,0},{10,12},{12,10},{14,6},{16,24},{18,... | collective-permute-start | bytes 393224 | tf_op jit(solution)/shard_map/ppermute | solution.py:273
  33.9 6.5 %collective-permute-start.21 = (bf16[32,2048]{1,0:T(8,128)(2,1)S(1)}, bf16[32,2048]{1,0:T(8,128)(2,1)S(1)}, u32[]{:S(2)}, u32[]{:S(2)}) collective-permute-start(bf16[32,2048]{1,0:T(8,128)(2,1)S(1)} %choose.18), channel_id=1, source_target_pairs={{0,2},{2,0},{4,6},{6,4},{8,10},{10,8},{12,14},{14,12},{16,18},{18,... | collective-permute-start | bytes 393224 | tf_op jit(solution)/shard_map/ppermute | solution.py:270
  35.0 7.1 %collective-permute-start.22 = (bf16[32,2048]{1,0:T(8,128)(2,1)S(1)}, bf16[32,2048]{1,0:T(8,128)(2,1)S(1)}, u32[]{:S(2)}, u32[]{:S(2)}) collective-permute-start(bf16[32,2048]{1,0:T(8,128)(2,1)S(1)} %choose.19), channel_id=1, source_target_pairs={{0,2},{2,0},{4,6},{6,4},{8,10},{10,8},{12,14},{14,12},{16,18},{18,... | collective-permute-start | bytes 393224 | tf_op jit(solution)/shard_map/ppermute | solution.py:270
  36.1 6.0 %collective-permute-start.19 = (bf16[32,2048]{1,0:T(8,128)(2,1)S(1)}, bf16[32,2048]{1,0:T(8,128)(2,1)S(1)}, u32[]{:S(2)}, u32[]{:S(2)}) collective-permute-start(bf16[32,2048]{1,0:T(8,128)(2,1)S(1)} %add.9), channel_id=1, source_target_pairs={{0,8},{2,4},{4,2},{6,14},{8,0},{10,12},{12,10},{14,6},{16,24},{18,... | collective-permute-start | bytes 393224 | tf_op jit(solution)/shard_map/ppermute | solution.py:273
  42.2 6.4 %collective-permute-start.23 = (bf16[32,2048]{1,0:T(8,128)(2,1)S(1)}, bf16[32,2048]{1,0:T(8,128)(2,1)S(1)}, u32[]{:S(2)}, u32[]{:S(2)}) collective-permute-start(bf16[32,2048]{1,0:T(8,128)(2,1)S(1)} %add.10), channel_id=1, source_target_pairs={{0,8},{2,4},{4,2},{6,14},{8,0},{10,12},{12,10},{14,6},{16,24},{18,... | collective-permute-start | bytes 393224 | tf_op jit(solution)/shard_map/ppermute | solution.py:273
  43.2 6.2 %collective-permute-start.20 = (bf16[32,2048]{1,0:T(8,128)(2,1)S(1)}, bf16[32,2048]{1,0:T(8,128)(2,1)S(1)}, u32[]{:S(2)}, u32[]{:S(2)}) collective-permute-start(bf16[32,2048]{1,0:T(8,128)(2,1)S(1)} %choose_sum.4), channel_id=1, source_target_pairs={{0,2},{2,0},{4,6},{6,4},{8,10},{10,8},{12,14},{14,12},{16,18},{18,... | collective-permute-start | bytes 393224 | tf_op jit(solution)/shard_map/ppermute | solution.py:270
  43.3 7.5 %collective-permute-start.29 = (bf16[32,2048]{1,0:T(8,128)(2,1)S(1)}, bf16[32,2048]{1,0:T(8,128)(2,1)S(1)}, u32[]{:S(2)}, u32[]{:S(2)}) collective-permute-start(bf16[32,2048]{1,0:T(8,128)(2,1)S(1)} %add.14), channel_id=1, source_target_pairs={{0,8},{2,4},{4,2},{6,14},{8,0},{10,12},{12,10},{14,6},{16,24},{18,... | collective-permute-start | bytes 393224 | tf_op jit(solution)/shard_map/ppermute | solution.py:273
  44.9 7.3 %collective-permute-start.28 = (bf16[32,2048]{1,0:T(8,128)(2,1)S(1)}, bf16[32,2048]{1,0:T(8,128)(2,1)S(1)}, u32[]{:S(2)}, u32[]{:S(2)}) collective-permute-start(bf16[32,2048]{1,0:T(8,128)(2,1)S(1)} %choose_sum.6), channel_id=1, source_target_pairs={{0,2},{2,0},{4,6},{6,4},{8,10},{10,8},{12,14},{14,12},{16,18},{18,... | collective-permute-start | bytes 393224 | tf_op jit(solution)/shard_map/ppermute | solution.py:270
  48.6 6.5 %collective-permute-start.24 = (bf16[32,2048]{1,0:T(8,128)(2,1)S(1)}, bf16[32,2048]{1,0:T(8,128)(2,1)S(1)}, u32[]{:S(2)}, u32[]{:S(2)}) collective-permute-start(bf16[32,2048]{1,0:T(8,128)(2,1)S(1)} %choose_sum.5), channel_id=1, source_target_pairs={{0,2},{2,0},{4,6},{6,4},{8,10},{10,8},{12,14},{14,12},{16,18},{18,... | collective-permute-start | bytes 393224 | tf_op jit(solution)/shard_map/ppermute | solution.py:270
  49.4 5.7 %collective-permute-start.25 = (bf16[32,2048]{1,0:T(8,128)(2,1)S(1)}, bf16[32,2048]{1,0:T(8,128)(2,1)S(1)}, u32[]{:S(2)}, u32[]{:S(2)}) collective-permute-start(bf16[32,2048]{1,0:T(8,128)(2,1)S(1)} %add.11), channel_id=1, source_target_pairs={{0,8},{2,4},{4,2},{6,14},{8,0},{10,12},{12,10},{14,6},{16,24},{18,... | collective-permute-start | bytes 393224 | tf_op jit(solution)/shard_map/ppermute | solution.py:273
  50.8 5.8 %collective-permute-start.30 = (bf16[32,2048]{1,0:T(8,128)(2,1)S(1)}, bf16[32,2048]{1,0:T(8,128)(2,1)S(1)}, u32[]{:S(2)}, u32[]{:S(2)}) collective-permute-start(bf16[32,2048]{1,0:T(8,128)(2,1)S(1)} %choose_sum.7), channel_id=1, source_target_pairs={{0,2},{2,0},{4,6},{6,4},{8,10},{10,8},{12,14},{14,12},{16,18},{18,... | collective-permute-start | bytes 393224 | tf_op jit(solution)/shard_map/ppermute | solution.py:270
  53.6 8.7 %collective-permute-start.32 = (bf16[64,2048]{1,0:T(8,128)(2,1)S(1)}, bf16[64,2048]{1,0:T(8,128)(2,1)S(1)}, u32[]{:S(2)}, u32[]{:S(2)}) collective-permute-start(bf16[64,2048]{1,0:T(8,128)(2,1)S(1)} %join_two.1), channel_id=1, source_target_pairs={{0,8},{8,16},{16,24},{24,0},{1,9},{9,17},{17,25},{25,1},{2,10},{10... | collective-permute-start | bytes 786440 | tf_op jit(solution)/shard_map/ppermute | solution.py:379
  55.2 5.7 %collective-permute-start.33 = (bf16[32,2048]{1,0:T(8,128)(2,1)S(1)}, bf16[32,2048]{1,0:T(8,128)(2,1)S(1)}, u32[]{:S(2)}, u32[]{:S(2)}) collective-permute-start(bf16[32,2048]{1,0:T(8,128)(2,1)S(1)} %finish_second.2.refs_1_), channel_id=1, source_target_pairs={{0,8},{8,16},{16,24},{24,0},{1,9},{9,17},{17,25},{25,1},{2,10},{10... | collective-permute-start | bytes 393224 | tf_op jit(solution)/shard_map/ppermute | solution.py:380
  (3 other events, 15.0 us)

commit v7 on v6

--- a/solution.py
+++ b/solution.py
@@ -236,18 +236,22 @@
     result[half:] = b[...]
 
 
-def join_apart(firsts, *refs):
-    half = firsts.shape[0] // 2
-    join_handed(firsts.at[:half], refs[0], firsts.at[half:], *refs[1:])
-
-
-def join_handed(*refs):
-    @pl.when(lax.axis_index("section") == 0)
+def join_handed(firsts, *refs):
+    seconds, (whole, zeros, sems) = refs[:STREAMS], refs[STREAMS:]
+    piece = seconds[0].shape[0]
+    nothing = lax.axis_index("section") == 0
+
+    @pl.when(nothing)
     def _():
-        for ref in refs[:-2]:
-            ref[...] = jnp.zeros_like(ref)
-
-    join(*refs)
+        zeros[...] = jnp.zeros_like(zeros)
+        join(*[zeros] * (2 * STREAMS), whole, sems)
+
+    @pl.when(~nothing)
+    def _():
+        parts = []
+        for s in range(STREAMS):
+            parts += [firsts.at[pl.ds(s * piece, piece)], seconds[s]]
+        join(*parts, whole, sems)
 
 
 def on_line(tokens, routes, route_weights, expert_gate, expert_up, expert_down):
@@ -295,10 +299,10 @@
     def swap(k, s, to_outer, to_inner):
         if k == 3:
             o[s][k - 1], to_outer = lax.optimization_barrier((o[s][k - 1], to_outer))
-        if k in (5, 6):
+        if k in (5, 6, 7):
             i[s][k - 1], to_inner = lax.optimization_barrier((i[s][k - 1], to_inner))
-        if s == 1 and k == 4:
-            to_outer, _ = lax.optimization_barrier((to_outer, sent[0]))
+        if k == 7:
+            to_outer, to_inner = lax.optimization_barrier((to_outer, to_inner))
         sent[:] = [to_outer, to_inner]
         o[s][k], i[s][k] = outer(to_outer), inner(to_inner)
 
@@ -335,13 +339,14 @@
     p[1] = expert(False, lambda s: (o[s][0],) * 4)
     for s in both:
         swap(2, s, mixed(choose, p[1][s], i[s][1], shape=tagged), o[s][1])
-    p[2] = expert(False, lambda s: (o[s][1], i[s][0]) * 2)
+    *p[2], total = expert(False, lambda s: (o[s][1], i[s][0]) * 2, *pieces)
     for s in both:
         swap(3, s, mixed(choose, p[2][s], i[s][2]), second[s])
     p[3] = expert(False, lambda s: (o[s][2], i[s][1]) * 2)
     for s in both:
         swap(4, s, mixed(choose, p[3][s], i[s][3]), mixed(add, o[s][3], p[2][s]))
-    *p[4], total = expert(True, lambda s: (o[s][3], i[s][2], o[s][2], i[s][1]), *pieces)
+    o[1][3], _ = lax.optimization_barrier((o[1][3], sent[1]))
+    p[4] = expert(True, lambda s: (o[s][3], i[s][2], o[s][2], i[s][1]))
     for s in both:
         swap(5, s, mixed(choose, p[4][s], second[s]), mixed(add, o[s][4], p[3][s]))
     p[5] = expert(True, lambda s: (o[s][4], i[s][3], o[s][1], i[s][0]))
@@ -363,13 +368,13 @@
         )
         done[2 * s] = firsts[s]
 
-    def joined(body, parts):
+    def joined(body, parts, *scratch):
         return run(
             body,
             body.__name__,
             jax.ShapeDtypeStruct((count, width), jnp.bfloat16),
             *parts,
-            scratch=[pltpu.SemaphoreType.DMA((2 * STREAMS,))],
+            scratch=[*scratch, pltpu.SemaphoreType.DMA((2 * STREAMS,))],
             out_specs=ANYWHERE,
         )
 
@@ -378,7 +383,7 @@
     one = run(join_two, "join_two", held((2 * piece, width)), firsts[0], firsts[1])
     back = lax.ppermute(one, "section", ring)
     given = [back, *(lax.ppermute(done[k], "section", ring) for k in (1, 3))]
-    handed = joined(join_apart, given)
+    handed = joined(join_handed, given, held(block))
     return (joined(join, done)[None], handed[None])
 
 

time: 63.9 us -> 62.3 us (0.975)
  waiting for transfers between devices: 24.6 us -> 16.2 us
  starting transfers between devices: 23.1 us -> 29.5 us
    ppermute x16, starting transfers between devices: 16.3 us -> 25.7 us  [inner(): return lax.ppermute(value, axes, inner_pairs)]
    ppermute x16, waiting for transfers between devices: 14.4 us -> 5.74 us  [outer(): return lax.ppermute(value, axes, outer_pairs)]
    ppermute x16, starting transfers between devices: 6.64 us -> 3.63 us  [outer(): return lax.ppermute(value, axes, outer_pairs)]
  transfers between devices with their start and end apart: 35 -> 35, of which waited for: 22 -> 14; matrix products, arithmetic and copies ran while one was open for 0% -> 0% of each run, Pallas kernels for 20% -> 20%
where the time goes in v7:
time: 62.3 us; the launch traced here: 61.2 us
  starting transfers between devices  29.5 us (47%)
  waiting for transfers between devices  16.2 us (26%)
  Pallas kernels  14.5 us (23%)
  between operations  1 us (2%)
    ppermute x16, starting transfers between devices, inner(): return lax.ppermute(value, axes, inner_pairs)  25.7 us
    pallas_call x37, Pallas kernels, run(): pl.pallas_call(body, out_shape=out_shape, in_specs=specs, out_specs=out_s...  14.5 us
    ppermute x16, waiting for transfers between devices, inner(): return lax.ppermute(value, axes, inner_pairs)  6.62 us
    ppermute x16, waiting for transfers between devices, outer(): return lax.ppermute(value, axes, outer_pairs)  5.74 us
    ppermute x2, waiting for transfers between devices, on_line(): given = [back, *(lax.ppermute(done[k], 'section', ring) for k in (1, 3))]  3.81 us
    ppermute x16, starting transfers between devices, outer(): return lax.ppermute(value, axes, outer_pairs)  3.63 us
  transfers between devices with their start and end apart: 35, of which 14 were waited for; matrix products, arithmetic and copies ran while one was open for 0% of the time, Pallas kernels for 20%

profile of v7, /device:TPU:12, one launch (start us, length us, event | category | flops | bytes accessed | tf_op | source)
XLA Modules:
  0.0 61.2 jit_solution(7896629863721410873)
XLA Ops:
  0.6 1.2 %prepare.1 = (bf16[32,2176]{1,0:T(8,128)(2,1)S(1)}, bf16[32,2048]{1,0:T(8,128)(2,1)S(1)}, bf16[32,2176]{1,0:T(8,128)(2,1)S(1)}, bf16[32,2048]{1,0:T(8,128)(2,1)S(1)}) custom-call(bf16[128,2048]{1,0:T(8,128)(2,1)} %bitcast.15, s32[2,128]{1,0:T(2,128)} %bitcast.18, f32[2,128]{1,0:T(2,128)} %bitcast.19), custom_call_target="tpu_custom_call" | custom-call | tf_op jit(solution)/shard_map/prepare/pallas_call | solution.py:87
  1.8 1.6 %collective-permute-start.2 = (bf16[32,2176]{1,0:T(8,128)(2,1)S(1)}, bf16[32,2176]{1,0:T(8,128)(2,1)S(1)}, u32[]{:S(2)}, u32[]{:S(2)}) collective-permute-start(bf16[32,2176]{1,0:T(8,128)(2,1)S(1)} %get-tuple-element.50.refs_10_), channel_id=1, source_target_pairs={{0,8},{2,4},{4,2},{6,14},{8,0},{10,12},{12,10},{14,6},{16,24},{18,... | collective-permute-start | bytes 417800 | tf_op jit(solution)/shard_map/ppermute | solution.py:277
  3.5 1.7 %collective-permute-start = (bf16[32,2176]{1,0:T(8,128)(2,1)S(1)}, bf16[32,2176]{1,0:T(8,128)(2,1)S(1)}, u32[]{:S(2)}, u32[]{:S(2)}) collective-permute-start(bf16[32,2176]{1,0:T(8,128)(2,1)S(1)} %get-tuple-element.44.refs_8_), channel_id=1, source_target_pairs={{0,8},{2,4},{4,2},{6,14},{8,0},{10,12},{12,10},{14,6},{16,24},{18,... | collective-permute-start | bytes 417800 | tf_op jit(solution)/shard_map/ppermute | solution.py:277
  5.5 3.0 %collective-permute-done.2.at_mid.refs_5_.refs_7_ = bf16[32,2176]{1,0:T(8,128)(2,1)S(1)} collective-permute-done((bf16[32,2176]{1,0:T(8,128)(2,1)S(1)}, bf16[32,2176]{1,0:T(8,128)(2,1)S(1)}, u32[]{:S(2)}, u32[]{:S(2)}) %collective-permute-start.2) | collective-permute-done | bytes 139296 | tf_op jit(solution)/shard_map/ppermute | solution.py:277
  8.6 1.1 %collective-permute-done.5.refs_4_.refs_5_.refs_6_.refs_7_ = bf16[32,2176]{1,0:T(8,128)(2,1)S(1)} collective-permute-done((bf16[32,2176]{1,0:T(8,128)(2,1)S(1)}, bf16[32,2176]{1,0:T(8,128)(2,1)S(1)}, u32[]{:S(2)}, u32[]{:S(2)}) %collective-permute-start.5) | collective-permute-done | bytes 139296 | tf_op jit(solution)/shard_map/ppermute | solution.py:274
  9.6 0.8 %collective-permute-start.9 = (bf16[32,2176]{1,0:T(8,128)(2,1)S(1)}, bf16[32,2176]{1,0:T(8,128)(2,1)S(1)}, u32[]{:S(2)}, u32[]{:S(2)}) collective-permute-start(bf16[32,2176]{1,0:T(8,128)(2,1)S(1)} %collective-permute-done.5.refs_4_.refs_5_.refs_6_.refs_7_), channel_id=1, source_target_pairs={{0,8},{2,4},{4,2},{6,14},{8,0},{10,12},{12,10},{14,6},{16,24},{18,... | collective-permute-start | bytes 417800 | tf_op jit(solution)/shard_map/ppermute | solution.py:277
  10.5 2.9 %load.1 = (bf16[2048,512]{1,0:T(8,128)(2,1)S(1)}, bf16[2048,512]{1,0:T(8,128)(2,1)S(1)}, bf16[512,2048]{1,0:T(8,128)(2,1)S(1)}) custom-call(bf16[2048,512]{1,0:T(8,128)(2,1)} %bitcast.12, bf16[2048,512]{1,0:T(8,128)(2,1)} %bitcast.13, bf16[512,2048]{1,0:T(8,128)(2,1)} %bitcast.14), custom_call_target="tpu_custom_call" | custom-call | bytes 6291456 | tf_op jit(solution)/shard_map/load/pallas_call | solution.py:87
  13.6 1.4 %collective-permute-start.6 = (bf16[32,2176]{1,0:T(8,128)(2,1)S(1)}, bf16[32,2176]{1,0:T(8,128)(2,1)S(1)}, u32[]{:S(2)}, u32[]{:S(2)}) collective-permute-start(bf16[32,2176]{1,0:T(8,128)(2,1)S(1)} %collective-permute-done.4.refs_0_.refs_1_.refs_2_.refs_3_), channel_id=1, source_target_pairs={{0,8},{2,4},{4,2},{6,14},{8,0},{10,12},{12,10},{14,6},{16,24},{18,... | collective-permute-start | bytes 417800 | tf_op jit(solution)/shard_map/ppermute | solution.py:277
  15.0 1.3 %expert_pass.7 = (bf16[32,2048]{1,0:T(8,128)(2,1)S(1)}, bf16[32,2048]{1,0:T(8,128)(2,1)S(1)}) custom-call(bf16[32,2176]{1,0:T(8,128)(2,1)S(1)} %collective-permute-done.4.refs_0_.refs_1_.refs_2_.refs_3_, bf16[32,2176]{1,0:T(8,128)(2,1)S(1)} %collective-permute-done.4.refs_0_.refs_1_.refs_2_.refs_3_, ...), custom_call_target="tpu_custom_call" | custom-call | flops 402653184 | bytes 6291456 | tf_op jit(solution)/shard_map/expert_pass/pallas_call | solution.py:87
  17.5 1.1 %collective-permute-done.1.refs_0_.refs_2_.refs_1_ = bf16[32,2176]{1,0:T(8,128)(2,1)S(1)} collective-permute-done((bf16[32,2176]{1,0:T(8,128)(2,1)S(1)}, bf16[32,2176]{1,0:T(8,128)(2,1)S(1)}, u32[]{:S(2)}, u32[]{:S(2)}) %collective-permute-start.1) | collective-permute-done | bytes 139296 | tf_op jit(solution)/shard_map/ppermute | solution.py:274
  18.5 1.2 %collective-permute-start.8 = (bf16[32,2176]{1,0:T(8,128)(2,1)S(1)}, bf16[32,2176]{1,0:T(8,128)(2,1)S(1)}, u32[]{:S(2)}, u32[]{:S(2)}) collective-permute-start(bf16[32,2176]{1,0:T(8,128)(2,1)S(1)} %collective-permute-done.1.refs_0_.refs_2_.refs_1_), channel_id=1, source_target_pairs={{0,8},{2,4},{4,2},{6,14},{8,0},{10,12},{12,10},{14,6},{16,24},{18,... | collective-permute-start | bytes 417800 | tf_op jit(solution)/shard_map/ppermute | solution.py:277
  19.9 1.8 %collective-permute-start.14 = (bf16[32,2048]{1,0:T(8,128)(2,1)S(1)}, bf16[32,2048]{1,0:T(8,128)(2,1)S(1)}, u32[]{:S(2)}, u32[]{:S(2)}) collective-permute-start(bf16[32,2048]{1,0:T(8,128)(2,1)S(1)} %get-tuple-element.49.at_end.refs_11_.at_mid), channel_id=1, source_target_pairs={{0,8},{2,4},{4,2},{6,14},{8,0},{10,12},{12,10},{14,6},{16,24},{18,... | collective-permute-start | bytes 393224 | tf_op jit(solution)/shard_map/ppermute | solution.py:277
  21.7 1.5 %expert_pass.6 = (bf16[32,2048]{1,0:T(8,128)(2,1)S(1)}, bf16[32,2048]{1,0:T(8,128)(2,1)S(1)}, f32[128,2048]{1,0:T(8,128)S(1)}) custom-call(bf16[32,2176]{1,0:T(8,128)(2,1)S(1)} %collective-permute-done.1.refs_0_.refs_2_.refs_1_, bf16[32,2176]{1,0:T(8,128)(2,1)S(1)} %collective-permute-done.at_mid.refs_1_.refs_3_, ...), custom_call_target="tpu_custom_call" | custom-call | flops 1207959552 | bytes 6291456 | tf_op jit(solution)/shard_map/expert_pass/pallas_call | solution.py:87
  23.6 1.8 %collective-permute-start.12 = (bf16[32,2048]{1,0:T(8,128)(2,1)S(1)}, bf16[32,2048]{1,0:T(8,128)(2,1)S(1)}, u32[]{:S(2)}, u32[]{:S(2)}) collective-permute-start(bf16[32,2048]{1,0:T(8,128)(2,1)S(1)} %get-tuple-element.43.at_end.refs_9_.at_mid), channel_id=1, source_target_pairs={{0,8},{2,4},{4,2},{6,14},{8,0},{10,12},{12,10},{14,6},{16,24},{18,... | collective-permute-start | bytes 393224 | tf_op jit(solution)/shard_map/ppermute | solution.py:277
  26.1 1.3 %expert_pass.8 = (bf16[32,2048]{1,0:T(8,128)(2,1)S(1)}, bf16[32,2048]{1,0:T(8,128)(2,1)S(1)}) custom-call(bf16[32,2176]{1,0:T(8,128)(2,1)S(1)} %collective-permute-done.7.refs_0_.refs_2_.near, bf16[32,2176]{1,0:T(8,128)(2,1)S(1)} %collective-permute-done.6.at_mid.refs_1_.refs_3_, bf16[32,2176]{1,0:T(8,128)(2,1)S(1)} %collective-permute-done.7.refs_0_.refs_2_.near, ...), custom_call_target="tpu_custom_call" | custom-call | flops 402653184 | bytes 6291456 | tf_op jit(solution)/shard_map/expert_pass/pallas_call | solution.py:87
  27.3 1.4 %collective-permute-done.14.at_mid.refs_5_ = bf16[32,2048]{1,0:T(8,128)(2,1)S(1)} collective-permute-done((bf16[32,2048]{1,0:T(8,128)(2,1)S(1)}, bf16[32,2048]{1,0:T(8,128)(2,1)S(1)}, u32[]{:S(2)}, u32[]{:S(2)}) %collective-permute-start.14) | collective-permute-done | bytes 131104 | tf_op jit(solution)/shard_map/ppermute | solution.py:277
  29.5 1.7 %collective-permute-start.26 = (bf16[32,2048]{1,0:T(8,128)(2,1)S(1)}, bf16[32,2048]{1,0:T(8,128)(2,1)S(1)}, u32[]{:S(2)}, u32[]{:S(2)}) collective-permute-start(bf16[32,2048]{1,0:T(8,128)(2,1)S(1)} %add.10), channel_id=1, source_target_pairs={{0,8},{2,4},{4,2},{6,14},{8,0},{10,12},{12,10},{14,6},{16,24},{18,... | collective-permute-start | bytes 393224 | tf_op jit(solution)/shard_map/ppermute | solution.py:277
  31.9 1.7 %collective-permute-start.17 = (bf16[32,2048]{1,0:T(8,128)(2,1)S(1)}, bf16[32,2048]{1,0:T(8,128)(2,1)S(1)}, u32[]{:S(2)}, u32[]{:S(2)}) collective-permute-start(bf16[32,2048]{1,0:T(8,128)(2,1)S(1)} %add.8), channel_id=1, source_target_pairs={{0,8},{2,4},{4,2},{6,14},{8,0},{10,12},{12,10},{14,6},{16,24},{18,... | collective-permute-start | bytes 393224 | tf_op jit(solution)/shard_map/ppermute | solution.py:277
  33.6 1.3 %expert_pass.10 = (bf16[32,2048]{1,0:T(8,128)(2,1)S(1)}, bf16[32,2048]{1,0:T(8,128)(2,1)S(1)}) custom-call(bf16[32,2048]{1,0:T(8,128)(2,1)S(1)} %collective-permute-done.16.a.refs_0_, bf16[32,2176]{1,0:T(8,128)(2,1)S(1)} %collective-permute-done.8.at_mid.refs_1_, bf16[32,2176]{1,0:T(8,128)(2,1)S(1)} %collective-permute-done.7.refs_0_.refs_2_.near, ...), custom_call_target="tpu_custom_call" | custom-call | flops 402653184 | bytes 6291456 | tf_op jit(solution)/shard_map/expert_pass/pallas_call | solution.py:87
  35.1 1.6 %collective-permute-start.27 = (bf16[32,2048]{1,0:T(8,128)(2,1)S(1)}, bf16[32,2048]{1,0:T(8,128)(2,1)S(1)}, u32[]{:S(2)}, u32[]{:S(2)}) collective-permute-start(bf16[32,2048]{1,0:T(8,128)(2,1)S(1)} %add.13), channel_id=1, source_target_pairs={{0,8},{2,4},{4,2},{6,14},{8,0},{10,12},{12,10},{14,6},{16,24},{18,... | collective-permute-start | bytes 393224 | tf_op jit(solution)/shard_map/ppermute | solution.py:277
  37.3 1.6 %collective-permute-start.18 = (bf16[32,2048]{1,0:T(8,128)(2,1)S(1)}, bf16[32,2048]{1,0:T(8,128)(2,1)S(1)}, u32[]{:S(2)}, u32[]{:S(2)}) collective-permute-start(bf16[32,2048]{1,0:T(8,128)(2,1)S(1)} %add.9), channel_id=1, source_target_pairs={{0,8},{2,4},{4,2},{6,14},{8,0},{10,12},{12,10},{14,6},{16,24},{18,... | collective-permute-start | bytes 393224 | tf_op jit(solution)/shard_map/ppermute | solution.py:277
  38.9 1.3 %expert_pass.9 = (bf16[32,2048]{1,0:T(8,128)(2,1)S(1)}, bf16[32,2048]{1,0:T(8,128)(2,1)S(1)}) custom-call(bf16[32,2048]{1,0:T(8,128)(2,1)S(1)} %collective-permute-done.13.refs_0_.a, bf16[32,2048]{1,0:T(8,128)(2,1)S(1)} %collective-permute-done.12.at_mid.refs_1_, bf16[32,2176]{1,0:T(8,128)(2,1)S(1)} %collective-permute-done.1.refs_0_.refs_2_.refs_1_, ...), custom_call_target="tpu_custom_call" | custom-call | flops 402653184 | bytes 6291456 | tf_op jit(solution)/shard_map/expert_pass/pallas_call | solution.py:87
  41.2 2.0 %collective-permute-start.29 = (bf16[32,2048]{1,0:T(8,128)(2,1)S(1)}, bf16[32,2048]{1,0:T(8,128)(2,1)S(1)}, u32[]{:S(2)}, u32[]{:S(2)}) collective-permute-start(bf16[32,2048]{1,0:T(8,128)(2,1)S(1)} %add.14), channel_id=1, source_target_pairs={{0,8},{2,4},{4,2},{6,14},{8,0},{10,12},{12,10},{14,6},{16,24},{18,... | collective-permute-start | bytes 393224 | tf_op jit(solution)/shard_map/ppermute | solution.py:277
  43.7 2.0 %collective-permute-start.23 = (bf16[32,2048]{1,0:T(8,128)(2,1)S(1)}, bf16[32,2048]{1,0:T(8,128)(2,1)S(1)}, u32[]{:S(2)}, u32[]{:S(2)}) collective-permute-start(bf16[32,2048]{1,0:T(8,128)(2,1)S(1)} %add.11), channel_id=1, source_target_pairs={{0,8},{2,4},{4,2},{6,14},{8,0},{10,12},{12,10},{14,6},{16,24},{18,... | collective-permute-start | bytes 393224 | tf_op jit(solution)/shard_map/ppermute | solution.py:277
  45.7 1.3 %expert_pass.11 = (bf16[32,2048]{1,0:T(8,128)(2,1)S(1)}, bf16[32,2048]{1,0:T(8,128)(2,1)S(1)}) custom-call(bf16[32,2048]{1,0:T(8,128)(2,1)S(1)} %collective-permute-done.21.refs_0_.a, bf16[32,2176]{1,0:T(8,128)(2,1)S(1)} %collective-permute-done.1.refs_0_.refs_2_.refs_1_, bf16[32,2176]{1,0:T(8,128)(2,1)S(1)} %collective-permute-done.4.refs_0_.refs_1_.refs_2_.refs_3_, ...), custom_call_target="tpu_custom_call" | custom-call | flops 402653184 | bytes 6291456 | tf_op jit(solution)/shard_map/expert_pass/pallas_call | solution.py:87
  47.1 2.2 %collective-permute-start.31 = (bf16[32,2048]{1,0:T(8,128)(2,1)S(1)}, bf16[32,2048]{1,0:T(8,128)(2,1)S(1)}, u32[]{:S(2)}, u32[]{:S(2)}) collective-permute-start(bf16[32,2048]{1,0:T(8,128)(2,1)S(1)} %add.15), channel_id=1, source_target_pairs={{0,8},{2,4},{4,2},{6,14},{8,0},{10,12},{12,10},{14,6},{16,24},{18,... | collective-permute-start | bytes 393224 | tf_op jit(solution)/shard_map/ppermute | solution.py:277
  49.5 2.1 %collective-permute-start.25 = (bf16[32,2048]{1,0:T(8,128)(2,1)S(1)}, bf16[32,2048]{1,0:T(8,128)(2,1)S(1)}, u32[]{:S(2)}, u32[]{:S(2)}) collective-permute-start(bf16[32,2048]{1,0:T(8,128)(2,1)S(1)} %add.12), channel_id=1, source_target_pairs={{0,8},{2,4},{4,2},{6,14},{8,0},{10,12},{12,10},{14,6},{16,24},{18,... | collective-permute-start | bytes 393224 | tf_op jit(solution)/shard_map/ppermute | solution.py:277
  53.2 1.7 %collective-permute-done.24.outer = bf16[32,2048]{1,0:T(8,128)(2,1)S(1)} collective-permute-done((bf16[32,2048]{1,0:T(8,128)(2,1)S(1)}, bf16[32,2048]{1,0:T(8,128)(2,1)S(1)}, u32[]{:S(2)}, u32[]{:S(2)}) %collective-permute-start.24) | collective-permute-done | bytes 131104 | tf_op jit(solution)/shard_map/ppermute | solution.py:274
  55.8 0.8 %join.1 = bf16[128,2048]{1,0:T(8,128)(2,1)} custom-call(bf16[32,2048]{1,0:T(8,128)(2,1)S(1)} %finish_first.2.refs_0_.a, bf16[32,2048]{1,0:T(8,128)(2,1)S(1)} %finish_second.2.refs_1_, bf16[32,2048]{1,0:T(8,128)(2,1)S(1)} %finish_first.3.refs_2_.b, bf16[32,2048]{1,0:T(8,128)(2,1)S(1)} %finish_second.3.refs_3_), custom_call_target="tpu_custom_call" | custom-call | tf_op jit(solution)/shard_map/join/pallas_call | solution.py:87
  56.6 2.4 %collective-permute-done.34.refs_1_ = bf16[32,2048]{1,0:T(8,128)(2,1)S(1)} collective-permute-done((bf16[32,2048]{1,0:T(8,128)(2,1)S(1)}, bf16[32,2048]{1,0:T(8,128)(2,1)S(1)}, u32[]{:S(2)}, u32[]{:S(2)}) %collective-permute-start.34) | collective-permute-done | bytes 131104 | tf_op jit(solution)/shard_map/ppermute | solution.py:385
  59.0 1.4 %collective-permute-done.33.refs_0_ = bf16[32,2048]{1,0:T(8,128)(2,1)S(1)} collective-permute-done((bf16[32,2048]{1,0:T(8,128)(2,1)S(1)}, bf16[32,2048]{1,0:T(8,128)(2,1)S(1)}, u32[]{:S(2)}, u32[]{:S(2)}) %collective-permute-start.33) | collective-permute-done | bytes 131104 | tf_op jit(solution)/shard_map/ppermute | solution.py:385
  60.4 0.8 %join_handed.1 = bf16[128,2048]{1,0:T(8,128)(2,1)} custom-call(bf16[64,2048]{1,0:T(8,128)(2,1)S(1)} %collective-permute-done.32.firsts, bf16[32,2048]{1,0:T(8,128)(2,1)S(1)} %collective-permute-done.33.refs_0_, bf16[32,2048]{1,0:T(8,128)(2,1)S(1)} %collective-permute-done.34.refs_1_), custom_call_target="tpu_custom_call" | custom-call | tf_op jit(solution)/shard_map/join_handed/pallas_call | solution.py:87
  (75 shorter events, 9.6 us)
Async XLA Ops:
  1.8 6.6 %collective-permute-start.2 = (bf16[32,2176]{1,0:T(8,128)(2,1)S(1)}, bf16[32,2176]{1,0:T(8,128)(2,1)S(1)}, u32[]{:S(2)}, u32[]{:S(2)}) collective-permute-start(bf16[32,2176]{1,0:T(8,128)(2,1)S(1)} %get-tuple-element.50.refs_10_), channel_id=1, source_target_pairs={{0,8},{2,4},{4,2},{6,14},{8,0},{10,12},{12,10},{14,6},{16,24},{18,... | collective-permute-start | bytes 417800 | tf_op jit(solution)/shard_map/ppermute | solution.py:277
  3.5 6.2 %collective-permute-start.5 = (bf16[32,2176]{1,0:T(8,128)(2,1)S(1)}, bf16[32,2176]{1,0:T(8,128)(2,1)S(1)}, u32[]{:S(2)}, u32[]{:S(2)}) collective-permute-start(bf16[32,2176]{1,0:T(8,128)(2,1)S(1)} %get-tuple-element.50.refs_10_), channel_id=1, source_target_pairs={{0,2},{2,0},{4,6},{6,4},{8,10},{10,8},{12,14},{14,12},{16,18},{18,... | collective-permute-start | bytes 417800 | tf_op jit(solution)/shard_map/ppermute | solution.py:274
  3.5 9.9 %collective-permute-start = (bf16[32,2176]{1,0:T(8,128)(2,1)S(1)}, bf16[32,2176]{1,0:T(8,128)(2,1)S(1)}, u32[]{:S(2)}, u32[]{:S(2)}) collective-permute-start(bf16[32,2176]{1,0:T(8,128)(2,1)S(1)} %get-tuple-element.44.refs_8_), channel_id=1, source_target_pairs={{0,8},{2,4},{4,2},{6,14},{8,0},{10,12},{12,10},{14,6},{16,24},{18,... | collective-permute-start | bytes 417800 | tf_op jit(solution)/shard_map/ppermute | solution.py:277
  5.1 8.5 %collective-permute-start.4 = (bf16[32,2176]{1,0:T(8,128)(2,1)S(1)}, bf16[32,2176]{1,0:T(8,128)(2,1)S(1)}, u32[]{:S(2)}, u32[]{:S(2)}) collective-permute-start(bf16[32,2176]{1,0:T(8,128)(2,1)S(1)} %get-tuple-element.44.refs_8_), channel_id=1, source_target_pairs={{0,2},{2,0},{4,6},{6,4},{8,10},{10,8},{12,14},{14,12},{16,18},{18,... | collective-permute-start | bytes 417800 | tf_op jit(solution)/shard_map/ppermute | solution.py:274
  8.5 7.8 %collective-permute-start.3 = (bf16[32,2176]{1,0:T(8,128)(2,1)S(1)}, bf16[32,2176]{1,0:T(8,128)(2,1)S(1)}, u32[]{:S(2)}, u32[]{:S(2)}) collective-permute-start(bf16[32,2176]{1,0:T(8,128)(2,1)S(1)} %choose.11), channel_id=1, source_target_pairs={{0,2},{2,0},{4,6},{6,4},{8,10},{10,8},{12,14},{14,12},{16,18},{18,... | collective-permute-start | bytes 417800 | tf_op jit(solution)/shard_map/ppermute | solution.py:274
  9.6 7.3 %collective-permute-start.9 = (bf16[32,2176]{1,0:T(8,128)(2,1)S(1)}, bf16[32,2176]{1,0:T(8,128)(2,1)S(1)}, u32[]{:S(2)}, u32[]{:S(2)}) collective-permute-start(bf16[32,2176]{1,0:T(8,128)(2,1)S(1)} %collective-permute-done.5.refs_4_.refs_5_.refs_6_.refs_7_), channel_id=1, source_target_pairs={{0,8},{2,4},{4,2},{6,14},{8,0},{10,12},{12,10},{14,6},{16,24},{18,... | collective-permute-start | bytes 417800 | tf_op jit(solution)/shard_map/ppermute | solution.py:277
  13.6 6.2 %collective-permute-start.6 = (bf16[32,2176]{1,0:T(8,128)(2,1)S(1)}, bf16[32,2176]{1,0:T(8,128)(2,1)S(1)}, u32[]{:S(2)}, u32[]{:S(2)}) collective-permute-start(bf16[32,2176]{1,0:T(8,128)(2,1)S(1)} %collective-permute-done.4.refs_0_.refs_1_.refs_2_.refs_3_), channel_id=1, source_target_pairs={{0,8},{2,4},{4,2},{6,14},{8,0},{10,12},{12,10},{14,6},{16,24},{18,... | collective-permute-start | bytes 417800 | tf_op jit(solution)/shard_map/ppermute | solution.py:277
  16.3 6.9 %collective-permute-start.11 = (bf16[32,2176]{1,0:T(8,128)(2,1)S(1)}, bf16[32,2176]{1,0:T(8,128)(2,1)S(1)}, u32[]{:S(2)}, u32[]{:S(2)}) collective-permute-start(bf16[32,2176]{1,0:T(8,128)(2,1)S(1)} %collective-permute-done.3.refs_4_.refs_6_.refs_5_), channel_id=1, source_target_pairs={{0,8},{2,4},{4,2},{6,14},{8,0},{10,12},{12,10},{14,6},{16,24},{18,... | collective-permute-start | bytes 417800 | tf_op jit(solution)/shard_map/ppermute | solution.py:277
  17.0 6.3 %collective-permute-start.10 = (bf16[32,2176]{1,0:T(8,128)(2,1)S(1)}, bf16[32,2176]{1,0:T(8,128)(2,1)S(1)}, u32[]{:S(2)}, u32[]{:S(2)}) collective-permute-start(bf16[32,2176]{1,0:T(8,128)(2,1)S(1)} %choose.14), channel_id=1, source_target_pairs={{0,2},{2,0},{4,6},{6,4},{8,10},{10,8},{12,14},{14,12},{16,18},{18,... | collective-permute-start | bytes 417800 | tf_op jit(solution)/shard_map/ppermute | solution.py:274
  18.5 7.4 %collective-permute-start.8 = (bf16[32,2176]{1,0:T(8,128)(2,1)S(1)}, bf16[32,2176]{1,0:T(8,128)(2,1)S(1)}, u32[]{:S(2)}, u32[]{:S(2)}) collective-permute-start(bf16[32,2176]{1,0:T(8,128)(2,1)S(1)} %collective-permute-done.1.refs_0_.refs_2_.refs_1_), channel_id=1, source_target_pairs={{0,8},{2,4},{4,2},{6,14},{8,0},{10,12},{12,10},{14,6},{16,24},{18,... | collective-permute-start | bytes 417800 | tf_op jit(solution)/shard_map/ppermute | solution.py:277
  19.8 6.1 %collective-permute-start.7 = (bf16[32,2176]{1,0:T(8,128)(2,1)S(1)}, bf16[32,2176]{1,0:T(8,128)(2,1)S(1)}, u32[]{:S(2)}, u32[]{:S(2)}) collective-permute-start(bf16[32,2176]{1,0:T(8,128)(2,1)S(1)} %choose.12), channel_id=1, source_target_pairs={{0,2},{2,0},{4,6},{6,4},{8,10},{10,8},{12,14},{14,12},{16,18},{18,... | collective-permute-start | bytes 417800 | tf_op jit(solution)/shard_map/ppermute | solution.py:274
  19.9 8.8 %collective-permute-start.14 = (bf16[32,2048]{1,0:T(8,128)(2,1)S(1)}, bf16[32,2048]{1,0:T(8,128)(2,1)S(1)}, u32[]{:S(2)}, u32[]{:S(2)}) collective-permute-start(bf16[32,2048]{1,0:T(8,128)(2,1)S(1)} %get-tuple-element.49.at_end.refs_11_.at_mid), channel_id=1, source_target_pairs={{0,8},{2,4},{4,2},{6,14},{8,0},{10,12},{12,10},{14,6},{16,24},{18,... | collective-permute-start | bytes 393224 | tf_op jit(solution)/shard_map/ppermute | solution.py:277
  23.3 6.1 %collective-permute-start.20 = (bf16[32,2048]{1,0:T(8,128)(2,1)S(1)}, bf16[32,2048]{1,0:T(8,128)(2,1)S(1)}, u32[]{:S(2)}, u32[]{:S(2)}) collective-permute-start(bf16[32,2048]{1,0:T(8,128)(2,1)S(1)} %choose.15), channel_id=1, source_target_pairs={{0,2},{2,0},{4,6},{6,4},{8,10},{10,8},{12,14},{14,12},{16,18},{18,... | collective-permute-start | bytes 393224 | tf_op jit(solution)/shard_map/ppermute | solution.py:274
  23.6 7.6 %collective-permute-start.12 = (bf16[32,2048]{1,0:T(8,128)(2,1)S(1)}, bf16[32,2048]{1,0:T(8,128)(2,1)S(1)}, u32[]{:S(2)}, u32[]{:S(2)}) collective-permute-start(bf16[32,2048]{1,0:T(8,128)(2,1)S(1)} %get-tuple-element.43.at_end.refs_9_.at_mid), channel_id=1, source_target_pairs={{0,8},{2,4},{4,2},{6,14},{8,0},{10,12},{12,10},{14,6},{16,24},{18,... | collective-permute-start | bytes 393224 | tf_op jit(solution)/shard_map/ppermute | solution.py:277
  25.9 6.0 %collective-permute-start.16 = (bf16[32,2048]{1,0:T(8,128)(2,1)S(1)}, bf16[32,2048]{1,0:T(8,128)(2,1)S(1)}, u32[]{:S(2)}, u32[]{:S(2)}) collective-permute-start(bf16[32,2048]{1,0:T(8,128)(2,1)S(1)} %choose.13), channel_id=1, source_target_pairs={{0,2},{2,0},{4,6},{6,4},{8,10},{10,8},{12,14},{14,12},{16,18},{18,... | collective-permute-start | bytes 393224 | tf_op jit(solution)/shard_map/ppermute | solution.py:274
  28.7 6.3 %collective-permute-start.15 = (bf16[32,2048]{1,0:T(8,128)(2,1)S(1)}, bf16[32,2048]{1,0:T(8,128)(2,1)S(1)}, u32[]{:S(2)}, u32[]{:S(2)}) collective-permute-start(bf16[32,2048]{1,0:T(8,128)(2,1)S(1)} %choose.17), channel_id=1, source_target_pairs={{0,2},{2,0},{4,6},{6,4},{8,10},{10,8},{12,14},{14,12},{16,18},{18,... | collective-permute-start | bytes 393224 | tf_op jit(solution)/shard_map/ppermute | solution.py:274
  29.5 5.6 %collective-permute-start.26 = (bf16[32,2048]{1,0:T(8,128)(2,1)S(1)}, bf16[32,2048]{1,0:T(8,128)(2,1)S(1)}, u32[]{:S(2)}, u32[]{:S(2)}) collective-permute-start(bf16[32,2048]{1,0:T(8,128)(2,1)S(1)} %add.10), channel_id=1, source_target_pairs={{0,8},{2,4},{4,2},{6,14},{8,0},{10,12},{12,10},{14,6},{16,24},{18,... | collective-permute-start | bytes 393224 | tf_op jit(solution)/shard_map/ppermute | solution.py:277
  31.2 6.1 %collective-permute-start.13 = (bf16[32,2048]{1,0:T(8,128)(2,1)S(1)}, bf16[32,2048]{1,0:T(8,128)(2,1)S(1)}, u32[]{:S(2)}, u32[]{:S(2)}) collective-permute-start(bf16[32,2048]{1,0:T(8,128)(2,1)S(1)} %choose.16), channel_id=1, source_target_pairs={{0,2},{2,0},{4,6},{6,4},{8,10},{10,8},{12,14},{14,12},{16,18},{18,... | collective-permute-start | bytes 393224 | tf_op jit(solution)/shard_map/ppermute | solution.py:274
  34.9 5.8 %collective-permute-start.22 = (bf16[32,2048]{1,0:T(8,128)(2,1)S(1)}, bf16[32,2048]{1,0:T(8,128)(2,1)S(1)}, u32[]{:S(2)}, u32[]{:S(2)}) collective-permute-start(bf16[32,2048]{1,0:T(8,128)(2,1)S(1)} %choose.19), channel_id=1, source_target_pairs={{0,2},{2,0},{4,6},{6,4},{8,10},{10,8},{12,14},{14,12},{16,18},{18,... | collective-permute-start | bytes 393224 | tf_op jit(solution)/shard_map/ppermute | solution.py:274
  35.1 5.7 %collective-permute-start.27 = (bf16[32,2048]{1,0:T(8,128)(2,1)S(1)}, bf16[32,2048]{1,0:T(8,128)(2,1)S(1)}, u32[]{:S(2)}, u32[]{:S(2)}) collective-permute-start(bf16[32,2048]{1,0:T(8,128)(2,1)S(1)} %add.13), channel_id=1, source_target_pairs={{0,8},{2,4},{4,2},{6,14},{8,0},{10,12},{12,10},{14,6},{16,24},{18,... | collective-permute-start | bytes 393224 | tf_op jit(solution)/shard_map/ppermute | solution.py:277
  36.7 6.5 %collective-permute-start.21 = (bf16[32,2048]{1,0:T(8,128)(2,1)S(1)}, bf16[32,2048]{1,0:T(8,128)(2,1)S(1)}, u32[]{:S(2)}, u32[]{:S(2)}) collective-permute-start(bf16[32,2048]{1,0:T(8,128)(2,1)S(1)} %choose.18), channel_id=1, source_target_pairs={{0,2},{2,0},{4,6},{6,4},{8,10},{10,8},{12,14},{14,12},{16,18},{18,... | collective-permute-start | bytes 393224 | tf_op jit(solution)/shard_map/ppermute | solution.py:274
  37.3 6.1 %collective-permute-start.18 = (bf16[32,2048]{1,0:T(8,128)(2,1)S(1)}, bf16[32,2048]{1,0:T(8,128)(2,1)S(1)}, u32[]{:S(2)}, u32[]{:S(2)}) collective-permute-start(bf16[32,2048]{1,0:T(8,128)(2,1)S(1)} %add.9), channel_id=1, source_target_pairs={{0,8},{2,4},{4,2},{6,14},{8,0},{10,12},{12,10},{14,6},{16,24},{18,... | collective-permute-start | bytes 393224 | tf_op jit(solution)/shard_map/ppermute | solution.py:277
  40.8 6.1 %collective-permute-start.28 = (bf16[32,2048]{1,0:T(8,128)(2,1)S(1)}, bf16[32,2048]{1,0:T(8,128)(2,1)S(1)}, u32[]{:S(2)}, u32[]{:S(2)}) collective-permute-start(bf16[32,2048]{1,0:T(8,128)(2,1)S(1)} %choose_sum.6), channel_id=1, source_target_pairs={{0,2},{2,0},{4,6},{6,4},{8,10},{10,8},{12,14},{14,12},{16,18},{18,... | collective-permute-start | bytes 393224 | tf_op jit(solution)/shard_map/ppermute | solution.py:274
  41.2 5.8 %collective-permute-start.29 = (bf16[32,2048]{1,0:T(8,128)(2,1)S(1)}, bf16[32,2048]{1,0:T(8,128)(2,1)S(1)}, u32[]{:S(2)}, u32[]{:S(2)}) collective-permute-start(bf16[32,2048]{1,0:T(8,128)(2,1)S(1)} %add.14), channel_id=1, source_target_pairs={{0,8},{2,4},{4,2},{6,14},{8,0},{10,12},{12,10},{14,6},{16,24},{18,... | collective-permute-start | bytes 393224 | tf_op jit(solution)/shard_map/ppermute | solution.py:277
  43.4 5.9 %collective-permute-start.19 = (bf16[32,2048]{1,0:T(8,128)(2,1)S(1)}, bf16[32,2048]{1,0:T(8,128)(2,1)S(1)}, u32[]{:S(2)}, u32[]{:S(2)}) collective-permute-start(bf16[32,2048]{1,0:T(8,128)(2,1)S(1)} %choose_sum.4), channel_id=1, source_target_pairs={{0,2},{2,0},{4,6},{6,4},{8,10},{10,8},{12,14},{14,12},{16,18},{18,... | collective-permute-start | bytes 393224 | tf_op jit(solution)/shard_map/ppermute | solution.py:274
  43.7 5.7 %collective-permute-start.23 = (bf16[32,2048]{1,0:T(8,128)(2,1)S(1)}, bf16[32,2048]{1,0:T(8,128)(2,1)S(1)}, u32[]{:S(2)}, u32[]{:S(2)}) collective-permute-start(bf16[32,2048]{1,0:T(8,128)(2,1)S(1)} %add.11), channel_id=1, source_target_pairs={{0,8},{2,4},{4,2},{6,14},{8,0},{10,12},{12,10},{14,6},{16,24},{18,... | collective-permute-start | bytes 393224 | tf_op jit(solution)/shard_map/ppermute | solution.py:277
  47.0 5.5 %collective-permute-start.30 = (bf16[32,2048]{1,0:T(8,128)(2,1)S(1)}, bf16[32,2048]{1,0:T(8,128)(2,1)S(1)}, u32[]{:S(2)}, u32[]{:S(2)}) collective-permute-start(bf16[32,2048]{1,0:T(8,128)(2,1)S(1)} %choose_sum.7), channel_id=1, source_target_pairs={{0,2},{2,0},{4,6},{6,4},{8,10},{10,8},{12,14},{14,12},{16,18},{18,... | collective-permute-start | bytes 393224 | tf_op jit(solution)/shard_map/ppermute | solution.py:274
  47.1 6.0 %collective-permute-start.31 = (bf16[32,2048]{1,0:T(8,128)(2,1)S(1)}, bf16[32,2048]{1,0:T(8,128)(2,1)S(1)}, u32[]{:S(2)}, u32[]{:S(2)}) collective-permute-start(bf16[32,2048]{1,0:T(8,128)(2,1)S(1)} %add.15), channel_id=1, source_target_pairs={{0,8},{2,4},{4,2},{6,14},{8,0},{10,12},{12,10},{14,6},{16,24},{18,... | collective-permute-start | bytes 393224 | tf_op jit(solution)/shard_map/ppermute | solution.py:277
  49.4 5.5 %collective-permute-start.24 = (bf16[32,2048]{1,0:T(8,128)(2,1)S(1)}, bf16[32,2048]{1,0:T(8,128)(2,1)S(1)}, u32[]{:S(2)}, u32[]{:S(2)}) collective-permute-start(bf16[32,2048]{1,0:T(8,128)(2,1)S(1)} %choose_sum.5), channel_id=1, source_target_pairs={{0,2},{2,0},{4,6},{6,4},{8,10},{10,8},{12,14},{14,12},{16,18},{18,... | collective-permute-start | bytes 393224 | tf_op jit(solution)/shard_map/ppermute | solution.py:274
  49.5 6.2 %collective-permute-start.25 = (bf16[32,2048]{1,0:T(8,128)(2,1)S(1)}, bf16[32,2048]{1,0:T(8,128)(2,1)S(1)}, u32[]{:S(2)}, u32[]{:S(2)}) collective-permute-start(bf16[32,2048]{1,0:T(8,128)(2,1)S(1)} %add.12), channel_id=1, source_target_pairs={{0,8},{2,4},{4,2},{6,14},{8,0},{10,12},{12,10},{14,6},{16,24},{18,... | collective-permute-start | bytes 393224 | tf_op jit(solution)/shard_map/ppermute | solution.py:277
  51.8 8.7 %collective-permute-start.32 = (bf16[64,2048]{1,0:T(8,128)(2,1)S(1)}, bf16[64,2048]{1,0:T(8,128)(2,1)S(1)}, u32[]{:S(2)}, u32[]{:S(2)}) collective-permute-start(bf16[64,2048]{1,0:T(8,128)(2,1)S(1)} %join_two.1), channel_id=1, source_target_pairs={{0,8},{8,16},{16,24},{24,0},{1,9},{9,17},{17,25},{25,1},{2,10},{10... | collective-permute-start | bytes 786440 | tf_op jit(solution)/shard_map/ppermute | solution.py:384
  53.2 5.8 %collective-permute-start.34 = (bf16[32,2048]{1,0:T(8,128)(2,1)S(1)}, bf16[32,2048]{1,0:T(8,128)(2,1)S(1)}, u32[]{:S(2)}, u32[]{:S(2)}) collective-permute-start(bf16[32,2048]{1,0:T(8,128)(2,1)S(1)} %finish_second.3.refs_3_), channel_id=1, source_target_pairs={{0,8},{8,16},{16,24},{24,0},{1,9},{9,17},{17,25},{25,1},{2,10},{10... | collective-permute-start | bytes 393224 | tf_op jit(solution)/shard_map/ppermute | solution.py:385
  (3 other events, 15.2 us)

commit v8 on v7

--- a/solution.py
+++ b/solution.py
@@ -77,7 +77,7 @@
     return me, (me == 0) | (me == 3)
 
 
-def run(body, name, out_shape, *operands, scratch=(), specs=None, out_specs=None, work=(0, 0)):
+def run(body, name, out_shape, *operands, scratch=(), specs=None, out_specs=None, work=(0, 0), alias=()):
     several = isinstance(out_shape, list)
     specs = specs or [IN_VMEM] * len(operands)
     operands = [
@@ -92,6 +92,7 @@
         scratch_shapes=list(scratch),
         compiler_params=pltpu.CompilerParams(vmem_limit_bytes=24 * 2**20),
         cost_estimate=pl.CostEstimate(flops=work[0], bytes_accessed=work[1], transcendentals=0),
+        input_output_aliases=dict(alias),
         name=name,
     )(*operands)
 
@@ -236,22 +237,47 @@
     result[half:] = b[...]
 
 
-def join_handed(firsts, *refs):
-    seconds, (whole, zeros, sems) = refs[:STREAMS], refs[STREAMS:]
-    piece = seconds[0].shape[0]
+def join_handed(firsts, early, whole, zeros, sems):
+    piece = early.shape[0]
     nothing = lax.axis_index("section") == 0
+    places = [(firsts.at[pl.ds(s * piece, piece)], 2 * s) for s in range(STREAMS)] + [(early, 1)]
+
+    def put(parts):
+        copies = [
+            pltpu.make_async_copy(part, whole.at[pl.ds(place * piece, piece)], sems.at[place])
+            for part, place in parts
+        ]
+        for copy in copies:
+            copy.start()
+        for copy in copies:
+            copy.wait()
 
     @pl.when(nothing)
     def _():
         zeros[...] = jnp.zeros_like(zeros)
-        join(*[zeros] * (2 * STREAMS), whole, sems)
+        put([(zeros, place) for _, place in places])
 
     @pl.when(~nothing)
     def _():
-        parts = []
-        for s in range(STREAMS):
-            parts += [firsts.at[pl.ds(s * piece, piece)], seconds[s]]
-        join(*parts, whole, sems)
+        put(places)
+
+
+def join_last(begun, last, whole, zeros, sems):
+    piece = last.shape[0]
+    there = whole.at[pl.ds(whole.shape[0] - piece, piece)]
+    nothing = lax.axis_index("section") == 0
+
+    @pl.when(nothing)
+    def _():
+        zeros[...] = jnp.zeros_like(zeros)
+
+    @pl.when(~nothing)
+    def _():
+        zeros[...] = last[...]
+
+    copy = pltpu.make_async_copy(zeros, there, sems.at[0])
+    copy.start()
+    copy.wait()
 
 
 def on_line(tokens, routes, route_weights, expert_gate, expert_up, expert_down):
@@ -383,7 +409,18 @@
     one = run(join_two, "join_two", held((2 * piece, width)), firsts[0], firsts[1])
     back = lax.ppermute(one, "section", ring)
     given = [back, *(lax.ppermute(done[k], "section", ring) for k in (1, 3))]
-    handed = joined(join_handed, given, held(block))
+    begun = joined(join_handed, given[:2], held(block))
+    handed = run(
+        join_last,
+        "join_last",
+        jax.ShapeDtypeStruct((count, width), jnp.bfloat16),
+        begun,
+        given[2],
+        scratch=[held(block), pltpu.SemaphoreType.DMA((1,))],
+        specs=[ANYWHERE, IN_VMEM],
+        out_specs=ANYWHERE,
+        alias=[(0, 0)],
+    )
     return (joined(join, done)[None], handed[None])
 
 

time: 62.3 us -> 63.4 us (1.018)
  Pallas kernels: 14.5 us -> 15.2 us
    ppermute x16, waiting for transfers between devices: 5.74 us -> 6.46 us  [outer(): return lax.ppermute(value, axes, outer_pairs)]
    pallas_call x37 -> x38, Pallas kernels: 14.5 us -> 15.2 us  [run(): pl.pallas_call(body, out_shape=out_shape, in_specs=specs, out_specs=out_s...]
  transfers between devices with their start and end apart: 35 -> 35, of which waited for: 14 -> 12; matrix products, arithmetic and copies ran while one was open for 0% -> 0% of each run, Pallas kernels for 20% -> 21%
where the time goes in v8:
time: 63.4 us; the launch traced here: 62.2 us
  starting transfers between devices  30.1 us (47%)
  waiting for transfers between devices  16 us (25%)
  Pallas kernels  15.2 us (24%)
  between operations  1.02 us (2%)
    ppermute x16, starting transfers between devices, inner(): return lax.ppermute(value, axes, inner_pairs)  25.7 us
    pallas_call x38, Pallas kernels, run(): pl.pallas_call(body, out_shape=out_shape, in_specs=specs, out_specs=out_s...  15.2 us
    ppermute x16, waiting for transfers between devices, outer(): return lax.ppermute(value, axes, outer_pairs)  6.46 us
    ppermute x16, waiting for transfers between devices, inner(): return lax.ppermute(value, axes, inner_pairs)  6.03 us
    ppermute x16, starting transfers between devices, outer(): return lax.ppermute(value, axes, outer_pairs)  3.63 us
    ppermute x2, waiting for transfers between devices, on_line(): given = [back, *(lax.ppermute(done[k], 'section', ring) for k in (1, 3))]  3.46 us
  transfers between devices with their start and end apart: 35, of which 12 were waited for; matrix products, arithmetic and copies ran while one was open for 0% of the time, Pallas kernels for 21%

profile of v8, /device:TPU:12, one launch (start us, length us, event | category | flops | bytes accessed | tf_op | source)
XLA Modules:
  0.0 62.2 jit_solution(8279723818921587481)
XLA Ops:
  0.6 1.2 %prepare.1 = (bf16[32,2176]{1,0:T(8,128)(2,1)S(1)}, bf16[32,2048]{1,0:T(8,128)(2,1)S(1)}, bf16[32,2176]{1,0:T(8,128)(2,1)S(1)}, bf16[32,2048]{1,0:T(8,128)(2,1)S(1)}) custom-call(bf16[128,2048]{1,0:T(8,128)(2,1)} %bitcast.16, s32[2,128]{1,0:T(2,128)} %bitcast.18, f32[2,128]{1,0:T(2,128)} %bitcast.19), custom_call_target="tpu_custom_call" | custom-call | tf_op jit(solution)/shard_map/prepare/pallas_call | solution.py:87
  1.8 1.6 %collective-permute-start.2 = (bf16[32,2176]{1,0:T(8,128)(2,1)S(1)}, bf16[32,2176]{1,0:T(8,128)(2,1)S(1)}, u32[]{:S(2)}, u32[]{:S(2)}) collective-permute-start(bf16[32,2176]{1,0:T(8,128)(2,1)S(1)} %get-tuple-element.50.refs_10_), channel_id=1, source_target_pairs={{0,8},{2,4},{4,2},{6,14},{8,0},{10,12},{12,10},{14,6},{16,24},{18,... | collective-permute-start | bytes 417800 | tf_op jit(solution)/shard_map/ppermute | solution.py:303
  3.5 1.7 %collective-permute-start = (bf16[32,2176]{1,0:T(8,128)(2,1)S(1)}, bf16[32,2176]{1,0:T(8,128)(2,1)S(1)}, u32[]{:S(2)}, u32[]{:S(2)}) collective-permute-start(bf16[32,2176]{1,0:T(8,128)(2,1)S(1)} %get-tuple-element.44.refs_8_), channel_id=1, source_target_pairs={{0,8},{2,4},{4,2},{6,14},{8,0},{10,12},{12,10},{14,6},{16,24},{18,... | collective-permute-start | bytes 417800 | tf_op jit(solution)/shard_map/ppermute | solution.py:303
  5.5 3.0 %collective-permute-done.2.at_mid.refs_5_.refs_7_ = bf16[32,2176]{1,0:T(8,128)(2,1)S(1)} collective-permute-done((bf16[32,2176]{1,0:T(8,128)(2,1)S(1)}, bf16[32,2176]{1,0:T(8,128)(2,1)S(1)}, u32[]{:S(2)}, u32[]{:S(2)}) %collective-permute-start.2) | collective-permute-done | bytes 139296 | tf_op jit(solution)/shard_map/ppermute | solution.py:303
  8.6 1.1 %collective-permute-done.5.refs_4_.refs_5_.refs_6_.refs_7_ = bf16[32,2176]{1,0:T(8,128)(2,1)S(1)} collective-permute-done((bf16[32,2176]{1,0:T(8,128)(2,1)S(1)}, bf16[32,2176]{1,0:T(8,128)(2,1)S(1)}, u32[]{:S(2)}, u32[]{:S(2)}) %collective-permute-start.5) | collective-permute-done | bytes 139296 | tf_op jit(solution)/shard_map/ppermute | solution.py:300
  9.6 0.8 %collective-permute-start.9 = (bf16[32,2176]{1,0:T(8,128)(2,1)S(1)}, bf16[32,2176]{1,0:T(8,128)(2,1)S(1)}, u32[]{:S(2)}, u32[]{:S(2)}) collective-permute-start(bf16[32,2176]{1,0:T(8,128)(2,1)S(1)} %collective-permute-done.5.refs_4_.refs_5_.refs_6_.refs_7_), channel_id=1, source_target_pairs={{0,8},{2,4},{4,2},{6,14},{8,0},{10,12},{12,10},{14,6},{16,24},{18,... | collective-permute-start | bytes 417800 | tf_op jit(solution)/shard_map/ppermute | solution.py:303
  10.5 2.9 %load.1 = (bf16[2048,512]{1,0:T(8,128)(2,1)S(1)}, bf16[2048,512]{1,0:T(8,128)(2,1)S(1)}, bf16[512,2048]{1,0:T(8,128)(2,1)S(1)}) custom-call(bf16[2048,512]{1,0:T(8,128)(2,1)} %bitcast.12, bf16[2048,512]{1,0:T(8,128)(2,1)} %bitcast.13, bf16[512,2048]{1,0:T(8,128)(2,1)} %bitcast.14), custom_call_target="tpu_custom_call" | custom-call | bytes 6291456 | tf_op jit(solution)/shard_map/load/pallas_call | solution.py:87
  13.6 1.4 %collective-permute-start.6 = (bf16[32,2176]{1,0:T(8,128)(2,1)S(1)}, bf16[32,2176]{1,0:T(8,128)(2,1)S(1)}, u32[]{:S(2)}, u32[]{:S(2)}) collective-permute-start(bf16[32,2176]{1,0:T(8,128)(2,1)S(1)} %collective-permute-done.4.refs_0_.refs_1_.refs_2_.refs_3_), channel_id=1, source_target_pairs={{0,8},{2,4},{4,2},{6,14},{8,0},{10,12},{12,10},{14,6},{16,24},{18,... | collective-permute-start | bytes 417800 | tf_op jit(solution)/shard_map/ppermute | solution.py:303
  15.0 1.3 %expert_pass.7 = (bf16[32,2048]{1,0:T(8,128)(2,1)S(1)}, bf16[32,2048]{1,0:T(8,128)(2,1)S(1)}) custom-call(bf16[32,2176]{1,0:T(8,128)(2,1)S(1)} %collective-permute-done.4.refs_0_.refs_1_.refs_2_.refs_3_, bf16[32,2176]{1,0:T(8,128)(2,1)S(1)} %collective-permute-done.4.refs_0_.refs_1_.refs_2_.refs_3_, ...), custom_call_target="tpu_custom_call" | custom-call | flops 402653184 | bytes 6291456 | tf_op jit(solution)/shard_map/expert_pass/pallas_call | solution.py:87
  17.5 1.1 %collective-permute-done.1.refs_0_.refs_2_.refs_1_ = bf16[32,2176]{1,0:T(8,128)(2,1)S(1)} collective-permute-done((bf16[32,2176]{1,0:T(8,128)(2,1)S(1)}, bf16[32,2176]{1,0:T(8,128)(2,1)S(1)}, u32[]{:S(2)}, u32[]{:S(2)}) %collective-permute-start.1) | collective-permute-done | bytes 139296 | tf_op jit(solution)/shard_map/ppermute | solution.py:300
  18.5 1.2 %collective-permute-start.8 = (bf16[32,2176]{1,0:T(8,128)(2,1)S(1)}, bf16[32,2176]{1,0:T(8,128)(2,1)S(1)}, u32[]{:S(2)}, u32[]{:S(2)}) collective-permute-start(bf16[32,2176]{1,0:T(8,128)(2,1)S(1)} %collective-permute-done.1.refs_0_.refs_2_.refs_1_), channel_id=1, source_target_pairs={{0,8},{2,4},{4,2},{6,14},{8,0},{10,12},{12,10},{14,6},{16,24},{18,... | collective-permute-start | bytes 417800 | tf_op jit(solution)/shard_map/ppermute | solution.py:303
  19.9 1.8 %collective-permute-start.14 = (bf16[32,2048]{1,0:T(8,128)(2,1)S(1)}, bf16[32,2048]{1,0:T(8,128)(2,1)S(1)}, u32[]{:S(2)}, u32[]{:S(2)}) collective-permute-start(bf16[32,2048]{1,0:T(8,128)(2,1)S(1)} %get-tuple-element.49.at_end.refs_11_.at_mid), channel_id=1, source_target_pairs={{0,8},{2,4},{4,2},{6,14},{8,0},{10,12},{12,10},{14,6},{16,24},{18,... | collective-permute-start | bytes 393224 | tf_op jit(solution)/shard_map/ppermute | solution.py:303
  21.7 1.5 %expert_pass.6 = (bf16[32,2048]{1,0:T(8,128)(2,1)S(1)}, bf16[32,2048]{1,0:T(8,128)(2,1)S(1)}, f32[128,2048]{1,0:T(8,128)S(1)}) custom-call(bf16[32,2176]{1,0:T(8,128)(2,1)S(1)} %collective-permute-done.1.refs_0_.refs_2_.refs_1_, bf16[32,2176]{1,0:T(8,128)(2,1)S(1)} %collective-permute-done.at_mid.refs_1_.refs_3_, ...), custom_call_target="tpu_custom_call" | custom-call | flops 1207959552 | bytes 6291456 | tf_op jit(solution)/shard_map/expert_pass/pallas_call | solution.py:87
  23.6 1.8 %collective-permute-start.12 = (bf16[32,2048]{1,0:T(8,128)(2,1)S(1)}, bf16[32,2048]{1,0:T(8,128)(2,1)S(1)}, u32[]{:S(2)}, u32[]{:S(2)}) collective-permute-start(bf16[32,2048]{1,0:T(8,128)(2,1)S(1)} %get-tuple-element.43.at_end.refs_9_.at_mid), channel_id=1, source_target_pairs={{0,8},{2,4},{4,2},{6,14},{8,0},{10,12},{12,10},{14,6},{16,24},{18,... | collective-permute-start | bytes 393224 | tf_op jit(solution)/shard_map/ppermute | solution.py:303
  26.1 1.3 %expert_pass.8 = (bf16[32,2048]{1,0:T(8,128)(2,1)S(1)}, bf16[32,2048]{1,0:T(8,128)(2,1)S(1)}) custom-call(bf16[32,2176]{1,0:T(8,128)(2,1)S(1)} %collective-permute-done.7.refs_0_.refs_2_.near, bf16[32,2176]{1,0:T(8,128)(2,1)S(1)} %collective-permute-done.6.at_mid.refs_1_.refs_3_, bf16[32,2176]{1,0:T(8,128)(2,1)S(1)} %collective-permute-done.7.refs_0_.refs_2_.near, ...), custom_call_target="tpu_custom_call" | custom-call | flops 402653184 | bytes 6291456 | tf_op jit(solution)/shard_map/expert_pass/pallas_call | solution.py:87
  27.3 1.4 %collective-permute-done.14.at_mid.refs_5_ = bf16[32,2048]{1,0:T(8,128)(2,1)S(1)} collective-permute-done((bf16[32,2048]{1,0:T(8,128)(2,1)S(1)}, bf16[32,2048]{1,0:T(8,128)(2,1)S(1)}, u32[]{:S(2)}, u32[]{:S(2)}) %collective-permute-start.14) | collective-permute-done | bytes 131104 | tf_op jit(solution)/shard_map/ppermute | solution.py:303
  29.5 1.7 %collective-permute-start.26 = (bf16[32,2048]{1,0:T(8,128)(2,1)S(1)}, bf16[32,2048]{1,0:T(8,128)(2,1)S(1)}, u32[]{:S(2)}, u32[]{:S(2)}) collective-permute-start(bf16[32,2048]{1,0:T(8,128)(2,1)S(1)} %add.10), channel_id=1, source_target_pairs={{0,8},{2,4},{4,2},{6,14},{8,0},{10,12},{12,10},{14,6},{16,24},{18,... | collective-permute-start | bytes 393224 | tf_op jit(solution)/shard_map/ppermute | solution.py:303
  31.9 1.7 %collective-permute-start.17 = (bf16[32,2048]{1,0:T(8,128)(2,1)S(1)}, bf16[32,2048]{1,0:T(8,128)(2,1)S(1)}, u32[]{:S(2)}, u32[]{:S(2)}) collective-permute-start(bf16[32,2048]{1,0:T(8,128)(2,1)S(1)} %add.8), channel_id=1, source_target_pairs={{0,8},{2,4},{4,2},{6,14},{8,0},{10,12},{12,10},{14,6},{16,24},{18,... | collective-permute-start | bytes 393224 | tf_op jit(solution)/shard_map/ppermute | solution.py:303
  33.6 1.3 %expert_pass.10 = (bf16[32,2048]{1,0:T(8,128)(2,1)S(1)}, bf16[32,2048]{1,0:T(8,128)(2,1)S(1)}) custom-call(bf16[32,2048]{1,0:T(8,128)(2,1)S(1)} %collective-permute-done.16.a.refs_0_, bf16[32,2176]{1,0:T(8,128)(2,1)S(1)} %collective-permute-done.8.at_mid.refs_1_, bf16[32,2176]{1,0:T(8,128)(2,1)S(1)} %collective-permute-done.7.refs_0_.refs_2_.near, ...), custom_call_target="tpu_custom_call" | custom-call | flops 402653184 | bytes 6291456 | tf_op jit(solution)/shard_map/expert_pass/pallas_call | solution.py:87
  35.1 1.6 %collective-permute-start.27 = (bf16[32,2048]{1,0:T(8,128)(2,1)S(1)}, bf16[32,2048]{1,0:T(8,128)(2,1)S(1)}, u32[]{:S(2)}, u32[]{:S(2)}) collective-permute-start(bf16[32,2048]{1,0:T(8,128)(2,1)S(1)} %add.13), channel_id=1, source_target_pairs={{0,8},{2,4},{4,2},{6,14},{8,0},{10,12},{12,10},{14,6},{16,24},{18,... | collective-permute-start | bytes 393224 | tf_op jit(solution)/shard_map/ppermute | solution.py:303
  37.3 1.6 %collective-permute-start.18 = (bf16[32,2048]{1,0:T(8,128)(2,1)S(1)}, bf16[32,2048]{1,0:T(8,128)(2,1)S(1)}, u32[]{:S(2)}, u32[]{:S(2)}) collective-permute-start(bf16[32,2048]{1,0:T(8,128)(2,1)S(1)} %add.9), channel_id=1, source_target_pairs={{0,8},{2,4},{4,2},{6,14},{8,0},{10,12},{12,10},{14,6},{16,24},{18,... | collective-permute-start | bytes 393224 | tf_op jit(solution)/shard_map/ppermute | solution.py:303
  38.9 1.3 %expert_pass.9 = (bf16[32,2048]{1,0:T(8,128)(2,1)S(1)}, bf16[32,2048]{1,0:T(8,128)(2,1)S(1)}) custom-call(bf16[32,2048]{1,0:T(8,128)(2,1)S(1)} %collective-permute-done.13.refs_0_.a, bf16[32,2048]{1,0:T(8,128)(2,1)S(1)} %collective-permute-done.12.at_mid.refs_1_, bf16[32,2176]{1,0:T(8,128)(2,1)S(1)} %collective-permute-done.1.refs_0_.refs_2_.refs_1_, ...), custom_call_target="tpu_custom_call" | custom-call | flops 402653184 | bytes 6291456 | tf_op jit(solution)/shard_map/expert_pass/pallas_call | solution.py:87
  41.2 2.0 %collective-permute-start.29 = (bf16[32,2048]{1,0:T(8,128)(2,1)S(1)}, bf16[32,2048]{1,0:T(8,128)(2,1)S(1)}, u32[]{:S(2)}, u32[]{:S(2)}) collective-permute-start(bf16[32,2048]{1,0:T(8,128)(2,1)S(1)} %add.14), channel_id=1, source_target_pairs={{0,8},{2,4},{4,2},{6,14},{8,0},{10,12},{12,10},{14,6},{16,24},{18,... | collective-permute-start | bytes 393224 | tf_op jit(solution)/shard_map/ppermute | solution.py:303
  43.7 2.0 %collective-permute-start.23 = (bf16[32,2048]{1,0:T(8,128)(2,1)S(1)}, bf16[32,2048]{1,0:T(8,128)(2,1)S(1)}, u32[]{:S(2)}, u32[]{:S(2)}) collective-permute-start(bf16[32,2048]{1,0:T(8,128)(2,1)S(1)} %add.11), channel_id=1, source_target_pairs={{0,8},{2,4},{4,2},{6,14},{8,0},{10,12},{12,10},{14,6},{16,24},{18,... | collective-permute-start | bytes 393224 | tf_op jit(solution)/shard_map/ppermute | solution.py:303
  45.7 1.3 %expert_pass.11 = (bf16[32,2048]{1,0:T(8,128)(2,1)S(1)}, bf16[32,2048]{1,0:T(8,128)(2,1)S(1)}) custom-call(bf16[32,2048]{1,0:T(8,128)(2,1)S(1)} %collective-permute-done.21.refs_0_.a, bf16[32,2176]{1,0:T(8,128)(2,1)S(1)} %collective-permute-done.1.refs_0_.refs_2_.refs_1_, bf16[32,2176]{1,0:T(8,128)(2,1)S(1)} %collective-permute-done.4.refs_0_.refs_1_.refs_2_.refs_3_, ...), custom_call_target="tpu_custom_call" | custom-call | flops 402653184 | bytes 6291456 | tf_op jit(solution)/shard_map/expert_pass/pallas_call | solution.py:87
  47.1 2.2 %collective-permute-start.31 = (bf16[32,2048]{1,0:T(8,128)(2,1)S(1)}, bf16[32,2048]{1,0:T(8,128)(2,1)S(1)}, u32[]{:S(2)}, u32[]{:S(2)}) collective-permute-start(bf16[32,2048]{1,0:T(8,128)(2,1)S(1)} %add.15), channel_id=1, source_target_pairs={{0,8},{2,4},{4,2},{6,14},{8,0},{10,12},{12,10},{14,6},{16,24},{18,... | collective-permute-start | bytes 393224 | tf_op jit(solution)/shard_map/ppermute | solution.py:303
  49.5 2.1 %collective-permute-start.25 = (bf16[32,2048]{1,0:T(8,128)(2,1)S(1)}, bf16[32,2048]{1,0:T(8,128)(2,1)S(1)}, u32[]{:S(2)}, u32[]{:S(2)}) collective-permute-start(bf16[32,2048]{1,0:T(8,128)(2,1)S(1)} %add.12), channel_id=1, source_target_pairs={{0,8},{2,4},{4,2},{6,14},{8,0},{10,12},{12,10},{14,6},{16,24},{18,... | collective-permute-start | bytes 393224 | tf_op jit(solution)/shard_map/ppermute | solution.py:303
  51.8 3.1 %collective-permute-done.24.outer = bf16[32,2048]{1,0:T(8,128)(2,1)S(1)} collective-permute-done((bf16[32,2048]{1,0:T(8,128)(2,1)S(1)}, bf16[32,2048]{1,0:T(8,128)(2,1)S(1)}, u32[]{:S(2)}, u32[]{:S(2)}) %collective-permute-start.24) | collective-permute-done | bytes 131104 | tf_op jit(solution)/shard_map/ppermute | solution.py:300
  54.9 0.8 %collective-permute-done.25.inner = bf16[32,2048]{1,0:T(8,128)(2,1)S(1)} collective-permute-done((bf16[32,2048]{1,0:T(8,128)(2,1)S(1)}, bf16[32,2048]{1,0:T(8,128)(2,1)S(1)}, u32[]{:S(2)}, u32[]{:S(2)}) %collective-permute-start.25) | collective-permute-done | bytes 131104 | tf_op jit(solution)/shard_map/ppermute | solution.py:303
  56.5 0.8 %join.1 = bf16[128,2048]{1,0:T(8,128)(2,1)} custom-call(bf16[32,2048]{1,0:T(8,128)(2,1)S(1)} %finish_first.2.refs_0_.a, bf16[32,2048]{1,0:T(8,128)(2,1)S(1)} %finish_second.2.refs_1_, bf16[32,2048]{1,0:T(8,128)(2,1)S(1)} %finish_first.3.refs_2_.b, bf16[32,2048]{1,0:T(8,128)(2,1)S(1)} %finish_second.3.refs_3_), custom_call_target="tpu_custom_call" | custom-call | tf_op jit(solution)/shard_map/join/pallas_call | solution.py:87
  57.3 2.8 %collective-permute-done.33.early = bf16[32,2048]{1,0:T(8,128)(2,1)S(1)} collective-permute-done((bf16[32,2048]{1,0:T(8,128)(2,1)S(1)}, bf16[32,2048]{1,0:T(8,128)(2,1)S(1)}, u32[]{:S(2)}, u32[]{:S(2)}) %collective-permute-start.33) | collective-permute-done | bytes 131104 | tf_op jit(solution)/shard_map/ppermute | solution.py:411
  60.2 0.8 %join_handed.1.begun = bf16[128,2048]{1,0:T(8,128)(2,1)} custom-call(bf16[64,2048]{1,0:T(8,128)(2,1)S(1)} %collective-permute-done.32.firsts, bf16[32,2048]{1,0:T(8,128)(2,1)S(1)} %collective-permute-done.33.early), custom_call_target="tpu_custom_call" | custom-call | tf_op jit(solution)/shard_map/join_handed/pallas_call | solution.py:87
  (76 shorter events, 9.4 us)
Async XLA Ops:
  1.8 6.6 %collective-permute-start.2 = (bf16[32,2176]{1,0:T(8,128)(2,1)S(1)}, bf16[32,2176]{1,0:T(8,128)(2,1)S(1)}, u32[]{:S(2)}, u32[]{:S(2)}) collective-permute-start(bf16[32,2176]{1,0:T(8,128)(2,1)S(1)} %get-tuple-element.50.refs_10_), channel_id=1, source_target_pairs={{0,8},{2,4},{4,2},{6,14},{8,0},{10,12},{12,10},{14,6},{16,24},{18,... | collective-permute-start | bytes 417800 | tf_op jit(solution)/shard_map/ppermute | solution.py:303
  3.5 6.2 %collective-permute-start.5 = (bf16[32,2176]{1,0:T(8,128)(2,1)S(1)}, bf16[32,2176]{1,0:T(8,128)(2,1)S(1)}, u32[]{:S(2)}, u32[]{:S(2)}) collective-permute-start(bf16[32,2176]{1,0:T(8,128)(2,1)S(1)} %get-tuple-element.50.refs_10_), channel_id=1, source_target_pairs={{0,2},{2,0},{4,6},{6,4},{8,10},{10,8},{12,14},{14,12},{16,18},{18,... | collective-permute-start | bytes 417800 | tf_op jit(solution)/shard_map/ppermute | solution.py:300
  3.5 9.9 %collective-permute-start = (bf16[32,2176]{1,0:T(8,128)(2,1)S(1)}, bf16[32,2176]{1,0:T(8,128)(2,1)S(1)}, u32[]{:S(2)}, u32[]{:S(2)}) collective-permute-start(bf16[32,2176]{1,0:T(8,128)(2,1)S(1)} %get-tuple-element.44.refs_8_), channel_id=1, source_target_pairs={{0,8},{2,4},{4,2},{6,14},{8,0},{10,12},{12,10},{14,6},{16,24},{18,... | collective-permute-start | bytes 417800 | tf_op jit(solution)/shard_map/ppermute | solution.py:303
  5.1 8.5 %collective-permute-start.4 = (bf16[32,2176]{1,0:T(8,128)(2,1)S(1)}, bf16[32,2176]{1,0:T(8,128)(2,1)S(1)}, u32[]{:S(2)}, u32[]{:S(2)}) collective-permute-start(bf16[32,2176]{1,0:T(8,128)(2,1)S(1)} %get-tuple-element.44.refs_8_), channel_id=1, source_target_pairs={{0,2},{2,0},{4,6},{6,4},{8,10},{10,8},{12,14},{14,12},{16,18},{18,... | collective-permute-start | bytes 417800 | tf_op jit(solution)/shard_map/ppermute | solution.py:300
  8.5 7.8 %collective-permute-start.3 = (bf16[32,2176]{1,0:T(8,128)(2,1)S(1)}, bf16[32,2176]{1,0:T(8,128)(2,1)S(1)}, u32[]{:S(2)}, u32[]{:S(2)}) collective-permute-start(bf16[32,2176]{1,0:T(8,128)(2,1)S(1)} %choose.11), channel_id=1, source_target_pairs={{0,2},{2,0},{4,6},{6,4},{8,10},{10,8},{12,14},{14,12},{16,18},{18,... | collective-permute-start | bytes 417800 | tf_op jit(solution)/shard_map/ppermute | solution.py:300
  9.6 7.3 %collective-permute-start.9 = (bf16[32,2176]{1,0:T(8,128)(2,1)S(1)}, bf16[32,2176]{1,0:T(8,128)(2,1)S(1)}, u32[]{:S(2)}, u32[]{:S(2)}) collective-permute-start(bf16[32,2176]{1,0:T(8,128)(2,1)S(1)} %collective-permute-done.5.refs_4_.refs_5_.refs_6_.refs_7_), channel_id=1, source_target_pairs={{0,8},{2,4},{4,2},{6,14},{8,0},{10,12},{12,10},{14,6},{16,24},{18,... | collective-permute-start | bytes 417800 | tf_op jit(solution)/shard_map/ppermute | solution.py:303
  13.6 6.2 %collective-permute-start.6 = (bf16[32,2176]{1,0:T(8,128)(2,1)S(1)}, bf16[32,2176]{1,0:T(8,128)(2,1)S(1)}, u32[]{:S(2)}, u32[]{:S(2)}) collective-permute-start(bf16[32,2176]{1,0:T(8,128)(2,1)S(1)} %collective-permute-done.4.refs_0_.refs_1_.refs_2_.refs_3_), channel_id=1, source_target_pairs={{0,8},{2,4},{4,2},{6,14},{8,0},{10,12},{12,10},{14,6},{16,24},{18,... | collective-permute-start | bytes 417800 | tf_op jit(solution)/shard_map/ppermute | solution.py:303
  16.3 6.9 %collective-permute-start.11 = (bf16[32,2176]{1,0:T(8,128)(2,1)S(1)}, bf16[32,2176]{1,0:T(8,128)(2,1)S(1)}, u32[]{:S(2)}, u32[]{:S(2)}) collective-permute-start(bf16[32,2176]{1,0:T(8,128)(2,1)S(1)} %collective-permute-done.3.refs_4_.refs_6_.refs_5_), channel_id=1, source_target_pairs={{0,8},{2,4},{4,2},{6,14},{8,0},{10,12},{12,10},{14,6},{16,24},{18,... | collective-permute-start | bytes 417800 | tf_op jit(solution)/shard_map/ppermute | solution.py:303
  17.0 6.3 %collective-permute-start.10 = (bf16[32,2176]{1,0:T(8,128)(2,1)S(1)}, bf16[32,2176]{1,0:T(8,128)(2,1)S(1)}, u32[]{:S(2)}, u32[]{:S(2)}) collective-permute-start(bf16[32,2176]{1,0:T(8,128)(2,1)S(1)} %choose.14), channel_id=1, source_target_pairs={{0,2},{2,0},{4,6},{6,4},{8,10},{10,8},{12,14},{14,12},{16,18},{18,... | collective-permute-start | bytes 417800 | tf_op jit(solution)/shard_map/ppermute | solution.py:300
  18.5 7.4 %collective-permute-start.8 = (bf16[32,2176]{1,0:T(8,128)(2,1)S(1)}, bf16[32,2176]{1,0:T(8,128)(2,1)S(1)}, u32[]{:S(2)}, u32[]{:S(2)}) collective-permute-start(bf16[32,2176]{1,0:T(8,128)(2,1)S(1)} %collective-permute-done.1.refs_0_.refs_2_.refs_1_), channel_id=1, source_target_pairs={{0,8},{2,4},{4,2},{6,14},{8,0},{10,12},{12,10},{14,6},{16,24},{18,... | collective-permute-start | bytes 417800 | tf_op jit(solution)/shard_map/ppermute | solution.py:303
  19.8 6.1 %collective-permute-start.7 = (bf16[32,2176]{1,0:T(8,128)(2,1)S(1)}, bf16[32,2176]{1,0:T(8,128)(2,1)S(1)}, u32[]{:S(2)}, u32[]{:S(2)}) collective-permute-start(bf16[32,2176]{1,0:T(8,128)(2,1)S(1)} %choose.12), channel_id=1, source_target_pairs={{0,2},{2,0},{4,6},{6,4},{8,10},{10,8},{12,14},{14,12},{16,18},{18,... | collective-permute-start | bytes 417800 | tf_op jit(solution)/shard_map/ppermute | solution.py:300
  19.9 8.8 %collective-permute-start.14 = (bf16[32,2048]{1,0:T(8,128)(2,1)S(1)}, bf16[32,2048]{1,0:T(8,128)(2,1)S(1)}, u32[]{:S(2)}, u32[]{:S(2)}) collective-permute-start(bf16[32,2048]{1,0:T(8,128)(2,1)S(1)} %get-tuple-element.49.at_end.refs_11_.at_mid), channel_id=1, source_target_pairs={{0,8},{2,4},{4,2},{6,14},{8,0},{10,12},{12,10},{14,6},{16,24},{18,... | collective-permute-start | bytes 393224 | tf_op jit(solution)/shard_map/ppermute | solution.py:303
  23.3 6.1 %collective-permute-start.20 = (bf16[32,2048]{1,0:T(8,128)(2,1)S(1)}, bf16[32,2048]{1,0:T(8,128)(2,1)S(1)}, u32[]{:S(2)}, u32[]{:S(2)}) collective-permute-start(bf16[32,2048]{1,0:T(8,128)(2,1)S(1)} %choose.15), channel_id=1, source_target_pairs={{0,2},{2,0},{4,6},{6,4},{8,10},{10,8},{12,14},{14,12},{16,18},{18,... | collective-permute-start | bytes 393224 | tf_op jit(solution)/shard_map/ppermute | solution.py:300
  23.6 7.6 %collective-permute-start.12 = (bf16[32,2048]{1,0:T(8,128)(2,1)S(1)}, bf16[32,2048]{1,0:T(8,128)(2,1)S(1)}, u32[]{:S(2)}, u32[]{:S(2)}) collective-permute-start(bf16[32,2048]{1,0:T(8,128)(2,1)S(1)} %get-tuple-element.43.at_end.refs_9_.at_mid), channel_id=1, source_target_pairs={{0,8},{2,4},{4,2},{6,14},{8,0},{10,12},{12,10},{14,6},{16,24},{18,... | collective-permute-start | bytes 393224 | tf_op jit(solution)/shard_map/ppermute | solution.py:303
  25.9 6.0 %collective-permute-start.16 = (bf16[32,2048]{1,0:T(8,128)(2,1)S(1)}, bf16[32,2048]{1,0:T(8,128)(2,1)S(1)}, u32[]{:S(2)}, u32[]{:S(2)}) collective-permute-start(bf16[32,2048]{1,0:T(8,128)(2,1)S(1)} %choose.13), channel_id=1, source_target_pairs={{0,2},{2,0},{4,6},{6,4},{8,10},{10,8},{12,14},{14,12},{16,18},{18,... | collective-permute-start | bytes 393224 | tf_op jit(solution)/shard_map/ppermute | solution.py:300
  28.7 6.3 %collective-permute-start.15 = (bf16[32,2048]{1,0:T(8,128)(2,1)S(1)}, bf16[32,2048]{1,0:T(8,128)(2,1)S(1)}, u32[]{:S(2)}, u32[]{:S(2)}) collective-permute-start(bf16[32,2048]{1,0:T(8,128)(2,1)S(1)} %choose.17), channel_id=1, source_target_pairs={{0,2},{2,0},{4,6},{6,4},{8,10},{10,8},{12,14},{14,12},{16,18},{18,... | collective-permute-start | bytes 393224 | tf_op jit(solution)/shard_map/ppermute | solution.py:300
  29.5 5.6 %collective-permute-start.26 = (bf16[32,2048]{1,0:T(8,128)(2,1)S(1)}, bf16[32,2048]{1,0:T(8,128)(2,1)S(1)}, u32[]{:S(2)}, u32[]{:S(2)}) collective-permute-start(bf16[32,2048]{1,0:T(8,128)(2,1)S(1)} %add.10), channel_id=1, source_target_pairs={{0,8},{2,4},{4,2},{6,14},{8,0},{10,12},{12,10},{14,6},{16,24},{18,... | collective-permute-start | bytes 393224 | tf_op jit(solution)/shard_map/ppermute | solution.py:303
  31.2 6.1 %collective-permute-start.13 = (bf16[32,2048]{1,0:T(8,128)(2,1)S(1)}, bf16[32,2048]{1,0:T(8,128)(2,1)S(1)}, u32[]{:S(2)}, u32[]{:S(2)}) collective-permute-start(bf16[32,2048]{1,0:T(8,128)(2,1)S(1)} %choose.16), channel_id=1, source_target_pairs={{0,2},{2,0},{4,6},{6,4},{8,10},{10,8},{12,14},{14,12},{16,18},{18,... | collective-permute-start | bytes 393224 | tf_op jit(solution)/shard_map/ppermute | solution.py:300
  34.9 5.8 %collective-permute-start.22 = (bf16[32,2048]{1,0:T(8,128)(2,1)S(1)}, bf16[32,2048]{1,0:T(8,128)(2,1)S(1)}, u32[]{:S(2)}, u32[]{:S(2)}) collective-permute-start(bf16[32,2048]{1,0:T(8,128)(2,1)S(1)} %choose.19), channel_id=1, source_target_pairs={{0,2},{2,0},{4,6},{6,4},{8,10},{10,8},{12,14},{14,12},{16,18},{18,... | collective-permute-start | bytes 393224 | tf_op jit(solution)/shard_map/ppermute | solution.py:300
  35.1 5.7 %collective-permute-start.27 = (bf16[32,2048]{1,0:T(8,128)(2,1)S(1)}, bf16[32,2048]{1,0:T(8,128)(2,1)S(1)}, u32[]{:S(2)}, u32[]{:S(2)}) collective-permute-start(bf16[32,2048]{1,0:T(8,128)(2,1)S(1)} %add.13), channel_id=1, source_target_pairs={{0,8},{2,4},{4,2},{6,14},{8,0},{10,12},{12,10},{14,6},{16,24},{18,... | collective-permute-start | bytes 393224 | tf_op jit(solution)/shard_map/ppermute | solution.py:303
  36.7 6.5 %collective-permute-start.21 = (bf16[32,2048]{1,0:T(8,128)(2,1)S(1)}, bf16[32,2048]{1,0:T(8,128)(2,1)S(1)}, u32[]{:S(2)}, u32[]{:S(2)}) collective-permute-start(bf16[32,2048]{1,0:T(8,128)(2,1)S(1)} %choose.18), channel_id=1, source_target_pairs={{0,2},{2,0},{4,6},{6,4},{8,10},{10,8},{12,14},{14,12},{16,18},{18,... | collective-permute-start | bytes 393224 | tf_op jit(solution)/shard_map/ppermute | solution.py:300
  37.3 6.1 %collective-permute-start.18 = (bf16[32,2048]{1,0:T(8,128)(2,1)S(1)}, bf16[32,2048]{1,0:T(8,128)(2,1)S(1)}, u32[]{:S(2)}, u32[]{:S(2)}) collective-permute-start(bf16[32,2048]{1,0:T(8,128)(2,1)S(1)} %add.9), channel_id=1, source_target_pairs={{0,8},{2,4},{4,2},{6,14},{8,0},{10,12},{12,10},{14,6},{16,24},{18,... | collective-permute-start | bytes 393224 | tf_op jit(solution)/shard_map/ppermute | solution.py:303
  40.8 6.1 %collective-permute-start.28 = (bf16[32,2048]{1,0:T(8,128)(2,1)S(1)}, bf16[32,2048]{1,0:T(8,128)(2,1)S(1)}, u32[]{:S(2)}, u32[]{:S(2)}) collective-permute-start(bf16[32,2048]{1,0:T(8,128)(2,1)S(1)} %choose_sum.6), channel_id=1, source_target_pairs={{0,2},{2,0},{4,6},{6,4},{8,10},{10,8},{12,14},{14,12},{16,18},{18,... | collective-permute-start | bytes 393224 | tf_op jit(solution)/shard_map/ppermute | solution.py:300
  41.2 5.8 %collective-permute-start.29 = (bf16[32,2048]{1,0:T(8,128)(2,1)S(1)}, bf16[32,2048]{1,0:T(8,128)(2,1)S(1)}, u32[]{:S(2)}, u32[]{:S(2)}) collective-permute-start(bf16[32,2048]{1,0:T(8,128)(2,1)S(1)} %add.14), channel_id=1, source_target_pairs={{0,8},{2,4},{4,2},{6,14},{8,0},{10,12},{12,10},{14,6},{16,24},{18,... | collective-permute-start | bytes 393224 | tf_op jit(solution)/shard_map/ppermute | solution.py:303
  43.4 5.9 %collective-permute-start.19 = (bf16[32,2048]{1,0:T(8,128)(2,1)S(1)}, bf16[32,2048]{1,0:T(8,128)(2,1)S(1)}, u32[]{:S(2)}, u32[]{:S(2)}) collective-permute-start(bf16[32,2048]{1,0:T(8,128)(2,1)S(1)} %choose_sum.4), channel_id=1, source_target_pairs={{0,2},{2,0},{4,6},{6,4},{8,10},{10,8},{12,14},{14,12},{16,18},{18,... | collective-permute-start | bytes 393224 | tf_op jit(solution)/shard_map/ppermute | solution.py:300
  43.7 5.7 %collective-permute-start.23 = (bf16[32,2048]{1,0:T(8,128)(2,1)S(1)}, bf16[32,2048]{1,0:T(8,128)(2,1)S(1)}, u32[]{:S(2)}, u32[]{:S(2)}) collective-permute-start(bf16[32,2048]{1,0:T(8,128)(2,1)S(1)} %add.11), channel_id=1, source_target_pairs={{0,8},{2,4},{4,2},{6,14},{8,0},{10,12},{12,10},{14,6},{16,24},{18,... | collective-permute-start | bytes 393224 | tf_op jit(solution)/shard_map/ppermute | solution.py:303
  47.0 8.7 %collective-permute-start.30 = (bf16[32,2048]{1,0:T(8,128)(2,1)S(1)}, bf16[32,2048]{1,0:T(8,128)(2,1)S(1)}, u32[]{:S(2)}, u32[]{:S(2)}) collective-permute-start(bf16[32,2048]{1,0:T(8,128)(2,1)S(1)} %choose_sum.7), channel_id=1, source_target_pairs={{0,2},{2,0},{4,6},{6,4},{8,10},{10,8},{12,14},{14,12},{16,18},{18,... | collective-permute-start | bytes 393224 | tf_op jit(solution)/shard_map/ppermute | solution.py:300
  47.1 8.7 %collective-permute-start.31 = (bf16[32,2048]{1,0:T(8,128)(2,1)S(1)}, bf16[32,2048]{1,0:T(8,128)(2,1)S(1)}, u32[]{:S(2)}, u32[]{:S(2)}) collective-permute-start(bf16[32,2048]{1,0:T(8,128)(2,1)S(1)} %add.15), channel_id=1, source_target_pairs={{0,8},{2,4},{4,2},{6,14},{8,0},{10,12},{12,10},{14,6},{16,24},{18,... | collective-permute-start | bytes 393224 | tf_op jit(solution)/shard_map/ppermute | solution.py:303
  49.4 5.5 %collective-permute-start.24 = (bf16[32,2048]{1,0:T(8,128)(2,1)S(1)}, bf16[32,2048]{1,0:T(8,128)(2,1)S(1)}, u32[]{:S(2)}, u32[]{:S(2)}) collective-permute-start(bf16[32,2048]{1,0:T(8,128)(2,1)S(1)} %choose_sum.5), channel_id=1, source_target_pairs={{0,2},{2,0},{4,6},{6,4},{8,10},{10,8},{12,14},{14,12},{16,18},{18,... | collective-permute-start | bytes 393224 | tf_op jit(solution)/shard_map/ppermute | solution.py:300
  49.5 6.2 %collective-permute-start.25 = (bf16[32,2048]{1,0:T(8,128)(2,1)S(1)}, bf16[32,2048]{1,0:T(8,128)(2,1)S(1)}, u32[]{:S(2)}, u32[]{:S(2)}) collective-permute-start(bf16[32,2048]{1,0:T(8,128)(2,1)S(1)} %add.12), channel_id=1, source_target_pairs={{0,8},{2,4},{4,2},{6,14},{8,0},{10,12},{12,10},{14,6},{16,24},{18,... | collective-permute-start | bytes 393224 | tf_op jit(solution)/shard_map/ppermute | solution.py:303
  51.8 8.4 %collective-permute-start.32 = (bf16[64,2048]{1,0:T(8,128)(2,1)S(1)}, bf16[64,2048]{1,0:T(8,128)(2,1)S(1)}, u32[]{:S(2)}, u32[]{:S(2)}) collective-permute-start(bf16[64,2048]{1,0:T(8,128)(2,1)S(1)} %join_two.1), channel_id=1, source_target_pairs={{0,8},{8,16},{16,24},{24,0},{1,9},{9,17},{17,25},{25,1},{2,10},{10... | collective-permute-start | bytes 786440 | tf_op jit(solution)/shard_map/ppermute | solution.py:410
  55.9 5.7 %collective-permute-start.34 = (bf16[32,2048]{1,0:T(8,128)(2,1)S(1)}, bf16[32,2048]{1,0:T(8,128)(2,1)S(1)}, u32[]{:S(2)}, u32[]{:S(2)}) collective-permute-start(bf16[32,2048]{1,0:T(8,128)(2,1)S(1)} %finish_second.3.refs_3_), channel_id=1, source_target_pairs={{0,8},{8,16},{16,24},{24,0},{1,9},{9,17},{17,25},{25,1},{2,10},{10... | collective-permute-start | bytes 393224 | tf_op jit(solution)/shard_map/ppermute | solution.py:411
  (3 other events, 14.9 us)
